TPU v7x, 128 devices: a whole 4x4x4 slice. The times are simulated.
128 devices in a mesh: ctx: 16 (over x, z_lo, core), dp: 8 (over y, z_hi).
Axes of the slice: x: 4, y: 4, z: 4 (z_hi: 2, z_lo: 2; z = z_hi * 2 + z_lo), core: 2. Of those that a mesh axis runs over, the one named last changes fastest.
Arguments:
- query: bfloat16 [8, 8192, 1024], P('dp', 'ctx'), may hold values from -30 to 30
- key: bfloat16 [8, 8192, 1024], P('dp', 'ctx'), may hold values from -30 to 30
- value: bfloat16 [8, 8192, 1024], P('dp', 'ctx'), may hold values from -6 to 6
- segment_ids: int32 [8, 8192], P('dp', 'ctx'), may hold values from 0 to 1, never falling along the last dimension, each value on 1 to 7680 neighbouring positions
- out_weight: bfloat16 [1024, 2048], replicated, may hold values from -0.1875 to 0.1875
- cotangent: bfloat16 [8, 8192, 2048], P('dp', 'ctx'), may hold values from -6 to 6
Outputs:
- output: bfloat16 [8, 8192, 2048], P('dp', 'ctx')
- grad_query: bfloat16 [8, 8192, 1024], P('dp', 'ctx')
- grad_key: bfloat16 [8, 8192, 1024], P('dp', 'ctx')
- grad_value: bfloat16 [8, 8192, 1024], P('dp', 'ctx')
- grad_weight: float32 [1024, 2048], P(('ctx', 'dp'))
All inputs are finite; a program needn't handle non-finite values.
Results may differ from a plain program's by a relative error of at most 0.023.
Values may be sent and summed in bfloat16 or wider, within the bound.
No kernel may reach another device: no remote copies, remote signals or barrier semaphores. Data moves between devices by JAX's collectives and lax.ppermute only.
A program may use at most 192 MiB of HBM per device.

v0:
```python
from functools import partial
import math

import jax
import jax.numpy as jnp
from jax import lax
from jax.sharding import PartitionSpec as P

HEADS = 8
HEAD_DIM = 128
LEVELS = 3
HD = 1024


def partner(array, axis, stride):
    return lax.ppermute(array, axis, [(i, i ^ 1 << stride) for i in range(lax.axis_size(axis))])


def as_sent(array):
    return jax.tree.map(lambda a: a.astype(jnp.bfloat16) if a.dtype == jnp.float32 else a, array)


def level_heights(blocks):
    summit = int(blocks).bit_length() - 1
    return list(range(summit - LEVELS, summit))


def pool_rows(values32, factor):
    shape = values32.shape
    grouped = values32.reshape(shape[:-2] + (shape[-2] // factor, factor, shape[-1]))
    return jnp.mean(grouped, axis=-2).astype(jnp.bfloat16)


def attend(queries, keys32, values32, segments, coarse, heights=()):
    count = queries.shape[0]
    scale = 1.0 / math.sqrt(HEAD_DIM)
    query_f = queries.astype(jnp.float32).reshape(count, HEADS, HEAD_DIM)
    key_sets = [(keys32, values32, segments, 0.0)]
    for height, triple in zip(heights, coarse):
        key_sets.append(
            (
                triple[0].astype(jnp.float32),
                triple[1].astype(jnp.float32),
                triple[2],
                math.log(2.0 ** (height + 1)),
            )
        )
    blocks = []
    values_all = []
    for key_f, value_f, key_seg, offset in key_sets:
        width = key_f.shape[0]
        logits = (
            jnp.einsum("qhe,khe->hqk", query_f, key_f.reshape(width, HEADS, HEAD_DIM)) * scale
            + offset
        )
        allowed = segments[:, None] == key_seg[None, :]
        blocks.append(jnp.where(allowed[None], logits, -1e30))
        values_all.append(value_f.reshape(width, HEADS, HEAD_DIM))
    scores = jnp.concatenate(blocks, -1)
    top = lax.stop_gradient(jnp.max(scores, -1, keepdims=True))
    expo = jnp.exp(scores - top)
    weights = (expo / jnp.sum(expo, -1, keepdims=True)).astype(jnp.bfloat16)
    mixed = jnp.einsum("hqk,khe->qhe", weights.astype(jnp.float32), jnp.concatenate(values_all, 0))
    return mixed.reshape(count, HEADS * HEAD_DIM).astype(jnp.bfloat16)


def one_sequence(
    queries,
    keys32,
    values32,
    segments,
    coarse_keys,
    coarse_vals,
    coarse_segs,
    grad_attention,
    heights=(),
):

    def local(query_s, key_s, value_s, ckeys, cvals):
        return attend(
            query_s, key_s, value_s, segments, tuple(zip(ckeys, cvals, coarse_segs)), heights
        )

    attention, pull = jax.vjp(local, queries, keys32, values32, coarse_keys, coarse_vals)
    return (attention,) + pull(grad_attention)


def body(query, key, value, segment_ids, out_weight, cotangent):
    seq_count = query.shape[0]
    block_rows = query.shape[1]
    index = lax.axis_index("ctx")
    nblocks = lax.axis_size("ctx")
    heights = level_heights(nblocks)
    key32 = key.astype(jnp.float32)
    value32 = value.astype(jnp.float32)
    pooled = []
    for height in heights:
        factor = 2 ** (height + 1)
        pooled.append(
            (
                pool_rows(key32, factor),
                pool_rows(value32, factor),
                segment_ids[:, ::factor].astype(jnp.bfloat16),
            )
        )
    received = []
    stacked_keys = jnp.concatenate([entry[0] for entry in pooled], axis=1)
    stacked_vals = jnp.concatenate([entry[1] for entry in pooled], axis=1)
    stacked_segs = jnp.concatenate([entry[2] for entry in pooled], axis=1)
    span = stacked_keys.shape[1]
    whole = (
        lax.all_gather(stacked_keys, "ctx", axis=1, tiled=True),
        lax.all_gather(stacked_vals, "ctx", axis=1, tiled=True),
        lax.all_gather(stacked_segs, "ctx", axis=1, tiled=True),
    )
    arranged = (
        whole[0].reshape(seq_count, nblocks, span, HD),
        whole[1].reshape(seq_count, nblocks, span, HD),
        whole[2].reshape(seq_count, nblocks, span),
    )
    position = 0
    for height in heights:
        count = block_rows // 2 ** (height + 1)
        group = 2**height
        first = jnp.left_shift(jnp.bitwise_xor(jnp.right_shift(index, height), 1), height)
        taken = []
        for member in arranged:
            piece = lax.dynamic_slice_in_dim(member, first, group, 1)[
                :, :, position : position + count
            ]
            taken.append(piece.reshape((seq_count, group * count) + member.shape[3:]))
        received.append(tuple(taken))
        position = position + count
    coarse_keys = tuple((entry[0] for entry in received))
    coarse_vals = tuple((entry[1] for entry in received))
    coarse_segs = tuple((entry[2].astype(jnp.int32) for entry in received))
    grad_attention = jnp.einsum(
        "std,hd->sth", cotangent, out_weight, preferred_element_type=jnp.float32
    ).astype(jnp.bfloat16)
    results = jax.vmap(partial(one_sequence, heights=heights))(
        query, key32, value32, segment_ids, coarse_keys, coarse_vals, coarse_segs, grad_attention
    )
    attention, grad_query, grad_key32, grad_value32, grad_ckeys, grad_cvals = results
    for place, height in enumerate(heights):
        factor = 2 ** (height + 1)
        returned = partner((grad_ckeys[place], grad_cvals[place]), "ctx", height)
        sums = tuple((member.astype(jnp.float32) for member in returned))
        for bit in range(height - 1, -1, -1):
            half = sums[0].shape[1] // 2
            upper = jnp.bitwise_and(jnp.right_shift(index, bit), 1) == 1
            kept = tuple((jnp.where(upper, member[:, half:], member[:, :half]) for member in sums))
            given = tuple((jnp.where(upper, member[:, :half], member[:, half:]) for member in sums))
            got = jax.tree.map(
                lambda part, own: part.astype(own.dtype), partner(as_sent(given), "ctx", bit), given
            )
            sums = tuple((mine + theirs for mine, theirs in zip(kept, got)))
        grad_key32 = grad_key32 + jnp.repeat(sums[0] / factor, factor, axis=1)
        grad_value32 = grad_value32 + jnp.repeat(sums[1] / factor, factor, axis=1)
    output = jnp.einsum(
        "sth,hd->std", attention, out_weight, preferred_element_type=jnp.float32
    ).astype(jnp.bfloat16)
    attention_flat = attention.reshape(-1, HD)
    cotangent_flat = cotangent.reshape(-1, cotangent.shape[2])
    grad_weight = lax.psum_scatter(
        lax.dot_general(
            attention_flat,
            cotangent_flat,
            (((0,), (0,)), ((), ())),
            preferred_element_type=jnp.float32,
        ),
        ("ctx", "dp"),
        scatter_dimension=0,
        tiled=True,
    )
    return (
        output,
        grad_query,
        grad_key32.astype(jnp.bfloat16),
        grad_value32.astype(jnp.bfloat16),
        grad_weight,
    )


def solution(mesh):
    in_specs = (
        P("dp", "ctx", None),
        P("dp", "ctx", None),
        P("dp", "ctx", None),
        P("dp", "ctx"),
        P(),
        P("dp", "ctx", None),
    )
    out_specs = (
        P("dp", "ctx", None),
        P("dp", "ctx", None),
        P("dp", "ctx", None),
        P("dp", "ctx", None),
        P(("ctx", "dp"), None),
    )
    return jax.shard_map(body, mesh=mesh, in_specs=in_specs, out_specs=out_specs, check_vma=False)
```

profile of v0, /device:TPU:0, one launch (start us, length us, event | category | flops | bytes accessed | tf_op | source)
XLA Modules:
  0.0 889.2 jit_solution(13876242847321021381)
XLA Ops:
  7.2 2.1 bitcast_reduce_fusion
  9.3 2.7 reshape.912
  13.7 3.7 reduce_sum.79
  18.5 2.6 reduce_sum.81
  22.9 1.7 reshape.904
  26.3 3.7 reduce_sum.76
  29.9 2.0 reduce_sum.78
  35.2 2.3 copy.107
  40.4 32.3 %all-reduce = bf16[3584]{0:T(1024)(128)(2,1)S(1)} all-reduce(bf16[3584]{0:T(1024)(128)(2,1)S(1)} %dynamic-update-slice), channel_id=1, replica_groups=mesh['ctx'=16,'dp'=8] {'ctx'}, use_global_device_ids=true, to_apply=%add | all-reduce | flops 3584 | bytes 14336
  73.1 2.3 copy.106
  75.4 5.6 fusion.66
  81.0 2.3 copy.105
  84.5 6.7 fusion.110
  91.2 32.5 %all-gather.3.cloned.1.call-done = bf16[1,3584,1024]{2,1,0:T(8,128)(2,1)} async-done(((bf16[1,224,1024]{2,1,0:T(8,128)(2,1)}), bf16[1,3584,1024]{2,1,0:T(8,128)(2,1)}) %all-gather.3.cloned.1.call-update) | async-done | bytes 7340048 | tf_op jit(solution)/shard_map/all_gather | solution.py:113
  123.6 2.1 dynamic-slice_convert_fusion
  125.7 2.3 dynamic-slice_convert_fusion.1
  128.0 2.2 dynamic-slice_convert_fusion.2
  131.1 2.1 copy.51
  133.2 1.9 copy.113
  135.2 2.1 copy.66
  137.3 1.9 copy.108
  139.2 2.1 copy.104
  141.4 1.9 copy.111
  143.3 2.1 copy.70
  145.4 1.9 copy.109
  147.4 2.1 copy.50
  149.5 1.9 copy.112
  151.4 2.1 copy.68
  153.6 2.7 fusion.109
  160.3 1.8 slice-done.1
  162.1 6.9 fusion.7
  169.7 14.9 %fusion.4 = (f32[8,512]{1,0:T(8,128)}, bf16[8,512,1280]{1,2,0:T(8,128)(2,1)}) fusion(f32[8,512]{1,0:T(8,128)} %multiply_divide_fusion, f32[8,512]{1,0:T(8,128)S(1)} %maximum_maximum_fusion, f32[8,512,256]{1,2,0:T(8,128)} %copy-done.4, f32[8,512,256]{1,2,0:T(8,128)} %copy-done.2, f32[8,512,256]{1,2,0:T(8,128)} %copy-done.3, ...), kind=kOutput, calls=%fused_computation.6 | convolution fusion | flops 1394601984 | bytes 35176448 | tf_op jit(solution)/shard_map/vmap(transpose(jvp(hqk,khe->qhe)))/dot_general | solution.py:63
  185.9 23.8 %fusion.2 = (f32[1,8,512,1280]{2,3,1,0:T(8,128)}, bf16[8,512,1280]{1,2,0:T(8,128)(2,1)}) fusion(bf16[8,512,1280]{1,2,0:T(8,128)(2,1)} %get-tuple-element.32, f32[8,512]{1,0:T(8,128)} %neg.7, f32[8,512]{1,0:T(8,128)} %copy-done.33, f32[8,512]{1,0:T(8,128)S(1)} %maximum_maximum_fusion, f32[8,512,256]{1,2,0:T(8,128)} %copy-done.4, f32[8,512,256]{1,2,0:T(8,128)} %copy-done.2, ...), kind=kLoop, calls=%fused_computation.4 | loop fusion | flops 52428800 | bytes 62963712 | tf_op jit(solution)/shard_map/vmap(transpose(jvp()))/mul | solution.py:61
  209.7 6.3 fusion.69
  217.0 5.6 fusion.42
  223.8 3.8 fusion.76
  227.7 2.5 collective-permute-start.5
  230.2 3.8 fusion.73
  234.9 3.8 fusion.70
  239.7 9.8 %fusion.112 = (bf16[1,1280,8,128]{1,3,2,0:T(8,128)(2,1)S(1)}, f32[1,1280,8,128]{1,3,2,0:T(8,128)}) fusion(bf16[8,128,512]{2,1,0:T(8,128)(2,1)S(1)} %bitcast.223, bf16[8,512,1280]{1,2,0:T(8,128)(2,1)} %get-tuple-element.16), kind=kOutput, calls=%fused_computation.166 | convolution fusion | flops 1343488000 | bytes 19398656 | tf_op jit(solution)/shard_map/vmap(transpose(jvp(hqk,khe->qhe)))/dot_general | solution.py:63
  250.7 2.6 collective-permute-start.14
  253.7 2.9 fusion.28
  256.7 3.0 fusion.32
  259.7 3.1 fusion.36
  263.5 3.8 fusion.39
  267.2 6.1 add_convert_fusion
  273.3 6.4 fusion.10
  279.8 3.0 copy.78
  284.1 1.8 split.39
  285.9 1.8 copy.87
  289.4 2.1 collective-permute-start.6
  292.7 1.7 collective-permute-start.3
  298.9 8.8 collective-permute-done.9
  308.7 7.5 collective-permute-done.3
  318.2 2.2 copy.77
  321.3 2.0 collective-permute-start.16
  326.8 1.8 multiply_bitcast_fusion.2
  328.6 2.0 copy.86
  330.7 1.6 broadcast_in_dim.124
  332.3 1.8 broadcast_in_dim.125
  335.7 1.8 broadcast_in_dim.119
  345.9 4.0 fusion.41
  350.2 1.7 fusion.40
  351.9 530.6 %reduce-scatter.2.cloned.1.call-done = f32[8,2048]{1,0:T(8,128)} async-done(((f32[1024,2048]{1,0:T(8,128)}), f32[8,2048]{1,0:T(8,128)}) %reduce-scatter.2.cloned.1.call-update) | async-done | bytes 65552 | tf_op jit(solution)/shard_map/reduce_scatter | solution.py:164
  (192 shorter events, 52.4 us)
Async XLA Ops:
  7.2 68.2 %copy-start = (bf16[1,512,2048]{2,1,0:T(8,128)(2,1)S(1)}, bf16[1,512,2048]{2,1,0:T(8,128)(2,1)}, u32[]{:S(2)}) copy-start(bf16[1,512,2048]{2,1,0:T(8,128)(2,1)} %param.11) | copy-start | bytes 6291460
  7.2 4.9 copy-start.6
  7.2 84.0 %all-gather.5.cloned.1.call-start = ((), (), s32[]{:S(2)}) async-start(), calls=%async_computation.2 | async-start | bytes 7798784 | tf_op jit(solution)/shard_map/all_gather | solution.py:112
  13.7 9.3 %copy-start.5 = (bf16[1,512,1024]{2,1,0:T(8,128)(2,1)S(1)}, bf16[1,512,1024]{2,1,0:T(8,128)(2,1)}, u32[]{:S(2)}) copy-start(bf16[1,512,1024]{2,1,0:T(8,128)(2,1)} %param.8) | copy-start | bytes 3145732
  22.9 100.7 %all-gather.3.cloned.1.call-start = ((), (), s32[]{:S(2)}) async-start(), calls=%async_computation.1 | async-start | bytes 7798784 | tf_op jit(solution)/shard_map/all_gather | solution.py:113
  26.3 8.4 copy-start.35
  31.9 6.9 copy-start.39
  34.6 847.9 %reduce-scatter.2.cloned.1.call-start = ((), (), s32[]{:S(2)}) async-start(), calls=%async_computation.3 | async-start | bytes 8454144 | tf_op jit(solution)/shard_map/reduce_scatter | solution.py:164
  75.4 9.1 %copy-start.7 = (bf16[1,512,1024]{1,2,0:T(8,128)(2,1)S(1)}, bf16[1,512,1024]{1,2,0:T(8,128)(2,1)}, u32[]{:S(2)}) copy-start(bf16[1,512,1024]{1,2,0:T(8,128)(2,1)} %copy.107) | copy-start | bytes 3145732
  153.5 2.7 copy-start.18
  153.5 2.7 copy-start.23
  153.6 6.8 slice-start
  156.2 4.1 copy-start.2
  156.2 1.4 copy-start.21
  156.2 1.5 copy-start.28
  156.3 5.8 slice-start.1
  157.4 11.6 %copy-start.3 = (f32[8,512,256]{1,2,0:T(8,128)}, f32[8,512,256]{1,2,0:T(8,128)S(1)}, u32[]{:S(2)}) copy-start(f32[8,512,256]{1,2,0:T(8,128)S(1)} %get-tuple-element.30) | copy-start | bytes 12582916
  157.4 2.9 copy-start.34
  158.9 10.2 %copy-start.4 = (f32[8,512,256]{1,2,0:T(8,128)}, f32[8,512,256]{1,2,0:T(8,128)S(1)}, u32[]{:S(2)}) copy-start(f32[8,512,256]{1,2,0:T(8,128)S(1)} %get-tuple-element.24) | copy-start | bytes 12582916
  162.1 7.6 copy-start.15
  162.1 7.6 copy-start.31
  169.1 0.6 copy-start.33
  216.0 1.0 copy-start.37
  222.6 1.2 copy-start.19
  222.6 1.2 copy-start.29
  222.6 7.6 copy-start.26
  227.7 60.1 %collective-permute-start.5 = (bf16[1,256,1024]{1,2,0:T(8,128)(2,1)}, bf16[1,256,1024]{1,2,0:T(8,128)(2,1)}, u32[]{:S(2)}, u32[]{:S(2)}) collective-permute-start(bf16[1,256,1024]{1,2,0:T(8,128)(2,1)} %bitcast.54), channel_id=1, source_target_pairs={{0,64},{8,72},{16,80},{24,88},{32,96},{40,104},{48,112},{56,120},{... | collective-permute-start | bytes 1572872 | tf_op jit(solution)/shard_map/ppermute | solution.py:16
  234.0 5.7 copy-start.16
  234.0 55.4 %collective-permute-start.2 = (bf16[1,256,1024]{1,2,0:T(8,128)(2,1)}, bf16[1,256,1024]{1,2,0:T(8,128)(2,1)}, u32[]{:S(2)}, u32[]{:S(2)}) collective-permute-start(bf16[1,256,1024]{1,2,0:T(8,128)(2,1)} %bitcast.49), channel_id=1, source_target_pairs={{0,32},{8,40},{16,48},{24,56},{32,0},{40,8},{48,16},{56,24},{64,96... | collective-permute-start | bytes 1572872 | tf_op jit(solution)/shard_map/ppermute | solution.py:16
  238.7 15.0 %copy-start.22 = (bf16[256,8,128]{0,2,1:T(8,128)(2,1)S(1)}, bf16[256,8,128]{0,2,1:T(8,128)(2,1)}, u32[]{:S(2)}) copy-start(bf16[256,8,128]{0,2,1:T(8,128)(2,1)} %copy.66) | copy-start | bytes 1572868
  238.7 15.0 %copy-start.30 = (pred[512,256]{0,1:T(8,128)(4,1)S(1)}, pred[512,256]{0,1:T(8,128)(4,1)}, u32[]{:S(2)}) copy-start(pred[512,256]{0,1:T(8,128)(4,1)} %get-tuple-element.22) | copy-start | bytes 393220
  238.7 53.9 %collective-permute-start = (bf16[1,256,1024]{1,2,0:T(8,128)(2,1)}, bf16[1,256,1024]{1,2,0:T(8,128)(2,1)}, u32[]{:S(2)}, u32[]{:S(2)}) collective-permute-start(bf16[1,256,1024]{1,2,0:T(8,128)(2,1)} %bitcast.45), channel_id=1, source_target_pairs={{0,16},{8,24},{16,0},{24,8},{32,48},{40,56},{48,32},{56,40},{64,80... | collective-permute-start | bytes 1572872 | tf_op jit(solution)/shard_map/ppermute | solution.py:16
  250.7 6.0 copy-start.25
  250.7 6.0 copy-start.27
  250.7 44.9 %collective-permute-start.14 = (bf16[1,256,1024]{1,2,0:T(8,128)(2,1)}, bf16[1,256,1024]{1,2,0:T(8,128)(2,1)}, u32[]{:S(2)}, u32[]{:S(2)}) collective-permute-start(bf16[1,256,1024]{1,2,0:T(8,128)(2,1)} %bitcast.68), channel_id=1, source_target_pairs={{0,64},{8,72},{16,80},{24,88},{32,96},{40,104},{48,112},{56,120},{... | collective-permute-start | bytes 1572872 | tf_op jit(solution)/shard_map/ppermute | solution.py:16
  253.3 43.5 %collective-permute-start.11 = (bf16[1,256,1024]{1,2,0:T(8,128)(2,1)}, bf16[1,256,1024]{1,2,0:T(8,128)(2,1)}, u32[]{:S(2)}, u32[]{:S(2)}) collective-permute-start(bf16[1,256,1024]{1,2,0:T(8,128)(2,1)} %bitcast.65), channel_id=1, source_target_pairs={{0,32},{8,40},{16,48},{24,56},{32,0},{40,8},{48,16},{56,24},{64,96... | collective-permute-start | bytes 1572872 | tf_op jit(solution)/shard_map/ppermute | solution.py:16
  256.7 3.0 copy-start.24
  259.7 3.5 copy-start.36
  259.7 3.8 copy-start.38
  267.2 6.1 copy-start.20
  279.8 3.0 copy-start.17
  284.1 3.7 copy-start.32
  287.8 19.9 %collective-permute-start.9 = (bf16[1,256,1024]{1,2,0:T(8,128)(2,1)S(1)}, bf16[1,256,1024]{1,2,0:T(8,128)(2,1)S(1)}, u32[]{:S(2)}, u32[]{:S(2)}) collective-permute-start(bf16[1,256,1024]{1,2,0:T(8,128)(2,1)S(1)} %bitcast.248), channel_id=1, source_target_pairs={{0,16},{8,24},{16,0},{24,8},{32,48},{40,56},{48,32},{56,40},{64,80... | collective-permute-start | bytes 1572872 | tf_op jit(solution)/shard_map/ppermute | solution.py:16
  289.4 19.1 %collective-permute-start.6 = (bf16[1,128,1024]{1,2,0:T(8,128)(2,1)S(1)}, bf16[1,128,1024]{1,2,0:T(8,128)(2,1)S(1)}, u32[]{:S(2)}, u32[]{:S(2)}) collective-permute-start(bf16[1,128,1024]{1,2,0:T(8,128)(2,1)S(1)} %select_convert_fusion.8), channel_id=1, source_target_pairs={{0,32},{8,40},{16,48},{24,56},{32,0},{40,8},{48,16},{56,24},{64,96... | collective-permute-start | bytes 786440 | tf_op jit(solution)/shard_map/ppermute | solution.py:16
  292.7 23.5 %collective-permute-start.3 = (bf16[1,128,1024]{1,2,0:T(8,128)(2,1)S(1)}, bf16[1,128,1024]{1,2,0:T(8,128)(2,1)S(1)}, u32[]{:S(2)}, u32[]{:S(2)}) collective-permute-start(bf16[1,128,1024]{1,2,0:T(8,128)(2,1)S(1)} %select_convert_fusion.10), channel_id=1, source_target_pairs={{0,16},{8,24},{16,0},{24,8},{32,48},{40,56},{48,32},{56,40},{64,80... | collective-permute-start | bytes 786440 | tf_op jit(solution)/shard_map/ppermute | solution.py:16
  295.5 21.5 %collective-permute-start.1 = (bf16[1,128,1024]{1,2,0:T(8,128)(2,1)S(1)}, bf16[1,128,1024]{1,2,0:T(8,128)(2,1)S(1)}, u32[]{:S(2)}, u32[]{:S(2)}) collective-permute-start(bf16[1,128,1024]{1,2,0:T(8,128)(2,1)S(1)} %select_convert_fusion.11), channel_id=1, source_target_pairs={{0,8},{8,0},{16,24},{24,16},{32,40},{40,32},{48,56},{56,48},{64,72... | collective-permute-start | bytes 786440 | tf_op jit(solution)/shard_map/ppermute | solution.py:16
  296.8 21.3 %collective-permute-start.15 = (bf16[1,128,1024]{1,2,0:T(8,128)(2,1)S(1)}, bf16[1,128,1024]{1,2,0:T(8,128)(2,1)S(1)}, u32[]{:S(2)}, u32[]{:S(2)}) collective-permute-start(bf16[1,128,1024]{1,2,0:T(8,128)(2,1)S(1)} %select_convert_fusion.2), channel_id=1, source_target_pairs={{0,32},{8,40},{16,48},{24,56},{32,0},{40,8},{48,16},{56,24},{64,96... | collective-permute-start | bytes 786440 | tf_op jit(solution)/shard_map/ppermute | solution.py:16
  298.0 9.6 %copy-start.14 = (f32[1,256,1024]{1,2,0:T(8,128)}, f32[1,256,1024]{1,2,0:T(8,128)S(1)}, u32[]{:S(2)}) copy-start(f32[1,256,1024]{1,2,0:T(8,128)S(1)} %convert_element_type.518) | copy-start | bytes 3145732
  307.6 16.9 %collective-permute-start.12 = (bf16[1,128,1024]{1,2,0:T(8,128)(2,1)}, bf16[1,128,1024]{1,2,0:T(8,128)(2,1)}, u32[]{:S(2)}, u32[]{:S(2)}) collective-permute-start(bf16[1,128,1024]{1,2,0:T(8,128)(2,1)} %select_convert_fusion.4), channel_id=1, source_target_pairs={{0,16},{8,24},{16,0},{24,8},{32,48},{40,56},{48,32},{56,40},{64,80... | collective-permute-start | bytes 786440 | tf_op jit(solution)/shard_map/ppermute | solution.py:16
  308.5 18.3 %collective-permute-start.10 = (bf16[1,128,1024]{1,2,0:T(8,128)(2,1)}, bf16[1,128,1024]{1,2,0:T(8,128)(2,1)}, u32[]{:S(2)}, u32[]{:S(2)}) collective-permute-start(bf16[1,128,1024]{1,2,0:T(8,128)(2,1)} %select_convert_fusion.5), channel_id=1, source_target_pairs={{0,8},{8,0},{16,24},{24,16},{32,40},{40,32},{48,56},{56,48},{64,72... | collective-permute-start | bytes 786440 | tf_op jit(solution)/shard_map/ppermute | solution.py:16
  316.2 21.3 %collective-permute-start.7 = (bf16[1,64,1024]{1,2,0:T(8,128)(2,1)S(1)}, bf16[1,64,1024]{1,2,0:T(8,128)(2,1)}, u32[]{:S(2)}, u32[]{:S(2)}) collective-permute-start(bf16[1,64,1024]{1,2,0:T(8,128)(2,1)S(1)} %select_convert_fusion.7), channel_id=1, source_target_pairs={{0,16},{8,24},{16,0},{24,8},{32,48},{40,56},{48,32},{56,40},{64,80... | collective-permute-start | bytes 393224 | tf_op jit(solution)/shard_map/ppermute | solution.py:16
  317.1 23.0 %collective-permute-start.4 = (bf16[1,64,1024]{1,2,0:T(8,128)(2,1)}, bf16[1,64,1024]{1,2,0:T(8,128)(2,1)}, u32[]{:S(2)}, u32[]{:S(2)}) collective-permute-start(bf16[1,64,1024]{1,2,0:T(8,128)(2,1)} %select_convert_fusion.9), channel_id=1, source_target_pairs={{0,8},{8,0},{16,24},{24,16},{32,40},{40,32},{48,56},{56,48},{64,72... | collective-permute-start | bytes 393224 | tf_op jit(solution)/shard_map/ppermute | solution.py:16
  318.2 10.4 %copy-start.8 = (f32[1,128,1024]{1,2,0:T(8,128)}, f32[1,128,1024]{1,2,0:T(8,128)S(1)}, u32[]{:S(2)}) copy-start(f32[1,128,1024]{1,2,0:T(8,128)S(1)} %convert_add_fusion.1) | copy-start | bytes 1572868
  321.3 20.2 %collective-permute-start.16 = (bf16[1,64,1024]{1,2,0:T(8,128)(2,1)}, bf16[1,64,1024]{1,2,0:T(8,128)(2,1)}, u32[]{:S(2)}, u32[]{:S(2)}) collective-permute-start(bf16[1,64,1024]{1,2,0:T(8,128)(2,1)} %select_convert_fusion.1), channel_id=1, source_target_pairs={{0,16},{8,24},{16,0},{24,8},{32,48},{40,56},{48,32},{56,40},{64,80... | collective-permute-start | bytes 393224 | tf_op jit(solution)/shard_map/ppermute | solution.py:16
  325.9 2.7 copy-start.10
  326.8 16.7 %collective-permute-start.13 = (bf16[1,64,1024]{1,2,0:T(8,128)(2,1)}, bf16[1,64,1024]{1,2,0:T(8,128)(2,1)}, u32[]{:S(2)}, u32[]{:S(2)}) collective-permute-start(bf16[1,64,1024]{1,2,0:T(8,128)(2,1)} %select_convert_fusion.3), channel_id=1, source_target_pairs={{0,8},{8,0},{16,24},{24,16},{32,40},{40,32},{48,56},{56,48},{64,72... | collective-permute-start | bytes 393224 | tf_op jit(solution)/shard_map/ppermute | solution.py:16
  337.5 4.0 copy-start.9
  337.5 6.0 copy-start.11
  339.6 5.2 collective-permute-start.8
  343.5 1.7 collective-permute-start.17
  345.9 4.3 copy-start.12
  345.9 4.3 copy-start.13
  349.9 532.6 %copy-start.1 = (bf16[1,512,2048]{2,1,0:T(8,128)(2,1)S(1)}, bf16[1,512,2048]{2,1,0:T(8,128)(2,1)}, u32[]{:S(2)}) copy-start(bf16[1,512,2048]{2,1,0:T(8,128)(2,1)} %param.11) | copy-start | bytes 6291460
Sparse Core Ops, SparseCore 0:
  23.0 50.9 all-gather.4
  75.7 47.8 all-gather.2
  222.8 659.6 reduce-scatter.1
where the time goes:
time: 897 us; the launch traced here: 889 us
  waiting for transfers between devices  581 us (65%)
  matrix products  90.5 us (10%)
  other arithmetic  83.6 us (9%)
  local copies, waits for them, and re-layouts  72.1 us (8%)
  blocking collectives  32.3 us (4%)
  between operations  15.4 us (2%)
  starting transfers between devices  14.7 us (2%)
    reduce_scatter x1, waiting for transfers between devices, body(): lax.psum_scatter(lax.dot_general(attention_flat, cotangent_flat, (((0,),...  531 us
    dot_general x12, matrix products, attend(): jnp.einsum('qhe,khe->hqk', query_f, key_f.reshape(width, HEADS, HEAD_DIM))  44.6 us
    all_gather x1, waiting for transfers between devices, body(): lax.all_gather(stacked_vals, 'ctx', axis=1, tiled=True)  32.5 us
    unnamed x1, blocking collectives  32.3 us
    dot_general x3, matrix products, attend(): jnp.einsum('hqk,khe->qhe', weights.astype(jnp.float32), jnp.concatenate(v...  31 us
    mul x1, other arithmetic, attend(): expo = jnp.exp(scores - top)  23.8 us
    unnamed x94, local copies, waits for them, and re-layouts  19.1 us
  transfers between devices with their start and end apart: 21, of which 5 were waited for; matrix products, arithmetic and copies ran while one was open for 15% of the time, Pallas kernels for 0%

commit v1 on v0

v1 whole, which is shorter than its diff:
```python
from functools import partial
import math

import jax
import jax.numpy as jnp
import numpy as np
from jax import lax
from jax.experimental import pallas as pl
from jax.experimental.pallas import tpu as pltpu
from jax.sharding import PartitionSpec as P

HEADS = 8
HEAD_DIM = 128
HD = 1024
D = 2048
ROWS = 512
GROUPS = 2
PER = HEADS // GROUPS
COLS = PER * HEAD_DIM
FACTORS = (4, 8, 16)
COARSE = tuple(ROWS // factor for factor in FACTORS)
SCALE = 1.0 / math.sqrt(HEAD_DIM)
BIG = float(2**30)
F32 = jnp.float32
BF16 = jnp.bfloat16
VMEM_LIMIT = 48 * 1024 * 1024


def params(**kwargs):
    return pltpu.CompilerParams(vmem_limit_bytes=VMEM_LIMIT, **kwargs)


def swap(array, axis, bits):
    return lax.ppermute(array, axis, [(i, i ^ bits) for i in range(lax.axis_size(axis))])


def shift(array, axis, step):
    size = lax.axis_size(axis)
    return lax.ppermute(array, axis, [(i, (i + step) % size) for i in range(size)])


def dot_nt(a, b):
    return lax.dot_general(a, b, (((1,), (1,)), ((), ())), preferred_element_type=F32)


def dot_nn(a, b):
    return lax.dot_general(a, b, (((1,), (0,)), ((), ())), preferred_element_type=F32)


def dot_tn(a, b):
    return lax.dot_general(a, b, (((0,), (0,)), ((), ())), preferred_element_type=F32)


def iota(shape, dim):
    return lax.broadcasted_iota(jnp.int32, shape, dim)


def offset_parts(factor):
    rest = math.log(factor) / SCALE
    parts = []
    for _ in range(3):
        part = float(np.asarray(rest, dtype=jnp.bfloat16))
        parts.append(part)
        rest = rest - part
    return parts


def pool_matrices():
    pools, picks = [], []
    for factor, count in zip(FACTORS, COARSE):
        row, col = iota((count, ROWS), 0), iota((count, ROWS), 1)
        inside = (col >= row * factor) & (col < row * factor + factor)
        pools.append(jnp.where(inside, 1.0 / factor, 0.0))
        picks.append(jnp.where(col == row * factor, 1.0, 0.0))
    return jnp.concatenate(pools, 0).astype(BF16), jnp.concatenate(picks, 0).astype(BF16)


def pool_kernel(with_features, *refs):
    if with_features:
        seg_ref, refs = refs[0], refs[1:]
    keys, values = refs[:PER], refs[PER : 2 * PER]
    outs = refs[2 * PER : 2 * PER + 3]
    pool, pick = pool_matrices()
    starts = np.cumsum((0,) + COARSE)

    def put(rows, column):
        for place, out in enumerate(outs):
            out[:, column : column + HEAD_DIM] = rows[starts[place] : starts[place + 1]].astype(BF16)

    for place, ref in enumerate(keys + values):
        put(dot_nn(pool, ref[...]), place * HEAD_DIM)
    if with_features:
        query_feature, key_feature = refs[2 * PER + 3 :]
        seg = seg_ref[...]
        kind = iota((8, ROWS), 0)
        rows = jnp.where(kind < 2, jnp.where(seg == kind, 1.0, 0.0), jnp.where(kind == 2, 1.0, 0.0)).astype(BF16)
        i, j = iota((8, HEAD_DIM), 0), iota((8, HEAD_DIM), 1)
        to_key = jnp.where((i < 2) & (i == j), 1.0, 0.0).astype(BF16)
        wrong = ((i == 0) & (j == 1)) | ((i == 1) & (j == 0))
        ones = (i == 2) & (j >= 2) & (j < 5)
        to_query = jnp.where(wrong, -BIG, jnp.where(ones, 1.0, 0.0)).astype(BF16)
        own = dot_tn(rows, to_key).astype(BF16)
        key_feature[...] = own
        query_feature[...] = dot_tn(rows, to_query).astype(BF16)
        picked = dot_nn(pick, own)
        lane = iota((1, HEAD_DIM), 1)
        for place, (factor, out) in enumerate(zip(FACTORS, outs)):
            parts = offset_parts(factor)
            offset = jnp.where(lane == 2, parts[0], jnp.where(lane == 3, parts[1], jnp.where(lane == 4, parts[2], 0.0)))
            rows_here = picked[starts[place] : starts[place + 1]] + offset
            out[:, 2 * COLS : 2 * COLS + HEAD_DIM] = rows_here.astype(BF16)


def pool(key, value, seg, group):
    with_features = group == 0
    width = 2 * COLS + (HEAD_DIM if with_features else 0)
    heads = [pl.BlockSpec((ROWS, HEAD_DIM), lambda i, h=j * GROUPS + group: (0, h)) for j in range(PER)]
    whole = pl.BlockSpec(memory_space=pltpu.VMEM)
    shapes = [jax.ShapeDtypeStruct((count, width), BF16) for count in COARSE]
    if with_features:
        shapes = shapes + [jax.ShapeDtypeStruct((ROWS, HEAD_DIM), BF16)] * 2
    args = ([seg] if with_features else []) + [key] * PER + [value] * PER
    return pl.pallas_call(
        partial(pool_kernel, with_features),
        grid=(1,),
        out_shape=shapes,
        in_specs=([whole] if with_features else []) + heads + heads,
        out_specs=[whole] * len(shapes),
        compiler_params=params(),
        cost_estimate=pl.CostEstimate(flops=2 * 224 * ROWS * 2 * COLS, bytes_accessed=3 * ROWS * COLS * 2, transcendentals=0),
    )(*args)


CHUNKS = ((0, 256), (256, 256), (512, 128), (640, 128), (768, 128), (896, 128), (1024, 128), (1152, 128))
KEYS = 1280


def attention_kernel(*refs):
    refs = list(refs)
    q_ref, k_ref, v_ref, g_ref, fq_ref, fk_ref = refs[:6]
    ck, cv, cf = refs[6:12], refs[12:18], refs[18:24]
    refs = refs[24:]
    refs = refs[len(refs) - 10 :]
    o_ref, ot_ref, dq_ref, dk_ref, dv_ref, keep_ref, give_ref = refs[:7]
    scores, weights, work = refs[7:]
    q = q_ref[...]
    g = g_ref[...]
    query = jnp.concatenate([q, fq_ref[...]], 1)
    rate = SCALE * math.log2(math.e)

    def part(local, coarse, place):
        start, size = CHUNKS[place]
        return local[pl.ds(start, size), :] if place < 2 else coarse[place - 2][...]

    top = None
    for place, (start, size) in enumerate(CHUNKS):
        key = jnp.concatenate([part(k_ref, ck, place), part(fk_ref, cf, place)], 1)
        here = dot_nt(key, query) * rate
        scores[pl.ds(start, size), :] = here
        peak = jnp.max(here, 0, keepdims=True)
        top = peak if top is None else jnp.maximum(top, peak)
    total = None
    for start, size in CHUNKS:
        here = jnp.exp2(scores[pl.ds(start, size), :] - top)
        scores[pl.ds(start, size), :] = here
        add = jnp.sum(here, 0, keepdims=True)
        total = add if total is None else total + add
    inverse = 1.0 / total
    mixed = None
    for place, (start, size) in enumerate(CHUNKS):
        here = (scores[pl.ds(start, size), :] * inverse).astype(BF16)
        weights[pl.ds(start, size), :] = here
        add = dot_tn(part(v_ref, cv, place), here)
        mixed = add if mixed is None else mixed + add
    ot_ref[...] = mixed.astype(BF16)
    o_ref[...] = mixed.T.astype(BF16)
    delta = jnp.sum(g.astype(F32).T * mixed, 0, keepdims=True)
    grad_q = None
    for place, (start, size) in enumerate(CHUNKS):
        value, key = part(v_ref, cv, place), part(k_ref, ck, place)
        here = weights[pl.ds(start, size), :]
        slope = (here.astype(F32) * (dot_nt(value, g) - delta)).astype(BF16)
        grad_v = dot_nn(here, g)
        grad_k = dot_nn(slope, q) * SCALE
        add = dot_tn(key, slope)
        grad_q = add if grad_q is None else grad_q + add
        if place < 2:
            dk_ref[pl.ds(start, size), :] = grad_k
            dv_ref[pl.ds(start, size), :] = grad_v
        else:
            out, row = (keep_ref, start - 512) if place < 5 else (give_ref, start - 896)
            out[0, pl.ds(row, size), :] = grad_k.astype(BF16)
            out[1, pl.ds(row, size), :] = grad_v.astype(BF16)
    dq_ref[...] = (grad_q * SCALE).T.astype(BF16)


def attention(query, key, value, grad, fq, fk, pieces, features, earlier, group):
    head = pl.BlockSpec((ROWS, HEAD_DIM), lambda j: (0, j * GROUPS + group))
    fixed = pl.BlockSpec((ROWS, HEAD_DIM), lambda j: (0, 0))
    k_piece = pl.BlockSpec((128, HEAD_DIM), lambda j: (0, j))
    v_piece = pl.BlockSpec((128, HEAD_DIM), lambda j: (0, PER + j))
    f_piece = pl.BlockSpec((128, HEAD_DIM), lambda j: (0, 2 * PER))
    compact = pl.BlockSpec((ROWS, HEAD_DIM), lambda j: (0, j))
    back = pl.BlockSpec((2, 384, HEAD_DIM), lambda j: (0, 0, j))
    in_specs = [head] * 4 + [fixed] * 2 + [k_piece] * 6 + [v_piece] * 6 + [f_piece] * 6
    args = [query, key, value, grad, fq, fk] + pieces + pieces + features
    aliases = {}
    if earlier:
        in_specs = in_specs + [pl.BlockSpec(memory_space=pl.ANY)] * 2
        args = args + list(earlier)
        aliases = {24: 0, 25: 2}
    return pl.pallas_call(
        attention_kernel,
        grid=(PER,),
        in_specs=in_specs,
        out_specs=[
            head,
            pl.BlockSpec((HEAD_DIM, ROWS), lambda j: (j, 0)),
            head,
            compact,
            compact,
            back,
            back,
        ],
        out_shape=[
            jax.ShapeDtypeStruct((ROWS, HD), BF16),
            jax.ShapeDtypeStruct((COLS, ROWS), BF16),
            jax.ShapeDtypeStruct((ROWS, HD), BF16),
            jax.ShapeDtypeStruct((ROWS, COLS), F32),
            jax.ShapeDtypeStruct((ROWS, COLS), F32),
            jax.ShapeDtypeStruct((2, 384, COLS), BF16),
            jax.ShapeDtypeStruct((2, 384, COLS), BF16),
        ],
        scratch_shapes=[
            pltpu.VMEM((KEYS, ROWS), F32),
            pltpu.VMEM((KEYS, ROWS), BF16),
            pltpu.VMEM((8, 128), F32),
        ],
        input_output_aliases=aliases,
        compiler_params=params(),
        cost_estimate=pl.CostEstimate(
            flops=PER * 12 * ROWS * KEYS * HEAD_DIM, bytes_accessed=12 * ROWS * COLS * 2, transcendentals=PER * ROWS * KEYS
        ),
    )(*args)


def grad_weight_kernel(place_ref, ot_ref, c_ref, keep_ref, give_ref, lhs):
    @pl.when(pl.program_id(0) == 0)
    def _():
        core, y = place_ref[0], place_ref[1]
        for slot in range(2):
            half = core if slot == 0 else 1 - core
            for step in range(4):
                target = lax.rem(y + step, 4)
                for j in range(PER):
                    source = pl.multiple_of(j * 128 + half * 64 + target * 16, 16)
                    lhs[pl.ds(((slot * 4 + step) * PER + j) * 16, 16), :] = ot_ref[pl.ds(source, 16), :]

    out = dot_nn(lhs[...], c_ref[...])
    keep_ref[...] = out[: COLS // 2].astype(BF16)
    give_ref[...] = out[COLS // 2 :].astype(BF16)


def grad_weight_part(place, ot, cotangent):
    tile = 512
    shape = jax.ShapeDtypeStruct((COLS // 2, D), BF16)
    out = pl.BlockSpec((COLS // 2, tile), lambda n, s: (0, n))
    return pl.pallas_call(
        grad_weight_kernel,
        grid_spec=pltpu.PrefetchScalarGridSpec(
            num_scalar_prefetch=1,
            grid=(D // tile,),
            in_specs=[
                pl.BlockSpec((COLS, ROWS), lambda n, s: (0, 0)),
                pl.BlockSpec((ROWS, tile), lambda n, s: (0, n)),
            ],
            out_specs=[out, out],
            scratch_shapes=[pltpu.VMEM((COLS, ROWS), BF16)],
        ),
        out_shape=[shape, shape],
        compiler_params=params(),
        cost_estimate=pl.CostEstimate(flops=2 * COLS * ROWS * D, bytes_accessed=6 * 1024 * 1024, transcendentals=0),
    )(place, ot, cotangent)


def split_sum_kernel(count, axis, bounds, *refs):
    ins, outs = refs[:count], refs[count:]
    for (start, size), out in zip(bounds, outs):
        at = (slice(None),) * axis + (pl.ds(start, size),)
        total = ins[0][at].astype(F32)
        for ref in ins[1:]:
            total = total + ref[at].astype(F32)
        out[...] = total.astype(out.dtype)


def split_sum(arrays, axis, sizes):
    shape = arrays[0].shape
    starts = np.cumsum([0] + list(sizes))
    bounds = [(int(start), int(size)) for start, size in zip(starts, sizes)]
    whole = pl.BlockSpec(memory_space=pltpu.VMEM)
    outs = [jax.ShapeDtypeStruct(shape[:axis] + (size,) + shape[axis + 1 :], BF16) for size in sizes]
    count = math.prod(shape)
    return pl.pallas_call(
        partial(split_sum_kernel, len(arrays), axis, bounds),
        in_specs=[whole] * len(arrays),
        out_specs=[whole] * len(sizes),
        out_shape=outs,
        compiler_params=params(),
        cost_estimate=pl.CostEstimate(flops=count * len(arrays), bytes_accessed=2 * count * (len(arrays) + 1), transcendentals=0),
    )(*arrays)


def turn_sum_kernel(rows, place_ref, a_ref, b_ref, c_ref, d_ref, *outs):
    x = place_ref[2]
    for step, out in enumerate(outs):
        at = pl.ds(pl.multiple_of(lax.rem(x + step, 4) * rows, 16), rows)
        total = (a_ref[at, :].astype(F32) + b_ref[at, :].astype(F32)) + (c_ref[at, :].astype(F32) + d_ref[at, :].astype(F32))
        out[...] = total.astype(BF16)


def turn_sum(place, arrays):
    rows = arrays[0].shape[0] // 4
    whole = pl.BlockSpec(memory_space=pltpu.VMEM)
    out = jax.ShapeDtypeStruct((rows, D), BF16)
    return pl.pallas_call(
        partial(turn_sum_kernel, rows),
        in_specs=[pl.BlockSpec(memory_space=pltpu.SMEM)] + [whole] * 4,
        out_specs=[whole] * 4,
        out_shape=[out] * 4,
        compiler_params=params(),
        cost_estimate=pl.CostEstimate(flops=16 * rows * D, bytes_accessed=40 * rows * D, transcendentals=0),
    )(place, *arrays)


def finish_kernel(*refs):
    dk_ref, dv_ref, one, two, three, four = refs[:6]
    outs = refs[len(refs) - 2 :]
    token, row = iota((ROWS, 256), 0), iota((ROWS, 256), 1)
    spread = jnp.zeros((ROWS, 256), F32)
    start = 0
    for factor, count in ((4, 128), (8, 64), (16, 32), (16, 32)):
        local = row - start
        inside = (local >= 0) & (local < count) & (token >= local * factor) & (token < local * factor + factor)
        spread = jnp.where(inside, 1.0 / factor, spread)
        start = start + count
    spread = spread.astype(BF16)
    for place, (own, out) in enumerate(zip((dk_ref, dv_ref), outs)):
        rows = jnp.concatenate([ref[place] for ref in (one, two, three, four)], 0)
        out[...] = (own[...] + dot_nn(spread, rows)).astype(BF16)


def finish(dk, dv, returned, earlier, group):
    head = pl.BlockSpec((ROWS, HEAD_DIM), lambda j: (0, j * GROUPS + group))
    compact = pl.BlockSpec((ROWS, HEAD_DIM), lambda j: (0, j))
    in_specs = [compact] * 2 + [pl.BlockSpec((2, r.shape[1], HEAD_DIM), lambda j: (0, 0, j)) for r in returned]
    args = [dk, dv] + list(returned)
    aliases = {}
    if earlier:
        in_specs = in_specs + [pl.BlockSpec(memory_space=pl.ANY)] * 2
        args = args + list(earlier)
        aliases = {6: 0, 7: 1}
    shape = jax.ShapeDtypeStruct((ROWS, HD), BF16)
    return pl.pallas_call(
        finish_kernel,
        grid=(PER,),
        in_specs=in_specs,
        out_specs=[head, head],
        out_shape=[shape, shape],
        input_output_aliases=aliases,
        compiler_params=params(),
        cost_estimate=pl.CostEstimate(flops=4 * ROWS * 256 * COLS, bytes_accessed=14 * ROWS * COLS, transcendentals=0),
    )(*args)


def body(query, key, value, segment_ids, out_weight, cotangent):
    query, key, value = query[0], key[0], value[0]
    cotangent = cotangent[0]
    index = lax.axis_index("ctx")
    other = lax.axis_index("dp")
    core, x = jnp.bitwise_and(index, 1), jnp.right_shift(index, 2)
    z_lo = jnp.bitwise_and(jnp.right_shift(index, 1), 1)
    y, z_hi = jnp.right_shift(other, 1), jnp.bitwise_and(other, 1)
    place = jnp.stack([core, y, x]).astype(jnp.int32)

    pooled = []
    for group in range(GROUPS):
        outs = pool(key, value, segment_ids, group)
        if group == 0:
            fq, fk = outs[3:]
        pooled.append(outs[:3])
    pieces = []
    for one, two, three in pooled:
        from_z = swap(one, "ctx", 2)
        from_x = jnp.concatenate([swap(two, "ctx", 4), swap(three, "ctx", 12), swap(three, "ctx", 8)], 0)
        from_xz = swap(from_x, "ctx", 2)
        mine = [from_z, from_x, from_xz]
        pieces.append(mine + [swap(member, "ctx", 1) for member in mine])
    grad_attention = lax.dot_general(
        cotangent, out_weight, (((1,), (1,)), ((), ())), preferred_element_type=F32
    ).astype(BF16)

    earlier, ended, ends = (), (), []
    for group in range(GROUPS):
        o, ot, dq, dk, dv, keep, give = attention(
            query, key, value, grad_attention, fq, fk, pieces[group], pieces[0], earlier, group
        )
        earlier = (o, dq)
        own_one, own_two, own_xz = split_sum([keep, swap(give, "ctx", 1)], 1, (128, 128, 128))
        back_xz = swap(own_xz, "ctx", 2)
        back_z = swap(own_one, "ctx", 2)
        two, three, four = split_sum([own_two, back_xz], 1, (64, 32, 32))
        returned = [back_z, swap(two, "ctx", 4), swap(three, "ctx", 12), swap(four, "ctx", 8)]
        ended = finish(dk, dv, returned, ended, group)

        kept, given = grad_weight_part(place, ot, cotangent)
        quarter = COLS // 8
        parts = split_sum([kept, swap(given, "ctx", 1)], 0, (quarter,) * 4)
        parts = [parts[0]] + [shift(parts[step], "dp", 2 * step) for step in (1, 2, 3)]
        parts = turn_sum(place, parts)
        parts = [parts[0]] + [shift(parts[step], "ctx", 4 * step) for step in (1, 2, 3)]
        total = parts[0].astype(F32)
        for member in parts[1:]:
            total = total + member.astype(F32)
        ends.append(total)
    ends = jnp.concatenate(ends, 0).reshape(2, 16, D)
    kept = lax.dynamic_index_in_dim(ends, z_lo, 0, keepdims=False)
    given = lax.dynamic_index_in_dim(ends, 1 - z_lo, 0, keepdims=False)
    ends = (kept + swap(given.astype(BF16), "ctx", 2).astype(F32)).reshape(2, 8, D)
    kept = lax.dynamic_index_in_dim(ends, z_hi, 0, keepdims=False)
    given = lax.dynamic_index_in_dim(ends, 1 - z_hi, 0, keepdims=False)
    grad_weight = kept + swap(given, "dp", 1)

    output = lax.dot_general(o, out_weight, (((1,), (0,)), ((), ())), preferred_element_type=F32).astype(BF16)
    return output[None], dq[None], ended[0][None], ended[1][None], grad_weight


def solution(mesh):
    in_specs = (
        P("dp", "ctx", None),
        P("dp", "ctx", None),
        P("dp", "ctx", None),
        P("dp", "ctx"),
        P(),
        P("dp", "ctx", None),
    )
    out_specs = (
        P("dp", "ctx", None),
        P("dp", "ctx", None),
        P("dp", "ctx", None),
        P("dp", "ctx", None),
        P(("ctx", "dp"), None),
    )
    return jax.shard_map(body, mesh=mesh, in_specs=in_specs, out_specs=out_specs, check_vma=False)
```

time: 897 us -> 166 us (0.19)
  waiting for transfers between devices: 581 us -> 30.2 us
  other arithmetic: 83.6 us -> 1.72 us
  matrix products: 90.5 us -> 9.72 us
  local copies, waits for them, and re-layouts: 72.1 us -> 18.3 us
  Pallas kernels: 0 us -> 52.5 us
  starting transfers between devices: 14.7 us -> 50.7 us
  blocking collectives: 32.3 us -> 0 us
  between operations: 15.4 us -> 0.94 us
    reduce_scatter x1 -> x0, waiting for transfers between devices: 531 us -> none  [body(): lax.psum_scatter(lax.dot_general(attention_flat, cotangent_flat, (((0,),...]
    dot_general x18 -> x2, matrix products: 90.5 us -> 9.72 us  [the longest x1 6.31 us: body(): lax.dot_general(o, out_weight, (((1,), (0,)), ((), ())), preferred_elemen...]
    pallas_call x0 -> x16, Pallas kernels: none -> 52.5 us  [the longest x2 33.6 us: attention(): pl.pallas_call(attention_kernel, grid=(PER,), in_specs=in_specs, out_spec...]
    ppermute x18 -> x44, starting transfers between devices: 14.6 us -> 50.7 us  [the longest x32 32.7 us: swap(): lax.ppermute(array, axis, [(i, i ^ bits) for i in range(lax.axis_size(axi...]
    all_gather x2 -> x0, waiting for transfers between devices: 32.5 us -> none  [the longest x1 32.5 us: body(): lax.all_gather(stacked_vals, 'ctx', axis=1, tiled=True)]
    unnamed x1 -> x0, blocking collectives: 32.3 us -> none
    convert_element_type x31 -> x0, other arithmetic: 23.9 us -> none  [the longest x12 6.17 us: as_sent(): a.astype(jnp.bfloat16)]
    mul x1 -> x0, other arithmetic: 23.8 us -> none  [attend(): expo = jnp.exp(scores - top)]
  transfers between devices with their start and end apart: 21 -> 44, of which waited for: 5 -> 10; matrix products, arithmetic and copies ran while one was open for 15% -> 7% of each run, Pallas kernels for 0% -> 31%
where the time goes in v1:
time: 166 us; the launch traced here: 164 us
  Pallas kernels  52.5 us (32%)
  starting transfers between devices  50.7 us (31%)
  waiting for transfers between devices  30.2 us (18%)
  local copies, waits for them, and re-layouts  18.3 us (11%)
  matrix products  9.72 us (6%)
  other arithmetic  1.72 us (1%)
    pallas_call x2, Pallas kernels, attention(): pl.pallas_call(attention_kernel, grid=(PER,), in_specs=in_specs, out_spec...  33.6 us
    ppermute x32, starting transfers between devices, swap(): lax.ppermute(array, axis, [(i, i ^ bits) for i in range(lax.axis_size(axi...  32.7 us
    ppermute x32, waiting for transfers between devices, swap(): lax.ppermute(array, axis, [(i, i ^ bits) for i in range(lax.axis_size(axi...  18.8 us
    unnamed x76, local copies, waits for them, and re-layouts  18.3 us
    ppermute x12, starting transfers between devices, shift(): lax.ppermute(array, axis, [(i, (i + step) % size) for i in range(size)])  17.9 us
    ppermute x12, waiting for transfers between devices, shift(): lax.ppermute(array, axis, [(i, (i + step) % size) for i in range(size)])  11.5 us
    dot_general x1, matrix products, body(): lax.dot_general(o, out_weight, (((1,), (0,)), ((), ())), preferred_elemen...  6.31 us
    pallas_call x2, Pallas kernels, finish(): pl.pallas_call(finish_kernel, grid=(PER,), in_specs=in_specs, out_specs=[...  5.56 us
  transfers between devices with their start and end apart: 44, of which 10 were waited for; matrix products, arithmetic and copies ran while one was open for 7% of the time, Pallas kernels for 31%

profile of v1, /device:TPU:0, one launch (start us, length us, event | category | flops | bytes accessed | tf_op | source)
XLA Modules:
  0.0 164.1 jit_solution(12726151298282300624)
XLA Ops:
  0.6 1.2 copy-done
  1.9 1.2 copy-done.2
  3.8 1.0 shard_map.101
  4.8 1.7 %collective-permute-start.9 = (bf16[64,1152]{1,0:T(8,128)(2,1)S(1)}, bf16[64,1152]{1,0:T(8,128)(2,1)S(1)}, u32[]{:S(2)}, u32[]{:S(2)}) collective-permute-start(bf16[64,1152]{1,0:T(8,128)(2,1)S(1)} %get-tuple-element.69), channel_id=1, source_target_pairs={{0,32},{8,40},{16,48},{24,56},{32,0},{40,8},{48,16},{56,24},{64,96... | collective-permute-start | bytes 442376 | tf_op jit(solution)/shard_map/ppermute | solution.py:34
  6.5 2.1 %collective-permute-start.10 = (bf16[32,1152]{1,0:T(8,128)(2,1)S(1)}, bf16[32,1152]{1,0:T(8,128)(2,1)S(1)}, u32[]{:S(2)}, u32[]{:S(2)}) collective-permute-start(bf16[32,1152]{1,0:T(8,128)(2,1)S(1)} %get-tuple-element.70), channel_id=1, source_target_pairs={{0,96},{8,104},{16,112},{24,120},{32,64},{40,72},{48,80},{56,88},{... | collective-permute-start | bytes 221192 | tf_op jit(solution)/shard_map/ppermute | solution.py:34
  9.2 1.4 shard_map.102
  10.6 2.6 %collective-permute-start.2 = (bf16[32,1024]{1,0:T(8,128)(2,1)S(1)}, bf16[32,1024]{1,0:T(8,128)(2,1)S(1)}, u32[]{:S(2)}, u32[]{:S(2)}) collective-permute-start(bf16[32,1024]{1,0:T(8,128)(2,1)S(1)} %get-tuple-element.67), channel_id=1, source_target_pairs={{0,96},{8,104},{16,112},{24,120},{32,64},{40,72},{48,80},{56,88},{... | collective-permute-start | bytes 196616 | tf_op jit(solution)/shard_map/ppermute | solution.py:34
  13.2 0.8 collective-permute-start.3
  14.0 1.9 %collective-permute-start.8 = (bf16[128,1152]{1,0:T(8,128)(2,1)S(1)}, bf16[128,1152]{1,0:T(8,128)(2,1)S(1)}, u32[]{:S(2)}, u32[]{:S(2)}) collective-permute-start(bf16[128,1152]{1,0:T(8,128)(2,1)S(1)} %get-tuple-element.68), channel_id=1, source_target_pairs={{0,16},{8,24},{16,0},{24,8},{32,48},{40,56},{48,32},{56,40},{64,80... | collective-permute-start | bytes 884744 | tf_op jit(solution)/shard_map/ppermute | solution.py:34
  16.0 0.7 collective-permute-start.1
  16.9 4.1 %collective-permute-done.1 = bf16[64,1024]{1,0:T(8,128)(2,1)S(1)} collective-permute-done((bf16[64,1024]{1,0:T(8,128)(2,1)S(1)}, bf16[64,1024]{1,0:T(8,128)(2,1)S(1)}, u32[]{:S(2)}, u32[]{:S(2)}) %collective-permute-start.1) | collective-permute-done | bytes 131104 | tf_op jit(solution)/shard_map/ppermute | solution.py:34
  21.2 2.0 %collective-permute-start.4 = (bf16[128,1024]{1,0:T(8,128)(2,1)S(1)}, bf16[128,1024]{1,0:T(8,128)(2,1)}, u32[]{:S(2)}, u32[]{:S(2)}) collective-permute-start(bf16[128,1024]{1,0:T(8,128)(2,1)S(1)} %constant_dynamic-update-slice_fusion.refs_7_.refs_13_), channel_id=1, source_target_pairs={{0,16},{8,24},{16,0},{24,8},{32,48},{40,56},{48,32},{56,40},{64,80... | collective-permute-start | bytes 786440 | tf_op jit(solution)/shard_map/ppermute | solution.py:34
  23.2 0.8 collective-permute-done.8.refs_6_.refs_12_.refs_18_
  24.0 11.9 %collective-permute-done.12.refs_8_.refs_14_.refs_20_ = bf16[128,1152]{1,0:T(8,128)(2,1)S(1)} collective-permute-done((bf16[128,1152]{1,0:T(8,128)(2,1)S(1)}, bf16[128,1152]{1,0:T(8,128)(2,1)S(1)}, u32[]{:S(2)}, u32[]{:S(2)}) %collective-permute-start.12) | collective-permute-done | bytes 294944 | tf_op jit(solution)/shard_map/ppermute | solution.py:34
  35.9 3.4 %convolution_convert_fusion.1.refs_3_ = bf16[512,1024]{1,0:T(8,128)(2,1)} fusion(bf16[1024,2048]{1,0:T(8,128)(2,1)S(1)} %copy-done.35, bf16[1,512,2048]{2,1,0:T(8,128)(2,1)S(1)} %copy-done.16), kind=kOutput, calls=%fused_computation.2 | convolution fusion | flops 2148007936 | bytes 7340032 | tf_op jit(solution)/shard_map/dot_general | solution.py:398
  41.9 1.0 copy-done.23
  42.9 1.0 copy-done.26
  43.8 0.9 copy-done.32
  44.8 16.9 %shard_map.103 = (bf16[512,1024]{1,0:T(8,128)(2,1)S(1)}, bf16[512,512]{1,0:T(8,128)(2,1)S(1)}, bf16[512,1024]{1,0:T(8,128)(2,1)}, f32[512,512]{1,0:T(8,128)S(1)}...) custom-call(bf16[512,1024]{1,0:T(8,128)(2,1)} %bitcast.56, ...), custom_call_target="tpu_custom_call" | custom-call | flops 4026531840 | bytes 6291456 | tf_op jit(solution)/shard_map/pallas_call | solution.py:212
  61.7 1.0 copy-done.34
  62.6 2.7 %shard_map.111 = (bf16[256,2048]{1,0:T(8,128)(2,1)S(1)}, bf16[256,2048]{1,0:T(8,128)(2,1)S(1)}) custom-call(s32[3]{0:T(128)S(1)} %pad_add_fusion.place_ref, bf16[512,512]{1,0:T(8,128)(2,1)S(1)} %get-tuple-element.99.ot_ref, bf16[512,2048]{1,0:T(8,128)(2,1)S(1)} %bitcast.50), custom_call_target="tpu_custom_call" | custom-call | flops 1073741824 | bytes 6291456 | tf_op jit(solution)/shard_map/pallas_call | solution.py:268
  65.7 1.0 copy-done.19
  66.7 1.0 copy-done.21
  67.7 0.9 copy-done.30
  68.6 16.7 %shard_map.104 = (bf16[512,1024]{1,0:T(8,128)(2,1)}, bf16[512,512]{1,0:T(8,128)(2,1)S(1)}, bf16[512,1024]{1,0:T(8,128)(2,1)}, f32[512,512]{1,0:T(8,128)}, f32[51...) custom-call(bf16[512,1024]{1,0:T(8,128)(2,1)} %bitcast.57, ...), custom_call_target="tpu_custom_call", output_to_operand_aliasing={{0}: (24, {}), {2}: (25, {})} | custom-call | flops 4026531840 | bytes 6291456 | tf_op jit(solution)/shard_map/pallas_call | solution.py:212
  85.3 2.7 %shard_map.114 = (bf16[256,2048]{1,0:T(8,128)(2,1)S(1)}, bf16[256,2048]{1,0:T(8,128)(2,1)S(1)}) custom-call(s32[3]{0:T(128)S(1)} %pad_add_fusion.place_ref, bf16[512,512]{1,0:T(8,128)(2,1)S(1)} %get-tuple-element.110.ot_ref, bf16[512,2048]{1,0:T(8,128)(2,1)S(1)} %bitcast.51), custom_call_target="tpu_custom_call" | custom-call | flops 1073741824 | bytes 6291456 | tf_op jit(solution)/shard_map/pallas_call | solution.py:268
  89.1 1.7 %collective-permute-start.29 = (bf16[64,2048]{1,0:T(8,128)(2,1)S(1)}, bf16[64,2048]{1,0:T(8,128)(2,1)S(1)}, u32[]{:S(2)}, u32[]{:S(2)}) collective-permute-start(bf16[64,2048]{1,0:T(8,128)(2,1)S(1)} %get-tuple-element.103), channel_id=1, source_target_pairs={{0,2},{1,3},{2,4},{3,5},{4,6},{5,7},{6,0},{7,1},{8,10},{9,11},{10,... | collective-permute-start | bytes 786440 | tf_op jit(solution)/shard_map/ppermute | solution.py:39
  90.7 2.9 %collective-permute-start.30 = (bf16[64,2048]{1,0:T(8,128)(2,1)S(1)}, bf16[64,2048]{1,0:T(8,128)(2,1)S(1)}, u32[]{:S(2)}, u32[]{:S(2)}) collective-permute-start(bf16[64,2048]{1,0:T(8,128)(2,1)S(1)} %get-tuple-element.104), channel_id=1, source_target_pairs={{0,4},{1,5},{2,6},{3,7},{4,0},{5,1},{6,2},{7,3},{8,12},{9,13},{10,... | collective-permute-start | bytes 786440 | tf_op jit(solution)/shard_map/ppermute | solution.py:39
  93.6 1.3 collective-permute-start.31
  95.0 1.0 shard_map.115
  96.7 2.3 %collective-permute-done.29.b_ref = bf16[64,2048]{1,0:T(8,128)(2,1)S(1)} collective-permute-done((bf16[64,2048]{1,0:T(8,128)(2,1)S(1)}, bf16[64,2048]{1,0:T(8,128)(2,1)S(1)}, u32[]{:S(2)}, u32[]{:S(2)}) %collective-permute-start.29) | collective-permute-done | bytes 262176 | tf_op jit(solution)/shard_map/ppermute | solution.py:39
  98.9 1.0 collective-permute-start.36
  99.9 6.5 %collective-permute-done.30.c_ref = bf16[64,2048]{1,0:T(8,128)(2,1)S(1)} collective-permute-done((bf16[64,2048]{1,0:T(8,128)(2,1)S(1)}, bf16[64,2048]{1,0:T(8,128)(2,1)S(1)}, u32[]{:S(2)}, u32[]{:S(2)}) %collective-permute-start.30) | collective-permute-done | bytes 262176 | tf_op jit(solution)/shard_map/ppermute | solution.py:39
  107.1 1.6 collective-permute-start.38
  108.6 1.2 shard_map.113
  109.9 0.9 copy-done.7
  111.4 2.9 %collective-permute-start.33 = (bf16[16,2048]{1,0:T(8,128)(2,1)}, bf16[16,2048]{1,0:T(8,128)(2,1)}, u32[]{:S(2)}, u32[]{:S(2)}) collective-permute-start(bf16[16,2048]{1,0:T(8,128)(2,1)} %get-tuple-element.108), channel_id=1, source_target_pairs={{0,64},{8,72},{16,80},{24,88},{32,96},{40,104},{48,112},{56,120},{... | collective-permute-start | bytes 196616 | tf_op jit(solution)/shard_map/ppermute | solution.py:39
  115.0 1.8 %collective-permute-start.34 = (bf16[16,2048]{1,0:T(8,128)(2,1)S(1)}, bf16[16,2048]{1,0:T(8,128)(2,1)}, u32[]{:S(2)}, u32[]{:S(2)}) collective-permute-start(bf16[16,2048]{1,0:T(8,128)(2,1)S(1)} %get-tuple-element.109), channel_id=1, source_target_pairs={{0,96},{8,104},{16,112},{24,120},{32,0},{40,8},{48,16},{56,24},{64... | collective-permute-start | bytes 196616 | tf_op jit(solution)/shard_map/ppermute | solution.py:39
  116.8 1.1 copy-done.8
  118.0 0.8 shard_map.107
  118.8 0.9 shard_map.105
  120.4 1.9 %collective-permute-start.24 = (bf16[2,128,512]{2,1,0:T(8,128)(2,1)}, bf16[2,128,512]{2,1,0:T(8,128)(2,1)S(1)}, u32[]{:S(2)}, u32[]{:S(2)}) collective-permute-start(bf16[2,128,512]{2,1,0:T(8,128)(2,1)} %get-tuple-element.91), channel_id=1, source_target_pairs={{0,16},{8,24},{16,0},{24,8},{32,48},{40,56},{48,32},{56,40},{64,80... | collective-permute-start | bytes 786440 | tf_op jit(solution)/shard_map/ppermute | solution.py:34
  122.4 0.9 copy-done.12
  123.4 0.9 copy-done.14
  124.3 1.2 shard_map.116
  125.8 1.4 collective-permute-start.40
  127.2 1.8 %collective-permute-start.41 = (bf16[16,2048]{1,0:T(8,128)(2,1)S(1)}, bf16[16,2048]{1,0:T(8,128)(2,1)S(1)}, u32[]{:S(2)}, u32[]{:S(2)}) collective-permute-start(bf16[16,2048]{1,0:T(8,128)(2,1)S(1)} %get-tuple-element.120), channel_id=1, source_target_pairs={{0,96},{8,104},{16,112},{24,120},{32,0},{40,8},{48,16},{56,24},{64... | collective-permute-start | bytes 196616 | tf_op jit(solution)/shard_map/ppermute | solution.py:39
  129.0 0.9 convert_add_fusion.1
  129.9 1.8 %collective-permute-done.39 = bf16[16,2048]{1,0:T(8,128)(2,1)S(1)} collective-permute-done((bf16[16,2048]{1,0:T(8,128)(2,1)S(1)}, bf16[16,2048]{1,0:T(8,128)(2,1)S(1)}, u32[]{:S(2)}, u32[]{:S(2)}) %collective-permute-start.39) | collective-permute-done | bytes 65568 | tf_op jit(solution)/shard_map/ppermute | solution.py:39
  131.8 0.9 collective-permute-done.41
  132.7 2.0 %collective-permute-start.42 = (bf16[16,2048]{1,0:T(8,128)(2,1)S(1)}, bf16[16,2048]{1,0:T(8,128)(2,1)S(1)}, u32[]{:S(2)}, u32[]{:S(2)}) collective-permute-start(bf16[16,2048]{1,0:T(8,128)(2,1)S(1)} %fusion.2), channel_id=1, source_target_pairs={{0,16},{8,24},{16,0},{24,8},{32,48},{40,56},{48,32},{56,40},{64,80... | collective-permute-start | bytes 196616 | tf_op jit(solution)/shard_map/ppermute | solution.py:34
  134.8 1.9 %collective-permute-start.17 = (bf16[2,128,512]{2,1,0:T(8,128)(2,1)}, bf16[2,128,512]{2,1,0:T(8,128)(2,1)S(1)}, u32[]{:S(2)}, u32[]{:S(2)}) collective-permute-start(bf16[2,128,512]{2,1,0:T(8,128)(2,1)} %copy-done.27), channel_id=1, source_target_pairs={{0,16},{8,24},{16,0},{24,8},{32,48},{40,56},{48,32},{56,40},{64,80... | collective-permute-start | bytes 786440 | tf_op jit(solution)/shard_map/ppermute | solution.py:34
  136.7 0.9 copy-done.10
  137.7 1.4 collective-permute-start.25
  139.2 1.4 collective-permute-start.26
  140.6 1.5 collective-permute-start.27
  142.1 1.3 collective-permute-done.23.refs_2_
  143.5 1.0 collective-permute-start.19
  144.6 1.4 collective-permute-start.20
  146.4 1.5 collective-permute-start.21
  147.9 3.6 %collective-permute-start.43 = (f32[8,2048]{1,0:T(8,128)S(1)}, f32[8,2048]{1,0:T(8,128)S(1)}, u32[]{:S(2)}, u32[]{:S(2)}) collective-permute-start(f32[8,2048]{1,0:T(8,128)S(1)} %dynamic-slice_bitcast_fusion), channel_id=1, source_target_pairs={{0,1},{1,0},{2,3},{3,2},{4,5},{5,4},{6,7},{7,6},{8,9},{9,8},{10,11... | collective-permute-start | bytes 196616 | tf_op jit(solution)/shard_map/ppermute | solution.py:34
  151.5 6.3 %fusion = bf16[1,512,2048]{2,1,0:T(8,128)(2,1)} fusion(bf16[512,1024]{1,0:T(8,128)(2,1)} %get-tuple-element.73, bf16[1024,2048]{1,0:T(8,128)(2,1)} %param.10), kind=kOutput, calls=%fused_computation.1 | convolution fusion | flops 2148532224 | bytes 7340032 | tf_op jit(solution)/shard_map/dot_general | solution.py:433
  157.8 2.8 %shard_map.109 = (bf16[512,1024]{1,0:T(8,128)(2,1)}, bf16[512,1024]{1,0:T(8,128)(2,1)}) custom-call(f32[512,512]{1,0:T(8,128)S(1)} %get-tuple-element.85.refs_0_, f32[512,512]{1,0:T(8,128)S(1)} %copy-done.4, bf16[2,128,512]{2,1,0:T(8,128)(2,1)S(1)} %collective-permute-done.23.refs_2_, bf16[2,64,512]{2,1,0:T(8,128)(2,1)S(1)} %collective-permute-done.25.refs_3_, ...), custom_call_target="tpu_custom_call" | custom-call | flops 268435456 | bytes 3670016 | tf_op jit(solution)/shard_map/pallas_call | solution.py:363
  160.6 2.8 %shard_map.110 = (bf16[512,1024]{1,0:T(8,128)(2,1)}, bf16[512,1024]{1,0:T(8,128)(2,1)}) custom-call(f32[512,512]{1,0:T(8,128)S(1)} %copy-done.5, f32[512,512]{1,0:T(8,128)S(1)} %copy-done.6, bf16[2,128,512]{2,1,0:T(8,128)(2,1)S(1)} %collective-permute-done.17.refs_2_, ...), custom_call_target="tpu_custom_call", output_to_operand_aliasing={{0}: (6, {}), {1}: (7, {})} | custom-call | flops 268435456 | bytes 3670016 | tf_op jit(solution)/shard_map/pallas_call | solution.py:363
  (128 shorter events, 11.2 us)
Async XLA Ops:
  0.6 1.2 copy-start
  1.9 1.2 copy-start.2
  3.8 5.4 %copy-start.1 = (bf16[1,512,1024]{2,1,0:T(8,128)(2,1)S(1)}, bf16[1,512,1024]{2,1,0:T(8,128)(2,1)}, u32[]{:S(2)}) copy-start(bf16[1,512,1024]{2,1,0:T(8,128)(2,1)} %param.7) | copy-start | bytes 3145732
  3.8 5.4 %copy-start.3 = (bf16[1,512,1024]{2,1,0:T(8,128)(2,1)S(1)}, bf16[1,512,1024]{2,1,0:T(8,128)(2,1)}, u32[]{:S(2)}) copy-start(bf16[1,512,1024]{2,1,0:T(8,128)(2,1)} %param.8) | copy-start | bytes 3145732
  4.8 5.8 %copy-start.31 = (bf16[512,128]{1,0:T(8,128)(2,1)}, bf16[512,128]{1,0:T(8,128)(2,1)S(1)}, u32[]{:S(2)}) copy-start(bf16[512,128]{1,0:T(8,128)(2,1)S(1)} %get-tuple-element.64.refs_5_) | copy-start | bytes 393220
  4.8 37.1 %copy-start.29 = (bf16[512,128]{1,0:T(8,128)(2,1)}, bf16[512,128]{1,0:T(8,128)(2,1)S(1)}, u32[]{:S(2)}) copy-start(bf16[512,128]{1,0:T(8,128)(2,1)S(1)} %get-tuple-element.63.refs_4_) | copy-start | bytes 393220
  4.8 9.2 %collective-permute-start.9 = (bf16[64,1152]{1,0:T(8,128)(2,1)S(1)}, bf16[64,1152]{1,0:T(8,128)(2,1)S(1)}, u32[]{:S(2)}, u32[]{:S(2)}) collective-permute-start(bf16[64,1152]{1,0:T(8,128)(2,1)S(1)} %get-tuple-element.69), channel_id=1, source_target_pairs={{0,32},{8,40},{16,48},{24,56},{32,0},{40,8},{48,16},{56,24},{64,96... | collective-permute-start | bytes 442376 | tf_op jit(solution)/shard_map/ppermute | solution.py:34
  6.4 29.5 %copy-start.16 = (bf16[1,512,2048]{2,1,0:T(8,128)(2,1)S(1)}, bf16[1,512,2048]{2,1,0:T(8,128)(2,1)}, u32[]{:S(2)}) copy-start(bf16[1,512,2048]{2,1,0:T(8,128)(2,1)} %param.11) | copy-start | bytes 6291460
  6.4 29.5 %copy-start.35 = (bf16[1024,2048]{1,0:T(8,128)(2,1)S(1)}, bf16[1024,2048]{1,0:T(8,128)(2,1)}, u32[]{:S(2)}) copy-start(bf16[1024,2048]{1,0:T(8,128)(2,1)} %param.10) | copy-start | bytes 12582916
  6.5 9.5 %collective-permute-start.10 = (bf16[32,1152]{1,0:T(8,128)(2,1)S(1)}, bf16[32,1152]{1,0:T(8,128)(2,1)S(1)}, u32[]{:S(2)}, u32[]{:S(2)}) collective-permute-start(bf16[32,1152]{1,0:T(8,128)(2,1)S(1)} %get-tuple-element.70), channel_id=1, source_target_pairs={{0,96},{8,104},{16,112},{24,120},{32,64},{40,72},{48,80},{56,88},{... | collective-permute-start | bytes 221192 | tf_op jit(solution)/shard_map/ppermute | solution.py:34
  8.5 8.2 %collective-permute-start.11 = (bf16[32,1152]{1,0:T(8,128)(2,1)S(1)}, bf16[32,1152]{1,0:T(8,128)(2,1)S(1)}, u32[]{:S(2)}, u32[]{:S(2)}) collective-permute-start(bf16[32,1152]{1,0:T(8,128)(2,1)S(1)} %get-tuple-element.70), channel_id=1, source_target_pairs={{0,64},{8,72},{16,80},{24,88},{32,96},{40,104},{48,112},{56,120},{... | collective-permute-start | bytes 221192 | tf_op jit(solution)/shard_map/ppermute | solution.py:34
  10.6 10.6 %collective-permute-start.2 = (bf16[32,1024]{1,0:T(8,128)(2,1)S(1)}, bf16[32,1024]{1,0:T(8,128)(2,1)S(1)}, u32[]{:S(2)}, u32[]{:S(2)}) collective-permute-start(bf16[32,1024]{1,0:T(8,128)(2,1)S(1)} %get-tuple-element.67), channel_id=1, source_target_pairs={{0,96},{8,104},{16,112},{24,120},{32,64},{40,72},{48,80},{56,88},{... | collective-permute-start | bytes 196616 | tf_op jit(solution)/shard_map/ppermute | solution.py:34
  13.2 7.9 %collective-permute-start.3 = (bf16[32,1024]{1,0:T(8,128)(2,1)S(1)}, bf16[32,1024]{1,0:T(8,128)(2,1)S(1)}, u32[]{:S(2)}, u32[]{:S(2)}) collective-permute-start(bf16[32,1024]{1,0:T(8,128)(2,1)S(1)} %get-tuple-element.67), channel_id=1, source_target_pairs={{0,64},{8,72},{16,80},{24,88},{32,96},{40,104},{48,112},{56,120},{... | collective-permute-start | bytes 196616 | tf_op jit(solution)/shard_map/ppermute | solution.py:34
  14.0 9.9 %collective-permute-start.8 = (bf16[128,1152]{1,0:T(8,128)(2,1)S(1)}, bf16[128,1152]{1,0:T(8,128)(2,1)S(1)}, u32[]{:S(2)}, u32[]{:S(2)}) collective-permute-start(bf16[128,1152]{1,0:T(8,128)(2,1)S(1)} %get-tuple-element.68), channel_id=1, source_target_pairs={{0,16},{8,24},{16,0},{24,8},{32,48},{40,56},{48,32},{56,40},{64,80... | collective-permute-start | bytes 884744 | tf_op jit(solution)/shard_map/ppermute | solution.py:34
  16.0 5.0 %collective-permute-start.1 = (bf16[64,1024]{1,0:T(8,128)(2,1)S(1)}, bf16[64,1024]{1,0:T(8,128)(2,1)S(1)}, u32[]{:S(2)}, u32[]{:S(2)}) collective-permute-start(bf16[64,1024]{1,0:T(8,128)(2,1)S(1)} %get-tuple-element.66), channel_id=1, source_target_pairs={{0,32},{8,40},{16,48},{24,56},{32,0},{40,8},{48,16},{56,24},{64,96... | collective-permute-start | bytes 393224 | tf_op jit(solution)/shard_map/ppermute | solution.py:34
  16.7 22.7 %collective-permute-start = (bf16[128,1024]{1,0:T(8,128)(2,1)}, bf16[128,1024]{1,0:T(8,128)(2,1)}, u32[]{:S(2)}, u32[]{:S(2)}) collective-permute-start(bf16[128,1024]{1,0:T(8,128)(2,1)} %get-tuple-element.65), channel_id=1, source_target_pairs={{0,16},{8,24},{16,0},{24,8},{32,48},{40,56},{48,32},{56,40},{64,80... | collective-permute-start | bytes 786440 | tf_op jit(solution)/shard_map/ppermute | solution.py:34
  21.0 14.9 %collective-permute-start.12 = (bf16[128,1152]{1,0:T(8,128)(2,1)S(1)}, bf16[128,1152]{1,0:T(8,128)(2,1)S(1)}, u32[]{:S(2)}, u32[]{:S(2)}) collective-permute-start(bf16[128,1152]{1,0:T(8,128)(2,1)S(1)} %constant_dynamic-update-slice_fusion.3.refs_7_.refs_13_.refs_19_), channel_id=1, source_target_pairs={{0,16},{8,24},{16,0},{24,8},{32,48},{40,56},{48,32},{56,40},{64,80... | collective-permute-start | bytes 884744 | tf_op jit(solution)/shard_map/ppermute | solution.py:34
  21.2 18.8 %collective-permute-start.4 = (bf16[128,1024]{1,0:T(8,128)(2,1)S(1)}, bf16[128,1024]{1,0:T(8,128)(2,1)}, u32[]{:S(2)}, u32[]{:S(2)}) collective-permute-start(bf16[128,1024]{1,0:T(8,128)(2,1)S(1)} %constant_dynamic-update-slice_fusion.refs_7_.refs_13_), channel_id=1, source_target_pairs={{0,16},{8,24},{16,0},{24,8},{32,48},{40,56},{48,32},{56,40},{64,80... | collective-permute-start | bytes 786440 | tf_op jit(solution)/shard_map/ppermute | solution.py:34
  23.2 16.9 %collective-permute-start.14 = (bf16[128,1152]{1,0:T(8,128)(2,1)S(1)}, bf16[128,1152]{1,0:T(8,128)(2,1)S(1)}, u32[]{:S(2)}, u32[]{:S(2)}) collective-permute-start(bf16[128,1152]{1,0:T(8,128)(2,1)S(1)} %constant_dynamic-update-slice_fusion.3.refs_7_.refs_13_.refs_19_), channel_id=1, source_target_pairs={{0,8},{8,0},{16,24},{24,16},{32,40},{40,32},{48,56},{56,48},{64,72... | collective-permute-start | bytes 884744 | tf_op jit(solution)/shard_map/ppermute | solution.py:34
  24.0 16.5 %collective-permute-start.13 = (bf16[128,1152]{1,0:T(8,128)(2,1)S(1)}, bf16[128,1152]{1,0:T(8,128)(2,1)S(1)}, u32[]{:S(2)}, u32[]{:S(2)}) collective-permute-start(bf16[128,1152]{1,0:T(8,128)(2,1)S(1)} %collective-permute-done.8.refs_6_.refs_12_.refs_18_), channel_id=1, source_target_pairs={{0,8},{8,0},{16,24},{24,16},{32,40},{40,32},{48,56},{56,48},{64,72... | collective-permute-start | bytes 884744 | tf_op jit(solution)/shard_map/ppermute | solution.py:34
  35.9 6.0 %copy-start.18 = (bf16[128,1152]{1,0:T(8,128)(2,1)}, bf16[128,1152]{1,0:T(8,128)(2,1)S(1)}, u32[]{:S(2)}) copy-start(bf16[128,1152]{1,0:T(8,128)(2,1)S(1)} %collective-permute-done.12.refs_8_.refs_14_.refs_20_) | copy-start | bytes 884740
  35.9 5.3 %collective-permute-start.15 = (bf16[128,1152]{1,0:T(8,128)(2,1)S(1)}, bf16[128,1152]{1,0:T(8,128)(2,1)S(1)}, u32[]{:S(2)}, u32[]{:S(2)}) collective-permute-start(bf16[128,1152]{1,0:T(8,128)(2,1)S(1)} %collective-permute-done.12.refs_8_.refs_14_.refs_20_), channel_id=1, source_target_pairs={{0,8},{8,0},{16,24},{24,16},{32,40},{40,32},{48,56},{56,48},{64,72... | collective-permute-start | bytes 884744 | tf_op jit(solution)/shard_map/ppermute | solution.py:34
  39.4 26.3 %collective-permute-start.6 = (bf16[128,1024]{1,0:T(8,128)(2,1)S(1)}, bf16[128,1024]{1,0:T(8,128)(2,1)S(1)}, u32[]{:S(2)}, u32[]{:S(2)}) collective-permute-start(bf16[128,1024]{1,0:T(8,128)(2,1)S(1)} %constant_dynamic-update-slice_fusion.refs_7_.refs_13_), channel_id=1, source_target_pairs={{0,8},{8,0},{16,24},{24,16},{32,40},{40,32},{48,56},{56,48},{64,72... | collective-permute-start | bytes 786440 | tf_op jit(solution)/shard_map/ppermute | solution.py:34
  40.0 25.8 %collective-permute-start.5 = (bf16[128,1024]{1,0:T(8,128)(2,1)}, bf16[128,1024]{1,0:T(8,128)(2,1)S(1)}, u32[]{:S(2)}, u32[]{:S(2)}) collective-permute-start(bf16[128,1024]{1,0:T(8,128)(2,1)} %collective-permute-done.refs_6_.refs_12_), channel_id=1, source_target_pairs={{0,8},{8,0},{16,24},{24,16},{32,40},{40,32},{48,56},{56,48},{64,72... | collective-permute-start | bytes 786440 | tf_op jit(solution)/shard_map/ppermute | solution.py:34
  40.1 21.6 %copy-start.20 = (bf16[128,1152]{1,0:T(8,128)(2,1)}, bf16[128,1152]{1,0:T(8,128)(2,1)S(1)}, u32[]{:S(2)}) copy-start(bf16[128,1152]{1,0:T(8,128)(2,1)S(1)} %collective-permute-done.14.refs_10_.refs_16_.refs_22_) | copy-start | bytes 884740
  40.1 25.6 %collective-permute-start.7 = (bf16[128,1024]{1,0:T(8,128)(2,1)}, bf16[128,1024]{1,0:T(8,128)(2,1)S(1)}, u32[]{:S(2)}, u32[]{:S(2)}) collective-permute-start(bf16[128,1024]{1,0:T(8,128)(2,1)} %collective-permute-done.4.refs_8_.refs_14_), channel_id=1, source_target_pairs={{0,8},{8,0},{16,24},{24,16},{32,40},{40,32},{48,56},{56,48},{64,72... | collective-permute-start | bytes 786440 | tf_op jit(solution)/shard_map/ppermute | solution.py:34
  41.9 1.0 copy-start.23
  44.8 17.9 %copy-start.17 = (bf16[1,512,2048]{2,1,0:T(8,128)(2,1)S(1)}, bf16[1,512,2048]{2,1,0:T(8,128)(2,1)}, u32[]{:S(2)}) copy-start(bf16[1,512,2048]{2,1,0:T(8,128)(2,1)} %param.11) | copy-start | bytes 6291460
  44.8 21.0 %copy-start.24 = (bf16[128,1152]{1,0:T(8,128)(2,1)S(1)}, bf16[128,1152]{1,0:T(8,128)(2,1)}, u32[]{:S(2)}) copy-start(bf16[128,1152]{1,0:T(8,128)(2,1)} %copy-done.22) | copy-start | bytes 884740
  44.8 21.0 %copy-start.33 = (bf16[512,128]{1,0:T(8,128)(2,1)S(1)}, bf16[512,128]{1,0:T(8,128)(2,1)}, u32[]{:S(2)}) copy-start(bf16[512,128]{1,0:T(8,128)(2,1)} %copy-done.31) | copy-start | bytes 393220
  65.3 23.5 %collective-permute-start.28 = (bf16[256,2048]{1,0:T(8,128)(2,1)S(1)}, bf16[256,2048]{1,0:T(8,128)(2,1)S(1)}, u32[]{:S(2)}, u32[]{:S(2)}) collective-permute-start(bf16[256,2048]{1,0:T(8,128)(2,1)S(1)} %get-tuple-element.101), channel_id=1, source_target_pairs={{0,8},{8,0},{16,24},{24,16},{32,40},{40,32},{48,56},{56,48},{64,72... | collective-permute-start | bytes 3145736 | tf_op jit(solution)/shard_map/ppermute | solution.py:34
  65.7 1.0 copy-start.19
  88.0 5.6 %collective-permute-start.35 = (bf16[256,2048]{1,0:T(8,128)(2,1)S(1)}, bf16[256,2048]{1,0:T(8,128)(2,1)S(1)}, u32[]{:S(2)}, u32[]{:S(2)}) collective-permute-start(bf16[256,2048]{1,0:T(8,128)(2,1)S(1)} %get-tuple-element.112), channel_id=1, source_target_pairs={{0,8},{8,0},{16,24},{24,16},{32,40},{40,32},{48,56},{56,48},{64,72... | collective-permute-start | bytes 3145736 | tf_op jit(solution)/shard_map/ppermute | solution.py:34
  88.3 21.5 %collective-permute-start.22 = (bf16[2,384,512]{2,1,0:T(8,128)(2,1)}, bf16[2,384,512]{2,1,0:T(8,128)(2,1)S(1)}, u32[]{:S(2)}, u32[]{:S(2)}) collective-permute-start(bf16[2,384,512]{2,1,0:T(8,128)(2,1)} %get-tuple-element.88), channel_id=1, source_target_pairs={{0,8},{8,0},{16,24},{24,16},{32,40},{40,32},{48,56},{56,48},{64,72... | collective-permute-start | bytes 2359304 | tf_op jit(solution)/shard_map/ppermute | solution.py:34
  88.6 22.8 %collective-permute-start.16 = (bf16[2,384,512]{2,1,0:T(8,128)(2,1)S(1)}, bf16[2,384,512]{2,1,0:T(8,128)(2,1)S(1)}, u32[]{:S(2)}, u32[]{:S(2)}) collective-permute-start(bf16[2,384,512]{2,1,0:T(8,128)(2,1)S(1)} %get-tuple-element.78), channel_id=1, source_target_pairs={{0,8},{8,0},{16,24},{24,16},{32,40},{40,32},{48,56},{56,48},{64,72... | collective-permute-start | bytes 2359304 | tf_op jit(solution)/shard_map/ppermute | solution.py:34
  89.1 9.8 %collective-permute-start.29 = (bf16[64,2048]{1,0:T(8,128)(2,1)S(1)}, bf16[64,2048]{1,0:T(8,128)(2,1)S(1)}, u32[]{:S(2)}, u32[]{:S(2)}) collective-permute-start(bf16[64,2048]{1,0:T(8,128)(2,1)S(1)} %get-tuple-element.103), channel_id=1, source_target_pairs={{0,2},{1,3},{2,4},{3,5},{4,6},{5,7},{6,0},{7,1},{8,10},{9,11},{10,... | collective-permute-start | bytes 786440 | tf_op jit(solution)/shard_map/ppermute | solution.py:39
  90.7 15.7 %collective-permute-start.30 = (bf16[64,2048]{1,0:T(8,128)(2,1)S(1)}, bf16[64,2048]{1,0:T(8,128)(2,1)S(1)}, u32[]{:S(2)}, u32[]{:S(2)}) collective-permute-start(bf16[64,2048]{1,0:T(8,128)(2,1)S(1)} %get-tuple-element.104), channel_id=1, source_target_pairs={{0,4},{1,5},{2,6},{3,7},{4,0},{5,1},{6,2},{7,3},{8,12},{9,13},{10,... | collective-permute-start | bytes 786440 | tf_op jit(solution)/shard_map/ppermute | solution.py:39
  93.6 13.4 %collective-permute-start.31 = (bf16[64,2048]{1,0:T(8,128)(2,1)S(1)}, bf16[64,2048]{1,0:T(8,128)(2,1)S(1)}, u32[]{:S(2)}, u32[]{:S(2)}) collective-permute-start(bf16[64,2048]{1,0:T(8,128)(2,1)S(1)} %get-tuple-element.105), channel_id=1, source_target_pairs={{0,6},{1,7},{2,0},{3,1},{4,2},{5,3},{6,4},{7,5},{8,14},{9,15},{10,... | collective-permute-start | bytes 786440 | tf_op jit(solution)/shard_map/ppermute | solution.py:39
  98.9 15.4 %collective-permute-start.36 = (bf16[64,2048]{1,0:T(8,128)(2,1)S(1)}, bf16[64,2048]{1,0:T(8,128)(2,1)S(1)}, u32[]{:S(2)}, u32[]{:S(2)}) collective-permute-start(bf16[64,2048]{1,0:T(8,128)(2,1)S(1)} %get-tuple-element.114), channel_id=1, source_target_pairs={{0,2},{1,3},{2,4},{3,5},{4,6},{5,7},{6,0},{7,1},{8,10},{9,11},{10,... | collective-permute-start | bytes 786440 | tf_op jit(solution)/shard_map/ppermute | solution.py:39
  106.4 14.0 %collective-permute-start.37 = (bf16[64,2048]{1,0:T(8,128)(2,1)}, bf16[64,2048]{1,0:T(8,128)(2,1)}, u32[]{:S(2)}, u32[]{:S(2)}) collective-permute-start(bf16[64,2048]{1,0:T(8,128)(2,1)} %get-tuple-element.115), channel_id=1, source_target_pairs={{0,4},{1,5},{2,6},{3,7},{4,0},{5,1},{6,2},{7,3},{8,12},{9,13},{10,... | collective-permute-start | bytes 786440 | tf_op jit(solution)/shard_map/ppermute | solution.py:39
  107.1 15.2 %collective-permute-start.38 = (bf16[64,2048]{1,0:T(8,128)(2,1)}, bf16[64,2048]{1,0:T(8,128)(2,1)}, u32[]{:S(2)}, u32[]{:S(2)}) collective-permute-start(bf16[64,2048]{1,0:T(8,128)(2,1)} %get-tuple-element.116), channel_id=1, source_target_pairs={{0,6},{1,7},{2,0},{3,1},{4,2},{5,3},{6,4},{7,5},{8,14},{9,15},{10,... | collective-permute-start | bytes 786440 | tf_op jit(solution)/shard_map/ppermute | solution.py:39
  110.7 14.7 %collective-permute-start.32 = (bf16[16,2048]{1,0:T(8,128)(2,1)}, bf16[16,2048]{1,0:T(8,128)(2,1)}, u32[]{:S(2)}, u32[]{:S(2)}) collective-permute-start(bf16[16,2048]{1,0:T(8,128)(2,1)} %get-tuple-element.107), channel_id=1, source_target_pairs={{0,32},{8,40},{16,48},{24,56},{32,64},{40,72},{48,80},{56,88},{64,... | collective-permute-start | bytes 196616 | tf_op jit(solution)/shard_map/ppermute | solution.py:39
  111.4 14.4 %collective-permute-start.33 = (bf16[16,2048]{1,0:T(8,128)(2,1)}, bf16[16,2048]{1,0:T(8,128)(2,1)}, u32[]{:S(2)}, u32[]{:S(2)}) collective-permute-start(bf16[16,2048]{1,0:T(8,128)(2,1)} %get-tuple-element.108), channel_id=1, source_target_pairs={{0,64},{8,72},{16,80},{24,88},{32,96},{40,104},{48,112},{56,120},{... | collective-permute-start | bytes 196616 | tf_op jit(solution)/shard_map/ppermute | solution.py:39
  115.0 12.2 %collective-permute-start.34 = (bf16[16,2048]{1,0:T(8,128)(2,1)S(1)}, bf16[16,2048]{1,0:T(8,128)(2,1)}, u32[]{:S(2)}, u32[]{:S(2)}) collective-permute-start(bf16[16,2048]{1,0:T(8,128)(2,1)S(1)} %get-tuple-element.109), channel_id=1, source_target_pairs={{0,96},{8,104},{16,112},{24,120},{32,0},{40,8},{48,16},{56,24},{64... | collective-permute-start | bytes 196616 | tf_op jit(solution)/shard_map/ppermute | solution.py:39
  116.8 1.1 copy-start.8
  118.8 3.6 %copy-start.28 = (bf16[2,128,512]{2,1,0:T(8,128)(2,1)}, bf16[2,128,512]{2,1,0:T(8,128)(2,1)S(1)}, u32[]{:S(2)}) copy-start(bf16[2,128,512]{2,1,0:T(8,128)(2,1)S(1)} %get-tuple-element.89) | copy-start | bytes 786436
  120.4 16.4 %collective-permute-start.24 = (bf16[2,128,512]{2,1,0:T(8,128)(2,1)}, bf16[2,128,512]{2,1,0:T(8,128)(2,1)S(1)}, u32[]{:S(2)}, u32[]{:S(2)}) collective-permute-start(bf16[2,128,512]{2,1,0:T(8,128)(2,1)} %get-tuple-element.91), channel_id=1, source_target_pairs={{0,16},{8,24},{16,0},{24,8},{32,48},{40,56},{48,32},{56,40},{64,80... | collective-permute-start | bytes 786440 | tf_op jit(solution)/shard_map/ppermute | solution.py:34
  122.3 16.9 %collective-permute-start.18 = (bf16[2,128,512]{2,1,0:T(8,128)(2,1)}, bf16[2,128,512]{2,1,0:T(8,128)(2,1)S(1)}, u32[]{:S(2)}, u32[]{:S(2)}) collective-permute-start(bf16[2,128,512]{2,1,0:T(8,128)(2,1)} %get-tuple-element.81), channel_id=1, source_target_pairs={{0,16},{8,24},{16,0},{24,8},{32,48},{40,56},{48,32},{56,40},{64,80... | collective-permute-start | bytes 786440 | tf_op jit(solution)/shard_map/ppermute | solution.py:34
  125.5 6.2 %collective-permute-start.39 = (bf16[16,2048]{1,0:T(8,128)(2,1)S(1)}, bf16[16,2048]{1,0:T(8,128)(2,1)S(1)}, u32[]{:S(2)}, u32[]{:S(2)}) collective-permute-start(bf16[16,2048]{1,0:T(8,128)(2,1)S(1)} %get-tuple-element.118), channel_id=1, source_target_pairs={{0,32},{8,40},{16,48},{24,56},{32,64},{40,72},{48,80},{56,88},{64,... | collective-permute-start | bytes 196616 | tf_op jit(solution)/shard_map/ppermute | solution.py:39
  125.8 6.0 %collective-permute-start.40 = (bf16[16,2048]{1,0:T(8,128)(2,1)S(1)}, bf16[16,2048]{1,0:T(8,128)(2,1)S(1)}, u32[]{:S(2)}, u32[]{:S(2)}) collective-permute-start(bf16[16,2048]{1,0:T(8,128)(2,1)S(1)} %get-tuple-element.119), channel_id=1, source_target_pairs={{0,64},{8,72},{16,80},{24,88},{32,96},{40,104},{48,112},{56,120},{... | collective-permute-start | bytes 196616 | tf_op jit(solution)/shard_map/ppermute | solution.py:39
  127.2 5.4 %collective-permute-start.41 = (bf16[16,2048]{1,0:T(8,128)(2,1)S(1)}, bf16[16,2048]{1,0:T(8,128)(2,1)S(1)}, u32[]{:S(2)}, u32[]{:S(2)}) collective-permute-start(bf16[16,2048]{1,0:T(8,128)(2,1)S(1)} %get-tuple-element.120), channel_id=1, source_target_pairs={{0,96},{8,104},{16,112},{24,120},{32,0},{40,8},{48,16},{56,24},{64... | collective-permute-start | bytes 196616 | tf_op jit(solution)/shard_map/ppermute | solution.py:39
  132.7 7.9 %collective-permute-start.42 = (bf16[16,2048]{1,0:T(8,128)(2,1)S(1)}, bf16[16,2048]{1,0:T(8,128)(2,1)S(1)}, u32[]{:S(2)}, u32[]{:S(2)}) collective-permute-start(bf16[16,2048]{1,0:T(8,128)(2,1)S(1)} %fusion.2), channel_id=1, source_target_pairs={{0,16},{8,24},{16,0},{24,8},{32,48},{40,56},{48,32},{56,40},{64,80... | collective-permute-start | bytes 196616 | tf_op jit(solution)/shard_map/ppermute | solution.py:34
  134.7 8.8 %collective-permute-start.23 = (bf16[2,128,512]{2,1,0:T(8,128)(2,1)}, bf16[2,128,512]{2,1,0:T(8,128)(2,1)S(1)}, u32[]{:S(2)}, u32[]{:S(2)}) collective-permute-start(bf16[2,128,512]{2,1,0:T(8,128)(2,1)} %copy-done.28), channel_id=1, source_target_pairs={{0,16},{8,24},{16,0},{24,8},{32,48},{40,56},{48,32},{56,40},{64,80... | collective-permute-start | bytes 786440 | tf_op jit(solution)/shard_map/ppermute | solution.py:34
  134.8 25.8 %collective-permute-start.17 = (bf16[2,128,512]{2,1,0:T(8,128)(2,1)}, bf16[2,128,512]{2,1,0:T(8,128)(2,1)S(1)}, u32[]{:S(2)}, u32[]{:S(2)}) collective-permute-start(bf16[2,128,512]{2,1,0:T(8,128)(2,1)} %copy-done.27), channel_id=1, source_target_pairs={{0,16},{8,24},{16,0},{24,8},{32,48},{40,56},{48,32},{56,40},{64,80... | collective-permute-start | bytes 786440 | tf_op jit(solution)/shard_map/ppermute | solution.py:34
  137.7 10.2 %collective-permute-start.25 = (bf16[2,64,512]{2,1,0:T(8,128)(2,1)S(1)}, bf16[2,64,512]{2,1,0:T(8,128)(2,1)S(1)}, u32[]{:S(2)}, u32[]{:S(2)}) collective-permute-start(bf16[2,64,512]{2,1,0:T(8,128)(2,1)S(1)} %get-tuple-element.92), channel_id=1, source_target_pairs={{0,32},{8,40},{16,48},{24,56},{32,0},{40,8},{48,16},{56,24},{64,96... | collective-permute-start | bytes 393224 | tf_op jit(solution)/shard_map/ppermute | solution.py:34
  139.2 5.5 %collective-permute-start.26 = (bf16[2,32,512]{2,1,0:T(8,128)(2,1)S(1)}, bf16[2,32,512]{2,1,0:T(8,128)(2,1)S(1)}, u32[]{:S(2)}, u32[]{:S(2)}) collective-permute-start(bf16[2,32,512]{2,1,0:T(8,128)(2,1)S(1)} %get-tuple-element.93), channel_id=1, source_target_pairs={{0,96},{8,104},{16,112},{24,120},{32,64},{40,72},{48,80},{56,88},{... | collective-permute-start | bytes 196616 | tf_op jit(solution)/shard_map/ppermute | solution.py:34
  140.6 5.8 %collective-permute-start.27 = (bf16[2,32,512]{2,1,0:T(8,128)(2,1)S(1)}, bf16[2,32,512]{2,1,0:T(8,128)(2,1)S(1)}, u32[]{:S(2)}, u32[]{:S(2)}) collective-permute-start(bf16[2,32,512]{2,1,0:T(8,128)(2,1)S(1)} %get-tuple-element.94), channel_id=1, source_target_pairs={{0,64},{8,72},{16,80},{24,88},{32,96},{40,104},{48,112},{56,120},{... | collective-permute-start | bytes 196616 | tf_op jit(solution)/shard_map/ppermute | solution.py:34
  143.5 17.1 %collective-permute-start.19 = (bf16[2,64,512]{2,1,0:T(8,128)(2,1)S(1)}, bf16[2,64,512]{2,1,0:T(8,128)(2,1)S(1)}, u32[]{:S(2)}, u32[]{:S(2)}) collective-permute-start(bf16[2,64,512]{2,1,0:T(8,128)(2,1)S(1)} %get-tuple-element.82), channel_id=1, source_target_pairs={{0,32},{8,40},{16,48},{24,56},{32,0},{40,8},{48,16},{56,24},{64,96... | collective-permute-start | bytes 393224 | tf_op jit(solution)/shard_map/ppermute | solution.py:34
  144.6 16.0 %collective-permute-start.20 = (bf16[2,32,512]{2,1,0:T(8,128)(2,1)S(1)}, bf16[2,32,512]{2,1,0:T(8,128)(2,1)S(1)}, u32[]{:S(2)}, u32[]{:S(2)}) collective-permute-start(bf16[2,32,512]{2,1,0:T(8,128)(2,1)S(1)} %get-tuple-element.83), channel_id=1, source_target_pairs={{0,96},{8,104},{16,112},{24,120},{32,64},{40,72},{48,80},{56,88},{... | collective-permute-start | bytes 196616 | tf_op jit(solution)/shard_map/ppermute | solution.py:34
  146.4 14.2 %collective-permute-start.21 = (bf16[2,32,512]{2,1,0:T(8,128)(2,1)S(1)}, bf16[2,32,512]{2,1,0:T(8,128)(2,1)S(1)}, u32[]{:S(2)}, u32[]{:S(2)}) collective-permute-start(bf16[2,32,512]{2,1,0:T(8,128)(2,1)S(1)} %get-tuple-element.84), channel_id=1, source_target_pairs={{0,64},{8,72},{16,80},{24,88},{32,96},{40,104},{48,112},{56,120},{... | collective-permute-start | bytes 196616 | tf_op jit(solution)/shard_map/ppermute | solution.py:34
  147.9 15.5 %collective-permute-start.43 = (f32[8,2048]{1,0:T(8,128)S(1)}, f32[8,2048]{1,0:T(8,128)S(1)}, u32[]{:S(2)}, u32[]{:S(2)}) collective-permute-start(f32[8,2048]{1,0:T(8,128)S(1)} %dynamic-slice_bitcast_fusion), channel_id=1, source_target_pairs={{0,1},{1,0},{2,3},{3,2},{4,5},{5,4},{6,7},{7,6},{8,9},{9,8},{10,11... | collective-permute-start | bytes 196616 | tf_op jit(solution)/shard_map/ppermute | solution.py:34
  151.5 6.3 %copy-start.4 = (f32[512,512]{1,0:T(8,128)S(1)}, f32[512,512]{1,0:T(8,128)}, u32[]{:S(2)}) copy-start(f32[512,512]{1,0:T(8,128)} %get-tuple-element.86.refs_1_) | copy-start | bytes 3145732
  151.5 9.1 %copy-start.5 = (f32[512,512]{1,0:T(8,128)S(1)}, f32[512,512]{1,0:T(8,128)}, u32[]{:S(2)}) copy-start(f32[512,512]{1,0:T(8,128)} %get-tuple-element.75.refs_0_) | copy-start | bytes 3145732
  151.5 9.1 %copy-start.6 = (f32[512,512]{1,0:T(8,128)S(1)}, f32[512,512]{1,0:T(8,128)}, u32[]{:S(2)}) copy-start(f32[512,512]{1,0:T(8,128)} %get-tuple-element.76.refs_1_) | copy-start | bytes 3145732
  (16 other events, 13.5 us)

commit v2 on v1

--- a/solution.py
+++ b/solution.py
@@ -14,7 +14,7 @@
 HD = 1024
 D = 2048
 ROWS = 512
-GROUPS = 2
+GROUPS = 1
 PER = HEADS // GROUPS
 COLS = PER * HEAD_DIM
 FACTORS = (4, 8, 16)
@@ -23,11 +23,10 @@
 BIG = float(2**30)
 F32 = jnp.float32
 BF16 = jnp.bfloat16
-VMEM_LIMIT = 48 * 1024 * 1024
-
-
-def params(**kwargs):
-    return pltpu.CompilerParams(vmem_limit_bytes=VMEM_LIMIT, **kwargs)
+
+
+def params(mebibytes):
+    return pltpu.CompilerParams(vmem_limit_bytes=mebibytes * 2**20)
 
 
 def swap(array, axis, bits):
@@ -126,122 +125,209 @@
         out_shape=shapes,
         in_specs=([whole] if with_features else []) + heads + heads,
         out_specs=[whole] * len(shapes),
-        compiler_params=params(),
+        compiler_params=params(16),
         cost_estimate=pl.CostEstimate(flops=2 * 224 * ROWS * 2 * COLS, bytes_accessed=3 * ROWS * COLS * 2, transcendentals=0),
     )(*args)
 
 
-CHUNKS = ((0, 256), (256, 256), (512, 128), (640, 128), (768, 128), (896, 128), (1024, 128), (1152, 128))
 KEYS = 1280
-
-
-def attention_kernel(*refs):
-    refs = list(refs)
+PAIRS = 3
+COARSE_ROWS = 768
+
+
+def pair(refs, place):
+    return jnp.concatenate([refs[2 * place][...], refs[2 * place + 1][...]], 0)
+
+
+def forward_kernel(*refs):
     q_ref, k_ref, v_ref, g_ref, fq_ref, fk_ref = refs[:6]
     ck, cv, cf = refs[6:12], refs[12:18], refs[18:24]
-    refs = refs[24:]
-    refs = refs[len(refs) - 10 :]
-    o_ref, ot_ref, dq_ref, dk_ref, dv_ref, keep_ref, give_ref = refs[:7]
-    scores, weights, work = refs[7:]
-    q = q_ref[...]
-    g = g_ref[...]
-    query = jnp.concatenate([q, fq_ref[...]], 1)
+    p_ref, o_ref, ot_ref, delta_ref, scores = refs[24:]
+    query = jnp.concatenate([q_ref[...], fq_ref[...]], 1)
     rate = SCALE * math.log2(math.e)
+    starts = range(0, KEYS, 256)
 
     def part(local, coarse, place):
-        start, size = CHUNKS[place]
-        return local[pl.ds(start, size), :] if place < 2 else coarse[place - 2][...]
+        return local[pl.ds(place * 256, 256), :] if place < 2 else pair(coarse, place - 2)
 
     top = None
-    for place, (start, size) in enumerate(CHUNKS):
+    for place, start in enumerate(starts):
         key = jnp.concatenate([part(k_ref, ck, place), part(fk_ref, cf, place)], 1)
         here = dot_nt(key, query) * rate
-        scores[pl.ds(start, size), :] = here
+        scores[pl.ds(start, 256), :] = here
         peak = jnp.max(here, 0, keepdims=True)
         top = peak if top is None else jnp.maximum(top, peak)
     total = None
-    for start, size in CHUNKS:
-        here = jnp.exp2(scores[pl.ds(start, size), :] - top)
-        scores[pl.ds(start, size), :] = here
+    for start in starts:
+        here = jnp.exp2(scores[pl.ds(start, 256), :] - top)
+        scores[pl.ds(start, 256), :] = here
         add = jnp.sum(here, 0, keepdims=True)
         total = add if total is None else total + add
     inverse = 1.0 / total
     mixed = None
-    for place, (start, size) in enumerate(CHUNKS):
-        here = (scores[pl.ds(start, size), :] * inverse).astype(BF16)
-        weights[pl.ds(start, size), :] = here
+    for place, start in enumerate(starts):
+        here = (scores[pl.ds(start, 256), :] * inverse).astype(BF16)
+        p_ref[0, pl.ds(start, 256), :] = here
         add = dot_tn(part(v_ref, cv, place), here)
         mixed = add if mixed is None else mixed + add
     ot_ref[...] = mixed.astype(BF16)
     o_ref[...] = mixed.T.astype(BF16)
-    delta = jnp.sum(g.astype(F32).T * mixed, 0, keepdims=True)
+    delta = jnp.sum(g_ref[...].astype(F32).T * mixed, 0, keepdims=True)
+    delta_ref[0] = jnp.broadcast_to(delta, (8, ROWS))
+
+
+HEAD = pl.BlockSpec((ROWS, HEAD_DIM), lambda j: (0, j))
+FIXED = pl.BlockSpec((ROWS, HEAD_DIM), lambda j: (0, 0))
+K_PIECE = pl.BlockSpec((128, HEAD_DIM), lambda j: (0, j))
+V_PIECE = pl.BlockSpec((128, HEAD_DIM), lambda j: (0, PER + j))
+F_PIECE = pl.BlockSpec((128, HEAD_DIM), lambda j: (0, 2 * PER))
+DELTA = pl.BlockSpec((1, 8, ROWS), lambda j: (j, 0, 0))
+ANY = pl.BlockSpec(memory_space=pl.ANY)
+
+
+def forward(query, key, value, grad, fq, fk, pieces):
+    return pl.pallas_call(
+        forward_kernel,
+        grid=(HEADS,),
+        in_specs=[HEAD] * 4 + [FIXED] * 2 + [K_PIECE] * 6 + [V_PIECE] * 6 + [F_PIECE] * 6,
+        out_specs=[
+            pl.BlockSpec((1, KEYS, ROWS), lambda j: (j, 0, 0)),
+            HEAD,
+            pl.BlockSpec((HEAD_DIM, ROWS), lambda j: (j, 0)),
+            DELTA,
+        ],
+        out_shape=[
+            jax.ShapeDtypeStruct((HEADS, KEYS, ROWS), BF16),
+            jax.ShapeDtypeStruct((ROWS, HD), BF16),
+            jax.ShapeDtypeStruct((HD, ROWS), BF16),
+            jax.ShapeDtypeStruct((HEADS, 8, ROWS), F32),
+        ],
+        scratch_shapes=[pltpu.VMEM((KEYS, ROWS), F32)],
+        compiler_params=params(20),
+        cost_estimate=pl.CostEstimate(
+            flops=HEADS * 4 * 4 * ROWS * KEYS * HEAD_DIM, bytes_accessed=20 * 2**20, transcendentals=HEADS * ROWS * KEYS
+        ),
+    )(query, key, value, grad, fq, fk, *pieces, *pieces, *pieces)
+
+
+def slope_of(weight, value, grad, delta):
+    return (weight.astype(F32) * (dot_nt(value, grad) - delta)).astype(BF16)
+
+
+def coarse_kernel(*refs):
+    q_ref, g_ref, delta_ref = refs[:3]
+    weights, ck, cv = refs[3:6], refs[6:12], refs[12:18]
+    keep_ref, give_ref, dq_ref = refs[19:]
+    q, g = q_ref[...], g_ref[...]
+    delta = delta_ref[0, 0:1, :]
     grad_q = None
-    for place, (start, size) in enumerate(CHUNKS):
-        value, key = part(v_ref, cv, place), part(k_ref, ck, place)
-        here = weights[pl.ds(start, size), :]
-        slope = (here.astype(F32) * (dot_nt(value, g) - delta)).astype(BF16)
-        grad_v = dot_nn(here, g)
-        grad_k = dot_nn(slope, q) * SCALE
+    for place in range(PAIRS):
+        weight, key, value = weights[place][0], pair(ck, place), pair(cv, place)
+        slope = slope_of(weight, value, g, delta)
+        grads = ((dot_nn(slope, q) * SCALE).astype(BF16), dot_nn(weight, g).astype(BF16))
+        for side, grad in enumerate(grads):
+            for half in range(2):
+                piece = 2 * place + half
+                out, row = (keep_ref, piece * 128) if piece < 3 else (give_ref, (piece - 3) * 128)
+                out[side, pl.ds(row, 128), :] = grad[half * 128 : half * 128 + 128]
         add = dot_tn(key, slope)
         grad_q = add if grad_q is None else grad_q + add
-        if place < 2:
-            dk_ref[pl.ds(start, size), :] = grad_k
-            dv_ref[pl.ds(start, size), :] = grad_v
-        else:
-            out, row = (keep_ref, start - 512) if place < 5 else (give_ref, start - 896)
-            out[0, pl.ds(row, size), :] = grad_k.astype(BF16)
-            out[1, pl.ds(row, size), :] = grad_v.astype(BF16)
+    dq_ref[...] = grad_q
+
+
+def coarse_backward(query, grad, delta, weights, pieces, after):
+    back = pl.BlockSpec((2, 384, HEAD_DIM), lambda j: (0, 0, j))
+    chunk = [pl.BlockSpec((1, 256, ROWS), lambda j, c=c: (j, c, 0)) for c in (2, 3, 4)]
+    return pl.pallas_call(
+        coarse_kernel,
+        grid=(HEADS,),
+        in_specs=[HEAD] * 2 + [DELTA] + chunk + [K_PIECE] * 6 + [V_PIECE] * 6 + [ANY],
+        out_specs=[back, back, pl.BlockSpec((HEAD_DIM, ROWS), lambda j: (j, 0))],
+        out_shape=[
+            jax.ShapeDtypeStruct((2, 384, HD), BF16),
+            jax.ShapeDtypeStruct((2, 384, HD), BF16),
+            jax.ShapeDtypeStruct((HD, ROWS), F32),
+        ],
+        compiler_params=params(20),
+        cost_estimate=pl.CostEstimate(
+            flops=HEADS * 4 * 4 * ROWS * COARSE_ROWS * HEAD_DIM, bytes_accessed=16 * 2**20, transcendentals=0
+        ),
+    )(query, grad, delta, weights, weights, weights, *pieces, *pieces, after)
+
+
+def local_kernel(q_ref, k_ref, v_ref, g_ref, delta_ref, p_ref, part_ref, _, dq_ref, dk_ref, dv_ref):
+    q, g = q_ref[...], g_ref[...]
+    delta = delta_ref[0, 0:1, :]
+    grad_q = part_ref[...]
+    for start in (0, 256):
+        at = pl.ds(start, 256)
+        weight = p_ref[0, at, :]
+        slope = slope_of(weight, v_ref[at, :], g, delta)
+        dk_ref[at, :] = dot_nn(slope, q) * SCALE
+        dv_ref[at, :] = dot_nn(weight, g)
+        grad_q = grad_q + dot_tn(k_ref[at, :], slope)
     dq_ref[...] = (grad_q * SCALE).T.astype(BF16)
 
 
-def attention(query, key, value, grad, fq, fk, pieces, features, earlier, group):
-    head = pl.BlockSpec((ROWS, HEAD_DIM), lambda j: (0, j * GROUPS + group))
-    fixed = pl.BlockSpec((ROWS, HEAD_DIM), lambda j: (0, 0))
-    k_piece = pl.BlockSpec((128, HEAD_DIM), lambda j: (0, j))
-    v_piece = pl.BlockSpec((128, HEAD_DIM), lambda j: (0, PER + j))
-    f_piece = pl.BlockSpec((128, HEAD_DIM), lambda j: (0, 2 * PER))
-    compact = pl.BlockSpec((ROWS, HEAD_DIM), lambda j: (0, j))
-    back = pl.BlockSpec((2, 384, HEAD_DIM), lambda j: (0, 0, j))
-    in_specs = [head] * 4 + [fixed] * 2 + [k_piece] * 6 + [v_piece] * 6 + [f_piece] * 6
-    args = [query, key, value, grad, fq, fk] + pieces + pieces + features
-    aliases = {}
-    if earlier:
-        in_specs = in_specs + [pl.BlockSpec(memory_space=pl.ANY)] * 2
-        args = args + list(earlier)
-        aliases = {24: 0, 25: 2}
-    return pl.pallas_call(
-        attention_kernel,
-        grid=(PER,),
-        in_specs=in_specs,
-        out_specs=[
-            head,
-            pl.BlockSpec((HEAD_DIM, ROWS), lambda j: (j, 0)),
-            head,
-            compact,
-            compact,
-            back,
-            back,
-        ],
+def local_backward(query, key, value, grad, delta, weights, partial_q, after):
+    return pl.pallas_call(
+        local_kernel,
+        grid=(HEADS,),
+        in_specs=[HEAD] * 4
+        + [DELTA, pl.BlockSpec((1, ROWS, ROWS), lambda j: (j, 0, 0)), pl.BlockSpec((HEAD_DIM, ROWS), lambda j: (j, 0)), ANY],
+        out_specs=[HEAD] * 3,
         out_shape=[
             jax.ShapeDtypeStruct((ROWS, HD), BF16),
-            jax.ShapeDtypeStruct((COLS, ROWS), BF16),
-            jax.ShapeDtypeStruct((ROWS, HD), BF16),
-            jax.ShapeDtypeStruct((ROWS, COLS), F32),
-            jax.ShapeDtypeStruct((ROWS, COLS), F32),
-            jax.ShapeDtypeStruct((2, 384, COLS), BF16),
-            jax.ShapeDtypeStruct((2, 384, COLS), BF16),
+            jax.ShapeDtypeStruct((ROWS, HD), F32),
+            jax.ShapeDtypeStruct((ROWS, HD), F32),
         ],
-        scratch_shapes=[
-            pltpu.VMEM((KEYS, ROWS), F32),
-            pltpu.VMEM((KEYS, ROWS), BF16),
-            pltpu.VMEM((8, 128), F32),
+        compiler_params=params(16),
+        cost_estimate=pl.CostEstimate(
+            flops=HEADS * 4 * 4 * ROWS * ROWS * HEAD_DIM, bytes_accessed=16 * 2**20, transcendentals=0
+        ),
+    )(query, key, value, grad, delta, weights, partial_q, after)
+
+
+def project_kernel(a_ref, w_ref, _, out_ref):
+    out_ref[...] = dot_nn(a_ref[...], w_ref[...]).astype(BF16)
+
+
+def project(attention, weight, after):
+    tile = 512
+    return pl.pallas_call(
+        project_kernel,
+        grid=(D // tile,),
+        in_specs=[
+            pl.BlockSpec((ROWS, HD), lambda n: (0, 0)),
+            pl.BlockSpec((HD, tile), lambda n: (0, n)),
+            ANY,
         ],
-        input_output_aliases=aliases,
-        compiler_params=params(),
-        cost_estimate=pl.CostEstimate(
-            flops=PER * 12 * ROWS * KEYS * HEAD_DIM, bytes_accessed=12 * ROWS * COLS * 2, transcendentals=PER * ROWS * KEYS
-        ),
-    )(*args)
+        out_specs=pl.BlockSpec((ROWS, tile), lambda n: (0, n)),
+        out_shape=jax.ShapeDtypeStruct((ROWS, D), BF16),
+        compiler_params=params(12),
+        cost_estimate=pl.CostEstimate(flops=2 * ROWS * HD * D, bytes_accessed=7 * 2**20, transcendentals=0),
+    )(attention, weight, after)
+
+
+def stack_kernel(*refs):
+    *ins, out = refs
+    start = 0
+    for ref in ins:
+        out[pl.ds(start, ref.shape[0]), :] = ref[...]
+        start = start + ref.shape[0]
+
+
+def stack(arrays):
+    rows, columns = sum(array.shape[0] for array in arrays), arrays[0].shape[1]
+    whole = pl.BlockSpec(memory_space=pltpu.VMEM)
+    return pl.pallas_call(
+        stack_kernel,
+        in_specs=[whole] * len(arrays),
+        out_specs=whole,
+        out_shape=jax.ShapeDtypeStruct((rows, columns), BF16),
+        compiler_params=params(4),
+        cost_estimate=pl.CostEstimate(flops=0, bytes_accessed=4 * rows * columns, transcendentals=0),
+    )(*arrays)
 
 
 def grad_weight_kernel(place_ref, ot_ref, c_ref, keep_ref, give_ref, lhs):
@@ -278,7 +364,7 @@
             scratch_shapes=[pltpu.VMEM((COLS, ROWS), BF16)],
         ),
         out_shape=[shape, shape],
-        compiler_params=params(),
+        compiler_params=params(16),
         cost_estimate=pl.CostEstimate(flops=2 * COLS * ROWS * D, bytes_accessed=6 * 1024 * 1024, transcendentals=0),
     )(place, ot, cotangent)
 
@@ -305,7 +391,7 @@
         in_specs=[whole] * len(arrays),
         out_specs=[whole] * len(sizes),
         out_shape=outs,
-        compiler_params=params(),
+        compiler_params=params(16),
         cost_estimate=pl.CostEstimate(flops=count * len(arrays), bytes_accessed=2 * count * (len(arrays) + 1), transcendentals=0),
     )(*arrays)
 
@@ -327,7 +413,7 @@
         in_specs=[pl.BlockSpec(memory_space=pltpu.SMEM)] + [whole] * 4,
         out_specs=[whole] * 4,
         out_shape=[out] * 4,
-        compiler_params=params(),
+        compiler_params=params(16),
         cost_estimate=pl.CostEstimate(flops=16 * rows * D, bytes_accessed=40 * rows * D, transcendentals=0),
     )(place, *arrays)
 
@@ -367,7 +453,7 @@
         out_specs=[head, head],
         out_shape=[shape, shape],
         input_output_aliases=aliases,
-        compiler_params=params(),
+        compiler_params=params(16),
         cost_estimate=pl.CostEstimate(flops=4 * ROWS * 256 * COLS, bytes_accessed=14 * ROWS * COLS, transcendentals=0),
     )(*args)
 
@@ -382,47 +468,37 @@
     y, z_hi = jnp.right_shift(other, 1), jnp.bitwise_and(other, 1)
     place = jnp.stack([core, y, x]).astype(jnp.int32)
 
-    pooled = []
-    for group in range(GROUPS):
-        outs = pool(key, value, segment_ids, group)
-        if group == 0:
-            fq, fk = outs[3:]
-        pooled.append(outs[:3])
-    pieces = []
-    for one, two, three in pooled:
-        from_z = swap(one, "ctx", 2)
-        from_x = jnp.concatenate([swap(two, "ctx", 4), swap(three, "ctx", 12), swap(three, "ctx", 8)], 0)
-        from_xz = swap(from_x, "ctx", 2)
-        mine = [from_z, from_x, from_xz]
-        pieces.append(mine + [swap(member, "ctx", 1) for member in mine])
+    one, two, three, fq, fk = pool(key, value, segment_ids, 0)
+    from_z = swap(one, "ctx", 2)
+    from_x = stack([swap(two, "ctx", 4), swap(three, "ctx", 12), swap(three, "ctx", 8)])
+    from_xz = swap(from_x, "ctx", 2)
+    mine = [from_z, from_x, from_xz]
+    pieces = mine + [swap(member, "ctx", 1) for member in mine]
     grad_attention = lax.dot_general(
         cotangent, out_weight, (((1,), (1,)), ((), ())), preferred_element_type=F32
     ).astype(BF16)
 
-    earlier, ended, ends = (), (), []
-    for group in range(GROUPS):
-        o, ot, dq, dk, dv, keep, give = attention(
-            query, key, value, grad_attention, fq, fk, pieces[group], pieces[0], earlier, group
-        )
-        earlier = (o, dq)
-        own_one, own_two, own_xz = split_sum([keep, swap(give, "ctx", 1)], 1, (128, 128, 128))
-        back_xz = swap(own_xz, "ctx", 2)
-        back_z = swap(own_one, "ctx", 2)
-        two, three, four = split_sum([own_two, back_xz], 1, (64, 32, 32))
-        returned = [back_z, swap(two, "ctx", 4), swap(three, "ctx", 12), swap(four, "ctx", 8)]
-        ended = finish(dk, dv, returned, ended, group)
-
-        kept, given = grad_weight_part(place, ot, cotangent)
-        quarter = COLS // 8
-        parts = split_sum([kept, swap(given, "ctx", 1)], 0, (quarter,) * 4)
-        parts = [parts[0]] + [shift(parts[step], "dp", 2 * step) for step in (1, 2, 3)]
-        parts = turn_sum(place, parts)
-        parts = [parts[0]] + [shift(parts[step], "ctx", 4 * step) for step in (1, 2, 3)]
-        total = parts[0].astype(F32)
-        for member in parts[1:]:
-            total = total + member.astype(F32)
-        ends.append(total)
-    ends = jnp.concatenate(ends, 0).reshape(2, 16, D)
+    weights, attention, attention_t, delta = forward(query, key, value, grad_attention, fq, fk, pieces)
+    kept, given = grad_weight_part(place, attention_t, cotangent)
+    keep, give, partial_q = coarse_backward(query, grad_attention, delta, weights, pieces, given)
+    quarter = COLS // 8
+    parts = split_sum([kept, swap(given, "ctx", 1)], 0, (quarter,) * 4)
+    own_one, own_two, own_xz = split_sum([keep, swap(give, "ctx", 1)], 1, (128, 128, 128))
+    back_xz = swap(own_xz, "ctx", 2)
+    back_z = swap(own_one, "ctx", 2)
+    grad_query, dk, dv = local_backward(query, key, value, grad_attention, delta, weights, partial_q, own_one)
+    output = project(attention, out_weight, grad_query)
+    two, three, four = split_sum([own_two, back_xz], 1, (64, 32, 32))
+    returned = [back_z, swap(two, "ctx", 4), swap(three, "ctx", 12), swap(four, "ctx", 8)]
+    grad_key, grad_value = finish(dk, dv, returned, (), 0)
+
+    parts = [parts[0]] + [shift(parts[step], "dp", 2 * step) for step in (1, 2, 3)]
+    parts = turn_sum(place, parts)
+    parts = [parts[0]] + [shift(parts[step], "ctx", 4 * step) for step in (1, 2, 3)]
+    ends = parts[0].astype(F32)
+    for member in parts[1:]:
+        ends = ends + member.astype(F32)
+    ends = ends.reshape(2, 16, D)
     kept = lax.dynamic_index_in_dim(ends, z_lo, 0, keepdims=False)
     given = lax.dynamic_index_in_dim(ends, 1 - z_lo, 0, keepdims=False)
     ends = (kept + swap(given.astype(BF16), "ctx", 2).astype(F32)).reshape(2, 8, D)
@@ -430,8 +506,7 @@
     given = lax.dynamic_index_in_dim(ends, 1 - z_hi, 0, keepdims=False)
     grad_weight = kept + swap(given, "dp", 1)
 
-    output = lax.dot_general(o, out_weight, (((1,), (0,)), ((), ())), preferred_element_type=F32).astype(BF16)
-    return output[None], dq[None], ended[0][None], ended[1][None], grad_weight
+    return output[None], grad_query[None], grad_key[None], grad_value[None], grad_weight
 
 
 def solution(mesh):

time: 166 us -> 158 us (0.952)
  starting transfers between devices: 50.7 us -> 31.9 us
  waiting for transfers between devices: 30.2 us -> 44.5 us
  matrix products: 9.72 us -> 5.18 us
  Pallas kernels: 52.5 us -> 56.1 us
    ppermute x32 -> x17, starting transfers between devices: 32.7 us -> 20.8 us  [swap(): lax.ppermute(array, axis, [(i, i ^ bits) for i in range(lax.axis_size(axi...]
    ppermute x12 -> x6, waiting for transfers between devices: 11.5 us -> 21.8 us  [shift(): lax.ppermute(array, axis, [(i, (i + step) % size) for i in range(size)])]
    pallas_call x2 -> x5, Pallas kernels: 33.6 us -> 40.9 us  [the longest x1 15.4 us: forward(): pl.pallas_call(forward_kernel, grid=(HEADS,), in_specs=[HEAD] * 4 + [FIXE...]
    ppermute x12 -> x6, starting transfers between devices: 17.9 us -> 11.1 us  [shift(): lax.ppermute(array, axis, [(i, (i + step) % size) for i in range(size)])]
    dot_general x1 -> x0, matrix products: 6.31 us -> none  [body(): lax.dot_general(o, out_weight, (((1,), (0,)), ((), ())), preferred_elemen...]
    ppermute x32 -> x17, waiting for transfers between devices: 18.8 us -> 22.7 us  [swap(): lax.ppermute(array, axis, [(i, i ^ bits) for i in range(lax.axis_size(axi...]
    dot_general x1, matrix products: 3.41 us -> 5.18 us  [body(): lax.dot_general(cotangent, out_weight, (((1,), (1,)), ((), ())), preferre...]
    pallas_call x2 -> x1, Pallas kernels: 5.42 us -> 3.97 us  [grad_weight_part(): pl.pallas_call(grad_weight_kernel, grid_spec=pltpu.PrefetchScalarGridSpec...]
  transfers between devices with their start and end apart: 44 -> 23, of which waited for: 10 -> 7; matrix products, arithmetic and copies ran while one was open for 7% -> 4% of each run, Pallas kernels for 31% -> 22%
where the time goes in v2:
time: 158 us; the launch traced here: 157 us
  Pallas kernels  56.1 us (36%)
  waiting for transfers between devices  44.5 us (28%)
  starting transfers between devices  31.9 us (20%)
  local copies, waits for them, and re-layouts  16.9 us (11%)
  matrix products  5.18 us (3%)
  other arithmetic  1.83 us (1%)
    ppermute x17, waiting for transfers between devices, swap(): lax.ppermute(array, axis, [(i, i ^ bits) for i in range(lax.axis_size(axi...  22.7 us
    ppermute x6, waiting for transfers between devices, shift(): lax.ppermute(array, axis, [(i, (i + step) % size) for i in range(size)])  21.8 us
    ppermute x17, starting transfers between devices, swap(): lax.ppermute(array, axis, [(i, i ^ bits) for i in range(lax.axis_size(axi...  20.8 us
    unnamed x44, local copies, waits for them, and re-layouts  16.8 us
    pallas_call x1, Pallas kernels, forward(): pl.pallas_call(forward_kernel, grid=(HEADS,), in_specs=[HEAD] * 4 + [FIXE...  15.4 us
    pallas_call x1, Pallas kernels, coarse_backward(): pl.pallas_call(coarse_kernel, grid=(HEADS,), in_specs=[HEAD] * 2 + [DELTA...  12.1 us
    ppermute x6, starting transfers between devices, shift(): lax.ppermute(array, axis, [(i, (i + step) % size) for i in range(size)])  11.1 us
    pallas_call x1, Pallas kernels, local_backward(): pl.pallas_call(local_kernel, grid=(HEADS,), in_specs=[HEAD] * 4 + [DELTA,...  9.37 us
  transfers between devices with their start and end apart: 23, of which 7 were waited for; matrix products, arithmetic and copies ran while one was open for 4% of the time, Pallas kernels for 22%

profile of v2, /device:TPU:0, one launch (start us, length us, event | category | flops | bytes accessed | tf_op | source)
XLA Modules:
  0.0 157.2 jit_solution(11311240551168091362)
XLA Ops:
  0.6 0.0 copy-start.2
  0.6 1.2 copy-done.2
  1.9 1.2 copy-done.4
  3.1 0.7 copy-done.18
  3.8 2.3 %shard_map.101 = (bf16[128,2176]{1,0:T(8,128)(2,1)}, bf16[64,2176]{1,0:T(8,128)(2,1)S(1)}, bf16[32,2176]{1,0:T(8,128)(2,1)S(1)}, bf16[512,128]{1,0:T(8,128)(2,1)S(1)}, bf16[512,128]{1,0:T(8,128)(2,1)S(1)}) custom-call(s32[1,512]{1,0:T(1,128)S(1)} %copy-done.18, bf16[512,1024]{1,0:T(8,128)(2,1)S(1)} %bitcast.27, bf16[512,1024]{1,0:T(8,128)(2,1)S(1)} %bitcast.28, ...), custom_call_target="tpu_custom_call" | custom-call | flops 469762048 | bytes 3145728 | tf_op jit(solution)/shard_map/pallas_call | solution.py:122
  6.1 1.6 %collective-permute-start.1 = (bf16[64,2176]{1,0:T(8,128)(2,1)S(1)}, bf16[64,2176]{1,0:T(8,128)(2,1)S(1)}, u32[]{:S(2)}, u32[]{:S(2)}) collective-permute-start(bf16[64,2176]{1,0:T(8,128)(2,1)S(1)} %get-tuple-element.41), channel_id=1, source_target_pairs={{0,32},{8,40},{16,48},{24,56},{32,0},{40,8},{48,16},{56,24},{64,96... | collective-permute-start | bytes 835592 | tf_op jit(solution)/shard_map/ppermute | solution.py:33
  7.6 2.1 %collective-permute-start.2 = (bf16[32,2176]{1,0:T(8,128)(2,1)S(1)}, bf16[32,2176]{1,0:T(8,128)(2,1)S(1)}, u32[]{:S(2)}, u32[]{:S(2)}) collective-permute-start(bf16[32,2176]{1,0:T(8,128)(2,1)S(1)} %get-tuple-element.42), channel_id=1, source_target_pairs={{0,96},{8,104},{16,112},{24,120},{32,64},{40,72},{48,80},{56,88},{... | collective-permute-start | bytes 417800 | tf_op jit(solution)/shard_map/ppermute | solution.py:33
  9.7 0.6 collective-permute-start.3
  10.4 1.9 %collective-permute-start = (bf16[128,2176]{1,0:T(8,128)(2,1)}, bf16[128,2176]{1,0:T(8,128)(2,1)S(1)}, u32[]{:S(2)}, u32[]{:S(2)}) collective-permute-start(bf16[128,2176]{1,0:T(8,128)(2,1)} %get-tuple-element.40), channel_id=1, source_target_pairs={{0,16},{8,24},{16,0},{24,8},{32,48},{40,56},{48,32},{56,40},{64,80... | collective-permute-start | bytes 1671176 | tf_op jit(solution)/shard_map/ppermute | solution.py:33
  12.3 1.7 %collective-permute-done.2.refs_1_ = bf16[32,2176]{1,0:T(8,128)(2,1)S(1)} collective-permute-done((bf16[32,2176]{1,0:T(8,128)(2,1)S(1)}, bf16[32,2176]{1,0:T(8,128)(2,1)S(1)}, u32[]{:S(2)}, u32[]{:S(2)}) %collective-permute-start.2) | collective-permute-done | bytes 139296 | tf_op jit(solution)/shard_map/ppermute | solution.py:33
  14.0 5.7 %collective-permute-done.3.refs_2_ = bf16[32,2176]{1,0:T(8,128)(2,1)S(1)} collective-permute-done((bf16[32,2176]{1,0:T(8,128)(2,1)S(1)}, bf16[32,2176]{1,0:T(8,128)(2,1)S(1)}, u32[]{:S(2)}, u32[]{:S(2)}) %collective-permute-start.3) | collective-permute-done | bytes 139296 | tf_op jit(solution)/shard_map/ppermute | solution.py:33
  19.7 0.0 collective-permute-done.1.refs_0_
  19.8 2.0 %collective-permute-start.4 = (bf16[128,2176]{1,0:T(8,128)(2,1)S(1)}, bf16[128,2176]{1,0:T(8,128)(2,1)}, u32[]{:S(2)}, u32[]{:S(2)}) collective-permute-start(bf16[128,2176]{1,0:T(8,128)(2,1)S(1)} %shard_map.102.refs_7_.refs_13_.refs_19_), channel_id=1, source_target_pairs={{0,16},{8,24},{16,0},{24,8},{32,48},{40,56},{48,32},{56,40},{64,80... | collective-permute-start | bytes 1671176 | tf_op jit(solution)/shard_map/ppermute | solution.py:33
  21.8 0.1 pad_add_fusion.place_ref
  21.9 0.1 collective-permute-start.6
  22.0 4.2 %collective-permute-done.refs_6_.refs_12_.refs_18_ = bf16[128,2176]{1,0:T(8,128)(2,1)S(1)} collective-permute-done((bf16[128,2176]{1,0:T(8,128)(2,1)}, bf16[128,2176]{1,0:T(8,128)(2,1)S(1)}, u32[]{:S(2)}, u32[]{:S(2)}) %collective-permute-start) | collective-permute-done | bytes 557088 | tf_op jit(solution)/shard_map/ppermute | solution.py:33
  26.2 10.5 %collective-permute-done.4.refs_8_.refs_14_.refs_20_ = bf16[128,2176]{1,0:T(8,128)(2,1)} collective-permute-done((bf16[128,2176]{1,0:T(8,128)(2,1)S(1)}, bf16[128,2176]{1,0:T(8,128)(2,1)}, u32[]{:S(2)}, u32[]{:S(2)}) %collective-permute-start.4) | collective-permute-done | bytes 557088 | tf_op jit(solution)/shard_map/ppermute | solution.py:33
  36.6 0.0 collective-permute-start.7
  36.6 5.2 %convolution_convert_fusion.refs_3_.refs_1_.g_ref = bf16[512,1024]{1,0:T(8,128)(2,1)S(1)} fusion(bf16[1024,2048]{1,0:T(8,128)(2,1)} %w_ref.1, bf16[1,512,2048]{2,1,0:T(8,128)(2,1)} %param.11), kind=kOutput, calls=%fused_computation | convolution fusion | flops 2148007936 | bytes 7340032 | tf_op jit(solution)/shard_map/dot_general | solution.py:477
  41.8 0.0 copy-start.9
  41.8 0.0 collective-permute-done.6.refs_10_.refs_16_.refs_22_
  41.8 0.0 collective-permute-done.7.refs_11_.refs_17_.refs_23_
  41.9 0.0 copy-start.19
  41.9 15.4 %shard_map.103 = (bf16[8,1280,512]{2,1,0:T(8,128)(2,1)S(1)}, bf16[512,1024]{1,0:T(8,128)(2,1)S(1)}, bf16[1024,512]{1,0:T(8,128)(2,1)S(1)}, f32[8,8,512]{2,1,0:T(8,128)S(1)}) custom-call(bf16[512,1024]{1,0:T(8,128)(2,1)S(1)} %bitcast.47, bf16[512,1024]{1,0:T(8,128)(2,1)S(1)} %bitcast.35, bf16[512,1024]{1,0:T(8,128)(2,1)S(1)} %bitcast.45, ...), custom_call_target="tpu_custom_call" | custom-call | flops 10737418240 | bytes 20971520 | tf_op jit(solution)/shard_map/pallas_call | solution.py:189
  57.3 0.0 copy-start.15
  57.3 4.0 %shard_map.104 = (bf16[512,2048]{1,0:T(8,128)(2,1)S(1)}, bf16[512,2048]{1,0:T(8,128)(2,1)S(1)}) custom-call(s32[3]{0:T(128)S(1)} %pad_add_fusion.place_ref, bf16[1024,512]{1,0:T(8,128)(2,1)S(1)} %get-tuple-element.46.ot_ref, bf16[512,2048]{1,0:T(8,128)(2,1)S(1)} %bitcast.51), custom_call_target="tpu_custom_call" | custom-call | flops 2147483648 | bytes 6291456 | tf_op jit(solution)/shard_map/pallas_call | solution.py:354
  61.3 0.6 collective-permute-start.14
  61.9 12.1 %shard_map.105 = (bf16[2,384,1024]{2,1,0:T(8,128)(2,1)S(1)}, bf16[2,384,1024]{2,1,0:T(8,128)(2,1)}, f32[1024,512]{1,0:T(8,128)S(1)}) custom-call(bf16[512,1024]{1,0:T(8,128)(2,1)S(1)} %bitcast.48, bf16[512,1024]{1,0:T(8,128)(2,1)S(1)} %convolution_convert_fusion.refs_3_.refs_1_.g_ref, f32[8,8,512]{2,1,0:T(8,128)S(1)} %get-tuple-element.44.refs_2_.delta_ref, ...), custom_call_target="tpu_custom_call" | custom-call | flops 6442450944 | bytes 16777216 | tf_op jit(solution)/shard_map/pallas_call | solution.py:241
  74.0 4.0 %copy-done = bf16[8,1280,512]{2,1,0:T(8,128)(2,1)} copy-done((bf16[8,1280,512]{2,1,0:T(8,128)(2,1)}, bf16[8,1280,512]{2,1,0:T(8,128)(2,1)S(1)}, u32[]{:S(2)}) %copy-start) | copy-done | bytes 10485784
  78.0 0.1 collective-permute-start.8
  78.1 0.0 collective-permute-done.14.refs_1_
  78.1 0.5 shard_map.111
  78.6 0.8 copy-done.11
  79.3 0.6 copy-done.13
  79.9 1.6 %collective-permute-start.15 = (bf16[128,2048]{1,0:T(8,128)(2,1)S(1)}, bf16[128,2048]{1,0:T(8,128)(2,1)S(1)}, u32[]{:S(2)}, u32[]{:S(2)}) collective-permute-start(bf16[128,2048]{1,0:T(8,128)(2,1)S(1)} %get-tuple-element.64), channel_id=1, source_target_pairs={{0,2},{1,3},{2,4},{3,5},{4,6},{5,7},{6,0},{7,1},{8,10},{9,11},{10,... | collective-permute-start | bytes 1572872 | tf_op jit(solution)/shard_map/ppermute | solution.py:38
  81.5 2.9 %collective-permute-start.16 = (bf16[128,2048]{1,0:T(8,128)(2,1)S(1)}, bf16[128,2048]{1,0:T(8,128)(2,1)S(1)}, u32[]{:S(2)}, u32[]{:S(2)}) collective-permute-start(bf16[128,2048]{1,0:T(8,128)(2,1)S(1)} %get-tuple-element.65), channel_id=1, source_target_pairs={{0,4},{1,5},{2,6},{3,7},{4,0},{5,1},{6,2},{7,3},{8,12},{9,13},{10,... | collective-permute-start | bytes 1572872 | tf_op jit(solution)/shard_map/ppermute | solution.py:38
  84.4 1.3 collective-permute-start.17
  85.7 9.3 %collective-permute-done.15.b_ref = bf16[128,2048]{1,0:T(8,128)(2,1)S(1)} collective-permute-done((bf16[128,2048]{1,0:T(8,128)(2,1)S(1)}, bf16[128,2048]{1,0:T(8,128)(2,1)S(1)}, u32[]{:S(2)}, u32[]{:S(2)}) %collective-permute-start.15) | collective-permute-done | bytes 524320 | tf_op jit(solution)/shard_map/ppermute | solution.py:38
  95.0 12.4 %collective-permute-done.16.c_ref = bf16[128,2048]{1,0:T(8,128)(2,1)S(1)} collective-permute-done((bf16[128,2048]{1,0:T(8,128)(2,1)S(1)}, bf16[128,2048]{1,0:T(8,128)(2,1)S(1)}, u32[]{:S(2)}, u32[]{:S(2)}) %collective-permute-start.16) | collective-permute-done | bytes 524320 | tf_op jit(solution)/shard_map/ppermute | solution.py:38
  107.5 0.0 collective-permute-done.17.d_ref
  107.5 1.4 shard_map.112
  108.8 1.1 collective-permute-start.18
  109.9 2.7 %collective-permute-start.19 = (bf16[32,2048]{1,0:T(8,128)(2,1)}, bf16[32,2048]{1,0:T(8,128)(2,1)}, u32[]{:S(2)}, u32[]{:S(2)}) collective-permute-start(bf16[32,2048]{1,0:T(8,128)(2,1)} %get-tuple-element.69), channel_id=1, source_target_pairs={{0,64},{8,72},{16,80},{24,88},{32,96},{40,104},{48,112},{56,120},{... | collective-permute-start | bytes 393224 | tf_op jit(solution)/shard_map/ppermute | solution.py:38
  112.7 1.4 collective-permute-start.20
  114.1 0.0 collective-permute-done.8.refs_1_
  114.1 1.5 copy-done.14
  115.6 1.8 %shard_map.106 = (bf16[2,128,1024]{2,1,0:T(8,128)(2,1)S(1)}, bf16[2,128,1024]{2,1,0:T(8,128)(2,1)S(1)}, bf16[2,128,1024]{2,1,0:T(8,128)(2,1)S(1)}) custom-call(bf16[2,384,1024]{2,1,0:T(8,128)(2,1)S(1)} %copy-done.14, bf16[2,384,1024]{2,1,0:T(8,128)(2,1)} %collective-permute-done.8.refs_1_), custom_call_target="tpu_custom_call" | custom-call | flops 1572864 | bytes 4718592 | tf_op jit(solution)/shard_map/pallas_call | solution.py:389
  117.4 1.8 %collective-permute-start.10 = (bf16[2,128,1024]{2,1,0:T(8,128)(2,1)S(1)}, bf16[2,128,1024]{2,1,0:T(8,128)(2,1)S(1)}, u32[]{:S(2)}, u32[]{:S(2)}) collective-permute-start(bf16[2,128,1024]{2,1,0:T(8,128)(2,1)S(1)} %get-tuple-element.56), channel_id=1, source_target_pairs={{0,16},{8,24},{16,0},{24,8},{32,48},{40,56},{48,32},{56,40},{64,80... | collective-permute-start | bytes 1572872 | tf_op jit(solution)/shard_map/ppermute | solution.py:33
  119.2 0.3 collective-permute-start.9
  119.5 1.1 convert_add_fusion
  120.6 1.8 %collective-permute-start.21 = (bf16[16,2048]{1,0:T(8,128)(2,1)S(1)}, bf16[16,2048]{1,0:T(8,128)(2,1)S(1)}, u32[]{:S(2)}, u32[]{:S(2)}) collective-permute-start(bf16[16,2048]{1,0:T(8,128)(2,1)S(1)} %fusion.1), channel_id=1, source_target_pairs={{0,16},{8,24},{16,0},{24,8},{32,48},{40,56},{48,32},{56,40},{64,80... | collective-permute-start | bytes 196616 | tf_op jit(solution)/shard_map/ppermute | solution.py:33
  122.4 4.0 %copy-done.1 = bf16[8,1280,512]{2,1,0:T(8,128)(2,1)S(1)} copy-done((bf16[8,1280,512]{2,1,0:T(8,128)(2,1)S(1)}, bf16[8,1280,512]{2,1,0:T(8,128)(2,1)}, u32[]{:S(2)}) %copy-start.1) | copy-done | bytes 10485784
  126.4 1.6 %copy-done.12 = f32[1024,512]{1,0:T(8,128)S(1)} copy-done((f32[1024,512]{1,0:T(8,128)S(1)}, f32[1024,512]{1,0:T(8,128)}, u32[]{:S(2)}) %copy-start.12) | copy-done | bytes 2097176
  128.0 9.4 %shard_map.107 = (bf16[512,1024]{1,0:T(8,128)(2,1)}, f32[512,1024]{1,0:T(8,128)S(1)}, f32[512,1024]{1,0:T(8,128)S(1)}) custom-call(bf16[512,1024]{1,0:T(8,128)(2,1)S(1)} %bitcast.49, bf16[512,1024]{1,0:T(8,128)(2,1)S(1)} %bitcast.36, bf16[512,1024]{1,0:T(8,128)(2,1)S(1)} %bitcast.46, bf16[512,1024]{1,0:T(8,128)(2,1)S(1)} %copy-done.10, ...), custom_call_target="tpu_custom_call" | custom-call | flops 4294967296 | bytes 16777216 | tf_op jit(solution)/shard_map/pallas_call | solution.py:273
  137.4 0.1 shard_map.109
  137.5 0.7 collective-permute-start.11
  138.2 1.5 collective-permute-start.12
  139.7 2.0 %collective-permute-start.13 = (bf16[2,32,1024]{2,1,0:T(8,128)(2,1)S(1)}, bf16[2,32,1024]{2,1,0:T(8,128)(2,1)S(1)}, u32[]{:S(2)}, u32[]{:S(2)}) collective-permute-start(bf16[2,32,1024]{2,1,0:T(8,128)(2,1)S(1)} %get-tuple-element.59), channel_id=1, source_target_pairs={{0,64},{8,72},{16,80},{24,88},{32,96},{40,104},{48,112},{56,120},{... | collective-permute-start | bytes 393224 | tf_op jit(solution)/shard_map/ppermute | solution.py:33
  141.7 0.6 collective-permute-done.21
  142.3 3.8 %collective-permute-start.22 = (f32[8,2048]{1,0:T(8,128)S(1)}, f32[8,2048]{1,0:T(8,128)S(1)}, u32[]{:S(2)}, u32[]{:S(2)}) collective-permute-start(f32[8,2048]{1,0:T(8,128)S(1)} %dynamic-slice_bitcast_fusion), channel_id=1, source_target_pairs={{0,1},{1,0},{2,3},{3,2},{4,5},{5,4},{6,7},{7,6},{8,9},{9,8},{10,11... | collective-permute-start | bytes 196616 | tf_op jit(solution)/shard_map/ppermute | solution.py:33
  146.1 1.2 copy-done.17
  147.3 4.0 %shard_map.108 = bf16[512,2048]{1,0:T(8,128)(2,1)} custom-call(bf16[512,1024]{1,0:T(8,128)(2,1)S(1)} %copy-done.16, bf16[1024,2048]{1,0:T(8,128)(2,1)S(1)} %copy-done.6, bf16[512,1024]{1,0:T(8,128)(2,1)S(1)} %copy-done.17), custom_call_target="tpu_custom_call" | custom-call | flops 2147483648 | bytes 7340032 | tf_op jit(solution)/shard_map/pallas_call | solution.py:297
  151.4 5.2 %shard_map.110 = (bf16[512,1024]{1,0:T(8,128)(2,1)}, bf16[512,1024]{1,0:T(8,128)(2,1)}) custom-call(f32[512,1024]{1,0:T(8,128)S(1)} %get-tuple-element.53.refs_0_, f32[512,1024]{1,0:T(8,128)S(1)} %get-tuple-element.54.refs_1_, bf16[2,128,1024]{2,1,0:T(8,128)(2,1)S(1)} %collective-permute-done.9.refs_2_, ...), custom_call_target="tpu_custom_call" | custom-call | flops 536870912 | bytes 7340032 | tf_op jit(solution)/shard_map/pallas_call | solution.py:449
  156.5 0.6 bitcast_add_fusion.1
  (45 shorter events, 0.2 us)
Async XLA Ops:
  0.6 1.2 copy-start.2
  1.9 1.2 copy-start.4
  3.1 0.7 copy-start.18
  6.1 13.7 %copy-start.20 = (bf16[512,128]{1,0:T(8,128)(2,1)}, bf16[512,128]{1,0:T(8,128)(2,1)S(1)}, u32[]{:S(2)}) copy-start(bf16[512,128]{1,0:T(8,128)(2,1)S(1)} %get-tuple-element.39.refs_5_) | copy-start | bytes 393220
  6.1 13.7 %collective-permute-start.1 = (bf16[64,2176]{1,0:T(8,128)(2,1)S(1)}, bf16[64,2176]{1,0:T(8,128)(2,1)S(1)}, u32[]{:S(2)}, u32[]{:S(2)}) collective-permute-start(bf16[64,2176]{1,0:T(8,128)(2,1)S(1)} %get-tuple-element.41), channel_id=1, source_target_pairs={{0,32},{8,40},{16,48},{24,56},{32,0},{40,8},{48,16},{56,24},{64,96... | collective-permute-start | bytes 835592 | tf_op jit(solution)/shard_map/ppermute | solution.py:33
  7.6 6.3 %collective-permute-start.2 = (bf16[32,2176]{1,0:T(8,128)(2,1)S(1)}, bf16[32,2176]{1,0:T(8,128)(2,1)S(1)}, u32[]{:S(2)}, u32[]{:S(2)}) collective-permute-start(bf16[32,2176]{1,0:T(8,128)(2,1)S(1)} %get-tuple-element.42), channel_id=1, source_target_pairs={{0,96},{8,104},{16,112},{24,120},{32,64},{40,72},{48,80},{56,88},{... | collective-permute-start | bytes 417800 | tf_op jit(solution)/shard_map/ppermute | solution.py:33
  9.7 10.0 %collective-permute-start.3 = (bf16[32,2176]{1,0:T(8,128)(2,1)S(1)}, bf16[32,2176]{1,0:T(8,128)(2,1)S(1)}, u32[]{:S(2)}, u32[]{:S(2)}) collective-permute-start(bf16[32,2176]{1,0:T(8,128)(2,1)S(1)} %get-tuple-element.42), channel_id=1, source_target_pairs={{0,64},{8,72},{16,80},{24,88},{32,96},{40,104},{48,112},{56,120},{... | collective-permute-start | bytes 417800 | tf_op jit(solution)/shard_map/ppermute | solution.py:33
  10.4 15.8 %collective-permute-start = (bf16[128,2176]{1,0:T(8,128)(2,1)}, bf16[128,2176]{1,0:T(8,128)(2,1)S(1)}, u32[]{:S(2)}, u32[]{:S(2)}) collective-permute-start(bf16[128,2176]{1,0:T(8,128)(2,1)} %get-tuple-element.40), channel_id=1, source_target_pairs={{0,16},{8,24},{16,0},{24,8},{32,48},{40,56},{48,32},{56,40},{64,80... | collective-permute-start | bytes 1671176 | tf_op jit(solution)/shard_map/ppermute | solution.py:33
  19.8 16.8 %collective-permute-start.4 = (bf16[128,2176]{1,0:T(8,128)(2,1)S(1)}, bf16[128,2176]{1,0:T(8,128)(2,1)}, u32[]{:S(2)}, u32[]{:S(2)}) collective-permute-start(bf16[128,2176]{1,0:T(8,128)(2,1)S(1)} %shard_map.102.refs_7_.refs_13_.refs_19_), channel_id=1, source_target_pairs={{0,16},{8,24},{16,0},{24,8},{32,48},{40,56},{48,32},{56,40},{64,80... | collective-permute-start | bytes 1671176 | tf_op jit(solution)/shard_map/ppermute | solution.py:33
  21.9 20.0 %copy-start.3 = (bf16[1,512,1024]{2,1,0:T(8,128)(2,1)S(1)}, bf16[1,512,1024]{2,1,0:T(8,128)(2,1)}, u32[]{:S(2)}) copy-start(bf16[1,512,1024]{2,1,0:T(8,128)(2,1)} %param.7) | copy-start | bytes 3145732
  21.9 20.0 %copy-start.5 = (bf16[1,512,1024]{2,1,0:T(8,128)(2,1)S(1)}, bf16[1,512,1024]{2,1,0:T(8,128)(2,1)}, u32[]{:S(2)}) copy-start(bf16[1,512,1024]{2,1,0:T(8,128)(2,1)} %param.8) | copy-start | bytes 3145732
  21.9 20.0 %copy-start.7 = (bf16[1,512,1024]{2,1,0:T(8,128)(2,1)S(1)}, bf16[1,512,1024]{2,1,0:T(8,128)(2,1)}, u32[]{:S(2)}) copy-start(bf16[1,512,1024]{2,1,0:T(8,128)(2,1)} %param.6) | copy-start | bytes 3145732
  21.9 20.0 %copy-start.21 = (bf16[512,128]{1,0:T(8,128)(2,1)S(1)}, bf16[512,128]{1,0:T(8,128)(2,1)}, u32[]{:S(2)}) copy-start(bf16[512,128]{1,0:T(8,128)(2,1)} %copy-done.20) | copy-start | bytes 393220
  21.9 19.9 %collective-permute-start.6 = (bf16[128,2176]{1,0:T(8,128)(2,1)S(1)}, bf16[128,2176]{1,0:T(8,128)(2,1)S(1)}, u32[]{:S(2)}, u32[]{:S(2)}) collective-permute-start(bf16[128,2176]{1,0:T(8,128)(2,1)S(1)} %shard_map.102.refs_7_.refs_13_.refs_19_), channel_id=1, source_target_pairs={{0,8},{8,0},{16,24},{24,16},{32,40},{40,32},{48,56},{56,48},{64,72... | collective-permute-start | bytes 1671176 | tf_op jit(solution)/shard_map/ppermute | solution.py:33
  26.2 15.7 %collective-permute-start.5 = (bf16[128,2176]{1,0:T(8,128)(2,1)S(1)}, bf16[128,2176]{1,0:T(8,128)(2,1)S(1)}, u32[]{:S(2)}, u32[]{:S(2)}) collective-permute-start(bf16[128,2176]{1,0:T(8,128)(2,1)S(1)} %collective-permute-done.refs_6_.refs_12_.refs_18_), channel_id=1, source_target_pairs={{0,8},{8,0},{16,24},{24,16},{32,40},{40,32},{48,56},{56,48},{64,72... | collective-permute-start | bytes 1671176 | tf_op jit(solution)/shard_map/ppermute | solution.py:33
  36.6 5.2 %collective-permute-start.7 = (bf16[128,2176]{1,0:T(8,128)(2,1)}, bf16[128,2176]{1,0:T(8,128)(2,1)S(1)}, u32[]{:S(2)}, u32[]{:S(2)}) collective-permute-start(bf16[128,2176]{1,0:T(8,128)(2,1)} %collective-permute-done.4.refs_8_.refs_14_.refs_20_), channel_id=1, source_target_pairs={{0,8},{8,0},{16,24},{24,16},{32,40},{40,32},{48,56},{56,48},{64,72... | collective-permute-start | bytes 1671176 | tf_op jit(solution)/shard_map/ppermute | solution.py:33
  41.8 20.1 %copy-start.9 = (bf16[512,1024]{1,0:T(8,128)(2,1)}, bf16[512,1024]{1,0:T(8,128)(2,1)S(1)}, u32[]{:S(2)}) copy-start(bf16[512,1024]{1,0:T(8,128)(2,1)S(1)} %convolution_convert_fusion.refs_3_.refs_1_.g_ref) | copy-start | bytes 3145732
  41.9 15.4 %copy-start.19 = (bf16[1,512,2048]{2,1,0:T(8,128)(2,1)S(1)}, bf16[1,512,2048]{2,1,0:T(8,128)(2,1)}, u32[]{:S(2)}) copy-start(bf16[1,512,2048]{2,1,0:T(8,128)(2,1)} %param.11) | copy-start | bytes 6291460
  57.3 4.0 %copy-start.15 = (bf16[512,1024]{1,0:T(8,128)(2,1)}, bf16[512,1024]{1,0:T(8,128)(2,1)S(1)}, u32[]{:S(2)}) copy-start(bf16[512,1024]{1,0:T(8,128)(2,1)S(1)} %get-tuple-element.43.a_ref) | copy-start | bytes 3145732
  61.3 16.8 %collective-permute-start.14 = (bf16[512,2048]{1,0:T(8,128)(2,1)S(1)}, bf16[512,2048]{1,0:T(8,128)(2,1)S(1)}, u32[]{:S(2)}, u32[]{:S(2)}) collective-permute-start(bf16[512,2048]{1,0:T(8,128)(2,1)S(1)} %get-tuple-element.47.refs_18_), channel_id=1, source_target_pairs={{0,8},{8,0},{16,24},{24,16},{32,40},{40,32},{48,56},{56,48},{64,72... | collective-permute-start | bytes 6291464 | tf_op jit(solution)/shard_map/ppermute | solution.py:33
  74.0 4.0 %copy-start = (bf16[8,1280,512]{2,1,0:T(8,128)(2,1)}, bf16[8,1280,512]{2,1,0:T(8,128)(2,1)S(1)}, u32[]{:S(2)}) copy-start(bf16[8,1280,512]{2,1,0:T(8,128)(2,1)S(1)} %get-tuple-element.45.refs_3_.refs_4_.refs_5_.p_ref) | copy-start | bytes 31457284
  78.0 1.3 copy-start.11
  78.0 1.9 %copy-start.13 = (bf16[2,384,1024]{2,1,0:T(8,128)(2,1)}, bf16[2,384,1024]{2,1,0:T(8,128)(2,1)S(1)}, u32[]{:S(2)}) copy-start(bf16[2,384,1024]{2,1,0:T(8,128)(2,1)S(1)} %get-tuple-element.49.refs_0_) | copy-start | bytes 4718596
  78.0 36.1 %collective-permute-start.8 = (bf16[2,384,1024]{2,1,0:T(8,128)(2,1)}, bf16[2,384,1024]{2,1,0:T(8,128)(2,1)}, u32[]{:S(2)}, u32[]{:S(2)}) collective-permute-start(bf16[2,384,1024]{2,1,0:T(8,128)(2,1)} %get-tuple-element.50), channel_id=1, source_target_pairs={{0,8},{8,0},{16,24},{24,16},{32,40},{40,32},{48,56},{56,48},{64,72... | collective-permute-start | bytes 4718600 | tf_op jit(solution)/shard_map/ppermute | solution.py:33
  79.9 15.2 %collective-permute-start.15 = (bf16[128,2048]{1,0:T(8,128)(2,1)S(1)}, bf16[128,2048]{1,0:T(8,128)(2,1)S(1)}, u32[]{:S(2)}, u32[]{:S(2)}) collective-permute-start(bf16[128,2048]{1,0:T(8,128)(2,1)S(1)} %get-tuple-element.64), channel_id=1, source_target_pairs={{0,2},{1,3},{2,4},{3,5},{4,6},{5,7},{6,0},{7,1},{8,10},{9,11},{10,... | collective-permute-start | bytes 1572872 | tf_op jit(solution)/shard_map/ppermute | solution.py:38
  81.5 26.0 %collective-permute-start.16 = (bf16[128,2048]{1,0:T(8,128)(2,1)S(1)}, bf16[128,2048]{1,0:T(8,128)(2,1)S(1)}, u32[]{:S(2)}, u32[]{:S(2)}) collective-permute-start(bf16[128,2048]{1,0:T(8,128)(2,1)S(1)} %get-tuple-element.65), channel_id=1, source_target_pairs={{0,4},{1,5},{2,6},{3,7},{4,0},{5,1},{6,2},{7,3},{8,12},{9,13},{10,... | collective-permute-start | bytes 1572872 | tf_op jit(solution)/shard_map/ppermute | solution.py:38
  84.4 23.1 %collective-permute-start.17 = (bf16[128,2048]{1,0:T(8,128)(2,1)S(1)}, bf16[128,2048]{1,0:T(8,128)(2,1)S(1)}, u32[]{:S(2)}, u32[]{:S(2)}) collective-permute-start(bf16[128,2048]{1,0:T(8,128)(2,1)S(1)} %get-tuple-element.66), channel_id=1, source_target_pairs={{0,6},{1,7},{2,0},{3,1},{4,2},{5,3},{6,4},{7,5},{8,14},{9,15},{10,... | collective-permute-start | bytes 1572872 | tf_op jit(solution)/shard_map/ppermute | solution.py:38
  108.8 13.6 %copy-start.8 = (bf16[1,512,1024]{2,1,0:T(8,128)(2,1)S(1)}, bf16[1,512,1024]{2,1,0:T(8,128)(2,1)}, u32[]{:S(2)}) copy-start(bf16[1,512,1024]{2,1,0:T(8,128)(2,1)} %param.6) | copy-start | bytes 3145732
  108.8 10.6 %collective-permute-start.18 = (bf16[32,2048]{1,0:T(8,128)(2,1)}, bf16[32,2048]{1,0:T(8,128)(2,1)}, u32[]{:S(2)}, u32[]{:S(2)}) collective-permute-start(bf16[32,2048]{1,0:T(8,128)(2,1)} %get-tuple-element.68), channel_id=1, source_target_pairs={{0,32},{8,40},{16,48},{24,56},{32,64},{40,72},{48,80},{56,88},{64,... | collective-permute-start | bytes 393224 | tf_op jit(solution)/shard_map/ppermute | solution.py:38
  109.9 9.5 %collective-permute-start.19 = (bf16[32,2048]{1,0:T(8,128)(2,1)}, bf16[32,2048]{1,0:T(8,128)(2,1)}, u32[]{:S(2)}, u32[]{:S(2)}) collective-permute-start(bf16[32,2048]{1,0:T(8,128)(2,1)} %get-tuple-element.69), channel_id=1, source_target_pairs={{0,64},{8,72},{16,80},{24,88},{32,96},{40,104},{48,112},{56,120},{... | collective-permute-start | bytes 393224 | tf_op jit(solution)/shard_map/ppermute | solution.py:38
  112.7 6.8 %collective-permute-start.20 = (bf16[32,2048]{1,0:T(8,128)(2,1)S(1)}, bf16[32,2048]{1,0:T(8,128)(2,1)}, u32[]{:S(2)}, u32[]{:S(2)}) collective-permute-start(bf16[32,2048]{1,0:T(8,128)(2,1)S(1)} %get-tuple-element.70), channel_id=1, source_target_pairs={{0,96},{8,104},{16,112},{24,120},{32,0},{40,8},{48,16},{56,24},{64... | collective-permute-start | bytes 393224 | tf_op jit(solution)/shard_map/ppermute | solution.py:38
  114.1 8.3 %copy-start.10 = (bf16[512,1024]{1,0:T(8,128)(2,1)S(1)}, bf16[512,1024]{1,0:T(8,128)(2,1)}, u32[]{:S(2)}) copy-start(bf16[512,1024]{1,0:T(8,128)(2,1)} %copy-done.9) | copy-start | bytes 3145732
  114.1 1.5 copy-start.14
  117.4 20.0 %collective-permute-start.10 = (bf16[2,128,1024]{2,1,0:T(8,128)(2,1)S(1)}, bf16[2,128,1024]{2,1,0:T(8,128)(2,1)S(1)}, u32[]{:S(2)}, u32[]{:S(2)}) collective-permute-start(bf16[2,128,1024]{2,1,0:T(8,128)(2,1)S(1)} %get-tuple-element.56), channel_id=1, source_target_pairs={{0,16},{8,24},{16,0},{24,8},{32,48},{40,56},{48,32},{56,40},{64,80... | collective-permute-start | bytes 1572872 | tf_op jit(solution)/shard_map/ppermute | solution.py:33
  119.2 32.2 %collective-permute-start.9 = (bf16[2,128,1024]{2,1,0:T(8,128)(2,1)S(1)}, bf16[2,128,1024]{2,1,0:T(8,128)(2,1)S(1)}, u32[]{:S(2)}, u32[]{:S(2)}) collective-permute-start(bf16[2,128,1024]{2,1,0:T(8,128)(2,1)S(1)} %get-tuple-element.51._), channel_id=1, source_target_pairs={{0,16},{8,24},{16,0},{24,8},{32,48},{40,56},{48,32},{56,40},{64,80... | collective-permute-start | bytes 1572872 | tf_op jit(solution)/shard_map/ppermute | solution.py:33
  120.6 21.7 %collective-permute-start.21 = (bf16[16,2048]{1,0:T(8,128)(2,1)S(1)}, bf16[16,2048]{1,0:T(8,128)(2,1)S(1)}, u32[]{:S(2)}, u32[]{:S(2)}) collective-permute-start(bf16[16,2048]{1,0:T(8,128)(2,1)S(1)} %fusion.1), channel_id=1, source_target_pairs={{0,16},{8,24},{16,0},{24,8},{32,48},{40,56},{48,32},{56,40},{64,80... | collective-permute-start | bytes 196616 | tf_op jit(solution)/shard_map/ppermute | solution.py:33
  122.4 4.0 %copy-start.1 = (bf16[8,1280,512]{2,1,0:T(8,128)(2,1)S(1)}, bf16[8,1280,512]{2,1,0:T(8,128)(2,1)}, u32[]{:S(2)}) copy-start(bf16[8,1280,512]{2,1,0:T(8,128)(2,1)} %copy-done) | copy-start | bytes 31457284
  126.4 1.6 %copy-start.12 = (f32[1024,512]{1,0:T(8,128)S(1)}, f32[1024,512]{1,0:T(8,128)}, u32[]{:S(2)}) copy-start(f32[1024,512]{1,0:T(8,128)} %copy-done.11) | copy-start | bytes 6291460
  128.0 18.1 %copy-start.6 = (bf16[1024,2048]{1,0:T(8,128)(2,1)S(1)}, bf16[1024,2048]{1,0:T(8,128)(2,1)}, u32[]{:S(2)}) copy-start(bf16[1024,2048]{1,0:T(8,128)(2,1)} %w_ref.1) | copy-start | bytes 12582916
  128.0 18.1 %copy-start.16 = (bf16[512,1024]{1,0:T(8,128)(2,1)S(1)}, bf16[512,1024]{1,0:T(8,128)(2,1)}, u32[]{:S(2)}) copy-start(bf16[512,1024]{1,0:T(8,128)(2,1)} %copy-done.15) | copy-start | bytes 3145732
  137.5 13.9 %collective-permute-start.11 = (bf16[2,64,1024]{2,1,0:T(8,128)(2,1)S(1)}, bf16[2,64,1024]{2,1,0:T(8,128)(2,1)S(1)}, u32[]{:S(2)}, u32[]{:S(2)}) collective-permute-start(bf16[2,64,1024]{2,1,0:T(8,128)(2,1)S(1)} %get-tuple-element.57), channel_id=1, source_target_pairs={{0,32},{8,40},{16,48},{24,56},{32,0},{40,8},{48,16},{56,24},{64,96... | collective-permute-start | bytes 786440 | tf_op jit(solution)/shard_map/ppermute | solution.py:33
  138.2 13.2 %collective-permute-start.12 = (bf16[2,32,1024]{2,1,0:T(8,128)(2,1)S(1)}, bf16[2,32,1024]{2,1,0:T(8,128)(2,1)S(1)}, u32[]{:S(2)}, u32[]{:S(2)}) collective-permute-start(bf16[2,32,1024]{2,1,0:T(8,128)(2,1)S(1)} %get-tuple-element.58), channel_id=1, source_target_pairs={{0,96},{8,104},{16,112},{24,120},{32,64},{40,72},{48,80},{56,88},{... | collective-permute-start | bytes 393224 | tf_op jit(solution)/shard_map/ppermute | solution.py:33
  139.7 11.7 %collective-permute-start.13 = (bf16[2,32,1024]{2,1,0:T(8,128)(2,1)S(1)}, bf16[2,32,1024]{2,1,0:T(8,128)(2,1)S(1)}, u32[]{:S(2)}, u32[]{:S(2)}) collective-permute-start(bf16[2,32,1024]{2,1,0:T(8,128)(2,1)S(1)} %get-tuple-element.59), channel_id=1, source_target_pairs={{0,64},{8,72},{16,80},{24,88},{32,96},{40,104},{48,112},{56,120},{... | collective-permute-start | bytes 393224 | tf_op jit(solution)/shard_map/ppermute | solution.py:33
  142.3 14.2 %collective-permute-start.22 = (f32[8,2048]{1,0:T(8,128)S(1)}, f32[8,2048]{1,0:T(8,128)S(1)}, u32[]{:S(2)}, u32[]{:S(2)}) collective-permute-start(f32[8,2048]{1,0:T(8,128)S(1)} %dynamic-slice_bitcast_fusion), channel_id=1, source_target_pairs={{0,1},{1,0},{2,3},{3,2},{4,5},{5,4},{6,7},{7,6},{8,9},{9,8},{10,11... | collective-permute-start | bytes 196616 | tf_op jit(solution)/shard_map/ppermute | solution.py:33
  146.1 1.2 copy-start.17

commit v3 on v2

v3 whole, which is shorter than its diff:
```python
from functools import partial
import math

import jax
import jax.numpy as jnp
import numpy as np
from jax import lax
from jax.experimental import pallas as pl
from jax.experimental.pallas import tpu as pltpu
from jax.sharding import PartitionSpec as P

HEADS = 8
HEAD_DIM = 128
HD = 1024
D = 2048
ROWS = 512
GROUPS = 1
PER = HEADS // GROUPS
COLS = PER * HEAD_DIM
FACTORS = (4, 8, 16)
COARSE = tuple(ROWS // factor for factor in FACTORS)
SCALE = 1.0 / math.sqrt(HEAD_DIM)
BIG = float(2**30)
F32 = jnp.float32
BF16 = jnp.bfloat16


def params(mebibytes):
    return pltpu.CompilerParams(vmem_limit_bytes=mebibytes * 2**20)


def swap(array, axis, bits):
    return lax.ppermute(array, axis, [(i, i ^ bits) for i in range(lax.axis_size(axis))])


def shift(array, axis, step):
    size = lax.axis_size(axis)
    return lax.ppermute(array, axis, [(i, (i + step) % size) for i in range(size)])


def dot_nt(a, b):
    return lax.dot_general(a, b, (((1,), (1,)), ((), ())), preferred_element_type=F32)


def dot_nn(a, b):
    return lax.dot_general(a, b, (((1,), (0,)), ((), ())), preferred_element_type=F32)


def dot_tn(a, b):
    return lax.dot_general(a, b, (((0,), (0,)), ((), ())), preferred_element_type=F32)


def iota(shape, dim):
    return lax.broadcasted_iota(jnp.int32, shape, dim)


def offset_parts(factor):
    rest = math.log(factor) / SCALE
    parts = []
    for _ in range(3):
        part = float(np.asarray(rest, dtype=jnp.bfloat16))
        parts.append(part)
        rest = rest - part
    return parts


def pool_matrix(factor, weight):
    count = ROWS // factor
    row, col = iota((count, ROWS), 0), iota((count, ROWS), 1)
    inside = (col >= row * factor) & (col < row * factor + weight)
    return jnp.where(inside, 1.0 / weight, 0.0).astype(BF16)


def pool_kernel(seg_hbm, key_hbm, value_hbm, one, two, three, fq_ref, fk_ref, seg_ref, key_ref, value_ref, sems):
    copies = [
        pltpu.make_async_copy(source, target, sems.at[place])
        for place, (source, target) in enumerate(((seg_hbm, seg_ref), (key_hbm, key_ref), (value_hbm, value_ref)))
    ]
    for copy in copies:
        copy.start()
    outs = (one, two, three)
    starts = np.cumsum((0,) + COARSE)
    pool = jnp.concatenate([pool_matrix(factor, factor) for factor in FACTORS], 0)
    pick = jnp.concatenate([pool_matrix(factor, 1) for factor in FACTORS], 0)
    copies[0].wait()
    seg = seg_ref[...]
    kind = iota((8, ROWS), 0)
    rows = jnp.where(kind < 2, jnp.where(seg == kind, 1.0, 0.0), jnp.where(kind == 2, 1.0, 0.0)).astype(BF16)
    i, j = iota((8, HEAD_DIM), 0), iota((8, HEAD_DIM), 1)
    to_key = jnp.where((i < 2) & (i == j), 1.0, 0.0).astype(BF16)
    wrong = ((i == 0) & (j == 1)) | ((i == 1) & (j == 0))
    ones = (i == 2) & (j >= 2) & (j < 5)
    to_query = jnp.where(wrong, -BIG, jnp.where(ones, 1.0, 0.0)).astype(BF16)
    own = dot_tn(rows, to_key).astype(BF16)
    fk_ref[...] = own
    fq_ref[...] = dot_tn(rows, to_query).astype(BF16)
    picked = dot_nn(pick, own)
    lane = iota((1, HEAD_DIM), 1)
    for place, (factor, out) in enumerate(zip(FACTORS, outs)):
        parts = offset_parts(factor)
        offset = jnp.where(lane == 2, parts[0], jnp.where(lane == 3, parts[1], jnp.where(lane == 4, parts[2], 0.0)))
        out[:, 2 * HD :] = (picked[starts[place] : starts[place + 1]] + offset).astype(BF16)
    for copy, ref, column in zip(copies[1:], (key_ref, value_ref), (0, HD)):
        copy.wait()
        for start in range(0, HD, 256):
            mean = dot_nn(pool, ref[:, start : start + 256])
            for place, out in enumerate(outs):
                out[:, column + start : column + start + 256] = mean[starts[place] : starts[place + 1]].astype(BF16)


WIDTH = 2 * HD + HEAD_DIM
POOL_LIMIT = 60
WHOLE = pl.BlockSpec(memory_space=pltpu.VMEM)
ANY = pl.BlockSpec(memory_space=pl.ANY)
HBM = pl.BlockSpec(memory_space=pltpu.HBM)
MARK = jax.ShapeDtypeStruct((8, 128), F32)


def pool(seg, key, value):
    feature = jax.ShapeDtypeStruct((ROWS, HEAD_DIM), BF16)
    token = pltpu.VMEM((ROWS, HD), BF16)
    return pl.pallas_call(
        pool_kernel,
        in_specs=[HBM] * 3,
        out_specs=[WHOLE] * 5,
        out_shape=[jax.ShapeDtypeStruct((count, WIDTH), BF16) for count in COARSE] + [feature, feature],
        scratch_shapes=[pltpu.VMEM((1, ROWS), jnp.int32), token, token, pltpu.SemaphoreType.DMA((3,))],
        compiler_params=params(POOL_LIMIT),
        cost_estimate=pl.CostEstimate(flops=2 * 224 * ROWS * 2 * HD, bytes_accessed=2 * 2**20, transcendentals=0),
    )(seg, key, value)


def pause_kernel(*refs):
    refs[-1][...] = jnp.zeros_like(refs[-1])


def pause(after):
    return pl.pallas_call(
        pause_kernel,
        in_specs=[ANY] * len(after),
        out_specs=WHOLE,
        out_shape=MARK,
        compiler_params=params(1),
        cost_estimate=pl.CostEstimate(flops=2 * 10**10, bytes_accessed=0, transcendentals=0),
    )(*after)


COARSE_ROWS = 768
RATE = SCALE * math.log2(math.e)


def columns(h):
    return pl.ds(pl.multiple_of(h * HEAD_DIM, HEAD_DIM), HEAD_DIM)


def pair(refs, place, at):
    return jnp.concatenate([refs[2 * place][:, at], refs[2 * place + 1][:, at]], 0)


def joined(total, add):
    return add if total is None else total + add


def each_head(step):
    lax.fori_loop(0, HEADS, lambda h, carry: (step(h), carry)[1], 0)


def local_forward_kernel(*refs):
    q_ref, k_ref, v_ref, fq_ref, fk_ref = refs[:5]
    p_ref, mixed_ref, stat_ref, scores = refs[-4:]

    def step(h):
        at = columns(h)
        query = jnp.concatenate([q_ref[:, at], fq_ref[...]], 1)
        top = None
        for start in (0, 256):
            rows = pl.ds(start, 256)
            here = dot_nt(jnp.concatenate([k_ref[rows, at], fk_ref[rows, :]], 1), query) * RATE
            scores[rows, :] = here
            peak = jnp.max(here, 0, keepdims=True)
            top = peak if top is None else jnp.maximum(top, peak)
        total, mixed = None, None
        for start in (0, 256):
            rows = pl.ds(start, 256)
            here = jnp.exp2(scores[rows, :] - top)
            total = joined(total, jnp.sum(here, 0, keepdims=True))
            here = here.astype(BF16)
            p_ref[h, rows, :] = here
            mixed = joined(mixed, dot_tn(v_ref[rows, at], here))
        mixed_ref[at, :] = mixed
        stat_ref[h, 0:1, :] = top
        stat_ref[h, 1:2, :] = total

    each_head(step)


def local_forward(query, key, value, fq, fk, after):
    return pl.pallas_call(
        local_forward_kernel,
        in_specs=[WHOLE] * 5 + [ANY] * len(after),
        out_specs=[WHOLE] * 3,
        out_shape=[
            jax.ShapeDtypeStruct((HEADS, ROWS, ROWS), BF16),
            jax.ShapeDtypeStruct((HD, ROWS), F32),
            jax.ShapeDtypeStruct((HEADS, 8, ROWS), F32),
        ],
        scratch_shapes=[pltpu.VMEM((ROWS, ROWS), F32)],
        compiler_params=params(12),
        cost_estimate=pl.CostEstimate(
            flops=HEADS * 16 * ROWS * ROWS * HEAD_DIM, bytes_accessed=9 * 2**20, transcendentals=HEADS * ROWS * ROWS
        ),
    )(query, key, value, fq, fk, *after)


def coarse_forward_kernel(*refs):
    q_ref, g_ref, fq_ref, mixed_ref, stat_ref = refs[:5]
    pieces = refs[5:11]
    p_ref, o_ref, ot_ref, row_ref, scores = refs[11:]

    def step(h):
        at = columns(h)
        query = jnp.concatenate([q_ref[:, at], fq_ref[...]], 1)
        before, total = stat_ref[h, 0:1, :], stat_ref[h, 1:2, :]
        top = before
        for place in range(3):
            key = jnp.concatenate([pair(pieces, place, at), pair(pieces, place, slice(2 * HD, WIDTH))], 1)
            here = dot_nt(key, query) * RATE
            scores[pl.ds(place * 256, 256), :] = here
            top = jnp.maximum(top, jnp.max(here, 0, keepdims=True))
        factor = jnp.exp2(before - top)
        total = total * factor
        for place in range(3):
            rows = pl.ds(place * 256, 256)
            here = jnp.exp2(scores[rows, :] - top)
            scores[rows, :] = here
            total = total + jnp.sum(here, 0, keepdims=True)
        inverse = 1.0 / total
        factor = factor * inverse
        mixed = mixed_ref[at, :] * factor
        for place in range(3):
            rows = pl.ds(place * 256, 256)
            here = (scores[rows, :] * inverse).astype(BF16)
            p_ref[h, rows, :] = here
            mixed = mixed + dot_tn(pair(pieces, place, columns(HEADS + h)), here)
        ot_ref[at, :] = mixed.astype(BF16)
        o_ref[:, at] = mixed.T.astype(BF16)
        row_ref[h, 0:1, :] = jnp.sum(g_ref[:, at].astype(F32).T * mixed, 0, keepdims=True)
        row_ref[h, 1:2, :] = factor

    each_head(step)


def coarse_forward(query, grad, fq, mixed, stats, pieces):
    return pl.pallas_call(
        coarse_forward_kernel,
        in_specs=[WHOLE] * 11,
        out_specs=[WHOLE] * 4,
        out_shape=[
            jax.ShapeDtypeStruct((HEADS, COARSE_ROWS, ROWS), BF16),
            jax.ShapeDtypeStruct((ROWS, HD), BF16),
            jax.ShapeDtypeStruct((HD, ROWS), BF16),
            jax.ShapeDtypeStruct((HEADS, 8, ROWS), F32),
        ],
        scratch_shapes=[pltpu.VMEM((COARSE_ROWS, ROWS), F32)],
        compiler_params=params(12),
        cost_estimate=pl.CostEstimate(
            flops=HEADS * 16 * ROWS * COARSE_ROWS * HEAD_DIM,
            bytes_accessed=16 * 2**20,
            transcendentals=HEADS * ROWS * COARSE_ROWS,
        ),
    )(query, grad, fq, mixed, stats, *pieces)


def slope_of(weight, value, grad, delta):
    return (weight.astype(F32) * (dot_nt(value, grad) - delta)).astype(BF16)


def coarse_backward_kernel(*refs):
    q_ref, g_ref, row_ref, p_ref = refs[:4]
    pieces = refs[4:10]
    keep_ref, give_ref, dq_ref = refs[-3:]

    def step(h):
        at = columns(h)
        q, g = q_ref[:, at], g_ref[:, at]
        delta = row_ref[h, 0:1, :]
        grad_q = None
        for place in range(3):
            weight = p_ref[h, pl.ds(place * 256, 256), :]
            key, value = pair(pieces, place, at), pair(pieces, place, columns(HEADS + h))
            slope = slope_of(weight, value, g, delta)
            grads = ((dot_nn(slope, q) * SCALE).astype(BF16), dot_nn(weight, g).astype(BF16))
            for side, grad in enumerate(grads):
                for half in range(2):
                    piece = 2 * place + half
                    out, row = (keep_ref, piece * 128) if piece < 3 else (give_ref, (piece - 3) * 128)
                    out[side, pl.ds(row, 128), at] = grad[half * 128 : half * 128 + 128]
            grad_q = joined(grad_q, dot_tn(key, slope))
        dq_ref[at, :] = grad_q

    each_head(step)


def coarse_backward(query, grad, rows, weights, pieces, after):
    return pl.pallas_call(
        coarse_backward_kernel,
        in_specs=[WHOLE] * 10 + [ANY] * len(after),
        out_specs=[WHOLE] * 3,
        out_shape=[
            jax.ShapeDtypeStruct((2, 384, HD), BF16),
            jax.ShapeDtypeStruct((2, 384, HD), BF16),
            jax.ShapeDtypeStruct((HD, ROWS), F32),
        ],
        compiler_params=params(12),
        cost_estimate=pl.CostEstimate(
            flops=HEADS * 16 * ROWS * COARSE_ROWS * HEAD_DIM, bytes_accessed=16 * 2**20, transcendentals=0
        ),
    )(query, grad, rows, weights, *pieces, *after)


def local_backward_kernel(*refs):
    q_ref, k_ref, v_ref, g_ref, row_ref, p_ref, part_ref = refs[:7]
    dq_ref, dk_ref, dv_ref, mark_ref = refs[-4:]
    mark_ref[...] = jnp.zeros_like(mark_ref)

    def step(h):
        at = columns(h)
        q, g = q_ref[:, at], g_ref[:, at]
        delta, factor = row_ref[h, 0:1, :], row_ref[h, 1:2, :]
        grad_q = part_ref[at, :]
        for start in (0, 256):
            rows = pl.ds(start, 256)
            weight = p_ref[h, rows, :].astype(F32) * factor
            slope = (weight * (dot_nt(v_ref[rows, at], g) - delta)).astype(BF16)
            dk_ref[rows, at] = dot_nn(slope, q) * SCALE
            dv_ref[rows, at] = dot_nn(weight.astype(BF16), g)
            grad_q = grad_q + dot_tn(k_ref[rows, at], slope)
        dq_ref[:, at] = (grad_q * SCALE).T.astype(BF16)

    each_head(step)


def local_backward(query, key, value, grad, rows, weights, partial_q, after):
    return pl.pallas_call(
        local_backward_kernel,
        in_specs=[WHOLE] * 7 + [ANY] * len(after),
        out_specs=[WHOLE] * 4,
        out_shape=[
            jax.ShapeDtypeStruct((ROWS, HD), BF16),
            jax.ShapeDtypeStruct((ROWS, HD), F32),
            jax.ShapeDtypeStruct((ROWS, HD), F32),
            MARK,
        ],
        compiler_params=params(12),
        cost_estimate=pl.CostEstimate(
            flops=HEADS * 16 * ROWS * ROWS * HEAD_DIM, bytes_accessed=16 * 2**20, transcendentals=0
        ),
    )(query, key, value, grad, rows, weights, partial_q, *after)


def project_kernel(a_ref, w_ref, _, out_ref, mark_ref):
    mark_ref[...] = jnp.zeros_like(mark_ref)
    out_ref[...] = dot_nn(a_ref[...], w_ref[...]).astype(BF16)


def project(attention, weight, after):
    tile = 512
    return pl.pallas_call(
        project_kernel,
        grid=(D // tile,),
        in_specs=[
            pl.BlockSpec((ROWS, HD), lambda n: (0, 0)),
            pl.BlockSpec((HD, tile), lambda n: (0, n)),
            ANY,
        ],
        out_specs=[pl.BlockSpec((ROWS, tile), lambda n: (0, n)), pl.BlockSpec((8, 128), lambda n: (0, 0))],
        out_shape=[jax.ShapeDtypeStruct((ROWS, D), BF16), MARK],
        compiler_params=params(12),
        cost_estimate=pl.CostEstimate(flops=2 * ROWS * HD * D, bytes_accessed=7 * 2**20, transcendentals=0),
    )(attention, weight, after)


def stack_kernel(count, *refs):
    out, start = refs[-1], 0
    for ref in refs[:count]:
        out[pl.ds(start, ref.shape[0]), :] = ref[...]
        start = start + ref.shape[0]


def stack(arrays, after):
    rows, width = sum(array.shape[0] for array in arrays), arrays[0].shape[1]
    return pl.pallas_call(
        partial(stack_kernel, len(arrays)),
        in_specs=[WHOLE] * len(arrays) + [ANY] * len(after),
        out_specs=WHOLE,
        out_shape=jax.ShapeDtypeStruct((rows, width), BF16),
        compiler_params=params(4),
        cost_estimate=pl.CostEstimate(flops=0, bytes_accessed=4 * rows * width, transcendentals=0),
    )(*arrays, *after)


def grad_weight_kernel(place_ref, ot_ref, c_ref, keep_ref, give_ref, lhs):
    @pl.when(pl.program_id(0) == 0)
    def _():
        core, y = place_ref[0], place_ref[1]
        for slot in range(2):
            half = core if slot == 0 else 1 - core
            for step in range(4):
                target = lax.rem(y + step, 4)
                for j in range(PER):
                    source = pl.multiple_of(j * 128 + half * 64 + target * 16, 16)
                    lhs[pl.ds(((slot * 4 + step) * PER + j) * 16, 16), :] = ot_ref[pl.ds(source, 16), :]

    out = dot_nn(lhs[...], c_ref[...])
    keep_ref[...] = out[: COLS // 2].astype(BF16)
    give_ref[...] = out[COLS // 2 :].astype(BF16)


def grad_weight_part(place, ot, cotangent):
    tile = 512
    shape = jax.ShapeDtypeStruct((COLS // 2, D), BF16)
    out = pl.BlockSpec((COLS // 2, tile), lambda n, s: (0, n))
    return pl.pallas_call(
        grad_weight_kernel,
        grid_spec=pltpu.PrefetchScalarGridSpec(
            num_scalar_prefetch=1,
            grid=(D // tile,),
            in_specs=[
                pl.BlockSpec((COLS, ROWS), lambda n, s: (0, 0)),
                pl.BlockSpec((ROWS, tile), lambda n, s: (0, n)),
            ],
            out_specs=[out, out],
            scratch_shapes=[pltpu.VMEM((COLS, ROWS), BF16)],
        ),
        out_shape=[shape, shape],
        compiler_params=params(16),
        cost_estimate=pl.CostEstimate(flops=2 * COLS * ROWS * D, bytes_accessed=6 * 1024 * 1024, transcendentals=0),
    )(place, ot, cotangent)


def split_sum_kernel(count, axis, bounds, *refs):
    ins, outs = refs[:count], refs[len(refs) - len(bounds) :]
    for (start, size), out in zip(bounds, outs):
        at = (slice(None),) * axis + (pl.ds(start, size),)
        total = ins[0][at].astype(F32)
        for ref in ins[1:]:
            total = total + ref[at].astype(F32)
        out[...] = total.astype(out.dtype)


def split_sum(arrays, axis, sizes, after=()):
    shape = arrays[0].shape
    starts = np.cumsum([0] + list(sizes))
    bounds = [(int(start), int(size)) for start, size in zip(starts, sizes)]
    whole = pl.BlockSpec(memory_space=pltpu.VMEM)
    outs = [jax.ShapeDtypeStruct(shape[:axis] + (size,) + shape[axis + 1 :], BF16) for size in sizes]
    count = math.prod(shape)
    return pl.pallas_call(
        partial(split_sum_kernel, len(arrays), axis, bounds),
        in_specs=[whole] * len(arrays) + [ANY] * len(after),
        out_specs=[whole] * len(sizes),
        out_shape=outs,
        compiler_params=params(16),
        cost_estimate=pl.CostEstimate(flops=count * len(arrays), bytes_accessed=2 * count * (len(arrays) + 1), transcendentals=0),
    )(*arrays, *after)


def turn_sum_kernel(rows, place_ref, a_ref, b_ref, c_ref, d_ref, *refs):
    x = place_ref[2]
    for step, out in enumerate(refs[len(refs) - 4 :]):
        at = pl.ds(pl.multiple_of(lax.rem(x + step, 4) * rows, 16), rows)
        total = (a_ref[at, :].astype(F32) + b_ref[at, :].astype(F32)) + (c_ref[at, :].astype(F32) + d_ref[at, :].astype(F32))
        out[...] = total.astype(BF16)


def turn_sum(place, arrays, after):
    rows = arrays[0].shape[0] // 4
    whole = pl.BlockSpec(memory_space=pltpu.VMEM)
    out = jax.ShapeDtypeStruct((rows, D), BF16)
    return pl.pallas_call(
        partial(turn_sum_kernel, rows),
        in_specs=[pl.BlockSpec(memory_space=pltpu.SMEM)] + [whole] * 4 + [ANY] * len(after),
        out_specs=[whole] * 4,
        out_shape=[out] * 4,
        compiler_params=params(16),
        cost_estimate=pl.CostEstimate(flops=16 * rows * D, bytes_accessed=40 * rows * D, transcendentals=0),
    )(place, *arrays, *after)


def finish_kernel(*refs):
    dk_ref, dv_ref, one, two, three, four = refs[:6]
    outs, mark_ref = refs[-3:-1], refs[-1]
    mark_ref[...] = jnp.zeros_like(mark_ref)
    token, row = iota((256, 128), 0), iota((256, 128), 1)
    spread = jnp.zeros((256, 128), F32)
    start = 0
    for factor, count in ((4, 64), (8, 32), (16, 16), (16, 16)):
        local = row - start
        inside = (local >= 0) & (local < count) & (token >= local * factor) & (token < local * factor + factor)
        spread = jnp.where(inside, 1.0 / factor, spread)
        start = start + count
    spread = spread.astype(BF16)
    for place, (own, out) in enumerate(zip((dk_ref, dv_ref), outs)):
        rows = jnp.concatenate([ref[place] for ref in (one, two, three, four)], 0)
        out[...] = (own[...] + dot_nn(spread, rows)).astype(BF16)


def finish(dk, dv, returned, after):
    half = pl.BlockSpec((256, HD), lambda i: (i, 0))
    shape = jax.ShapeDtypeStruct((ROWS, HD), BF16)
    return pl.pallas_call(
        finish_kernel,
        grid=(2,),
        in_specs=[half] * 2
        + [pl.BlockSpec((2, r.shape[1] // 2, HD), lambda i: (0, i, 0)) for r in returned]
        + [ANY] * len(after),
        out_specs=[half, half, pl.BlockSpec((8, 128), lambda i: (0, 0))],
        out_shape=[shape, shape, MARK],
        compiler_params=params(16),
        cost_estimate=pl.CostEstimate(flops=4 * ROWS * 128 * HD, bytes_accessed=10 * 2**20, transcendentals=0),
    )(dk, dv, *returned, *after)


def x_sum_kernel(place_ref, a_ref, b_ref, c_ref, d_ref, *refs):
    kept, given = refs[len(refs) - 2 :]
    z = place_ref[3]
    for out, half in ((kept, z), (given, 1 - z)):
        at = pl.ds(pl.multiple_of(half * 16, 16), 16)
        total = (a_ref[at, :].astype(F32) + b_ref[at, :].astype(F32)) + (c_ref[at, :].astype(F32) + d_ref[at, :].astype(F32))
        out[...] = total.astype(out.dtype)


def x_sum(place, arrays, after):
    return pl.pallas_call(
        x_sum_kernel,
        in_specs=[pl.BlockSpec(memory_space=pltpu.SMEM)] + [WHOLE] * 4 + [ANY] * len(after),
        out_specs=[WHOLE] * 2,
        out_shape=[jax.ShapeDtypeStruct((16, D), F32), jax.ShapeDtypeStruct((16, D), BF16)],
        compiler_params=params(4),
        cost_estimate=pl.CostEstimate(flops=128 * D, bytes_accessed=10 * 32 * D, transcendentals=0),
    )(place, *arrays, *after)


def z_sum_kernel(place_ref, a_ref, b_ref, kept, given):
    z = place_ref[4]
    total = a_ref[...] + b_ref[...].astype(F32)
    lower, upper = total[:8], total[8:]
    kept[...] = jnp.where(z == 0, lower, upper)
    given[...] = jnp.where(z == 0, upper, lower)


def z_sum(place, kept, received):
    shape = jax.ShapeDtypeStruct((8, D), F32)
    return pl.pallas_call(
        z_sum_kernel,
        in_specs=[pl.BlockSpec(memory_space=pltpu.SMEM)] + [WHOLE] * 2,
        out_specs=[WHOLE] * 2,
        out_shape=[shape, shape],
        compiler_params=params(4),
        cost_estimate=pl.CostEstimate(flops=32 * D, bytes_accessed=160 * D, transcendentals=0),
    )(place, kept, received)


def body(query, key, value, segment_ids, out_weight, cotangent):
    query, key, value = query[0], key[0], value[0]
    cotangent = cotangent[0]
    index = lax.axis_index("ctx")
    other = lax.axis_index("dp")
    core, x = jnp.bitwise_and(index, 1), jnp.right_shift(index, 2)
    z_lo = jnp.bitwise_and(jnp.right_shift(index, 1), 1)
    y, z_hi = jnp.right_shift(other, 1), jnp.bitwise_and(other, 1)
    place = jnp.stack([core, y, x, z_lo, z_hi]).astype(jnp.int32)

    one, two, three, fq, fk = pool(segment_ids, key, value)
    from_z = swap(one, "ctx", 2)
    two, three, mark = lax.optimization_barrier((two, three, pause([three])))
    grad_attention = lax.dot_general(
        cotangent, out_weight, (((1,), (1,)), ((), ())), preferred_element_type=F32
    ).astype(BF16)
    from_x = stack([swap(two, "ctx", 4), swap(three, "ctx", 12), swap(three, "ctx", 8)], [grad_attention, from_z, mark])
    from_xz = swap(from_x, "ctx", 2)
    local_weights, mixed, stats = local_forward(query, key, value, fq, fk, [from_x])
    from_xz, stats = lax.optimization_barrier((from_xz, stats))
    mine = [from_z, from_x, from_xz]
    pieces = mine + [swap(member, "ctx", 1) for member in mine]

    weights, attention, attention_t, rows = coarse_forward(query, grad_attention, fq, mixed, stats, pieces)
    kept, given = grad_weight_part(place, attention_t, cotangent)
    keep, give, partial_q = coarse_backward(query, grad_attention, rows, weights, pieces, [given])
    parts = split_sum([kept, swap(given, "ctx", 1)], 0, (128,) * 4, [keep])
    own_one, own_two, own_xz = split_sum([keep, swap(give, "ctx", 1)], 1, (128, 128, 128), [parts[0]])
    back_xz = swap(own_xz, "ctx", 2)
    back_z = swap(own_one, "ctx", 2)
    grad_query, dk, dv, mark = local_backward(
        query, key, value, grad_attention, rows, local_weights, partial_q, [own_one]
    )
    output, mark = project(attention, out_weight, mark)
    two, three, four = split_sum([own_two, back_xz], 1, (64, 32, 32), [mark])
    returned = [back_z, swap(two, "ctx", 4), swap(three, "ctx", 12), swap(four, "ctx", 8)]
    parts = [parts[0]] + [shift(parts[step], "dp", 2 * step) for step in (1, 2, 3)]
    parts = turn_sum(place, parts, [two])
    grad_key, grad_value, mark = finish(dk, dv, returned, [parts[0]])
    parts = [parts[0]] + [shift(parts[step], "ctx", 4 * step) for step in (1, 2, 3)]
    kept, given = x_sum(place, parts, [mark])
    kept, given = z_sum(place, kept, swap(given, "ctx", 2))
    grad_weight = kept + swap(given, "dp", 1)
    return output[None], grad_query[None], grad_key[None], grad_value[None], grad_weight


def solution(mesh):
    in_specs = (
        P("dp", "ctx", None),
        P("dp", "ctx", None),
        P("dp", "ctx", None),
        P("dp", "ctx"),
        P(),
        P("dp", "ctx", None),
    )
    out_specs = (
        P("dp", "ctx", None),
        P("dp", "ctx", None),
        P("dp", "ctx", None),
        P("dp", "ctx", None),
        P(("ctx", "dp"), None),
    )
    return jax.shard_map(body, mesh=mesh, in_specs=in_specs, out_specs=out_specs, check_vma=False)
```

time: 158 us -> 123 us (0.78)
  waiting for transfers between devices: 44.5 us -> 25.7 us
  local copies, waits for them, and re-layouts: 16.9 us -> 8.03 us
  Pallas kernels: 56.1 us -> 52.9 us
  matrix products: 5.18 us -> 2.38 us
    ppermute x6, waiting for transfers between devices: 21.8 us -> 6.66 us  [shift(): lax.ppermute(array, axis, [(i, (i + step) % size) for i in range(size)])]
    unnamed x44 -> x38, local copies, waits for them, and re-layouts: 16.8 us -> 7.95 us
    ppermute x17, waiting for transfers between devices: 22.7 us -> 19 us  [swap(): lax.ppermute(array, axis, [(i, i ^ bits) for i in range(lax.axis_size(axi...]
    dot_general x1, matrix products: 5.18 us -> 2.38 us  [body(): lax.dot_general(cotangent, out_weight, (((1,), (1,)), ((), ())), preferre...]
    ppermute x17, starting transfers between devices: 20.8 us -> 23 us  [swap(): lax.ppermute(array, axis, [(i, i ^ bits) for i in range(lax.axis_size(axi...]
    ppermute x6, starting transfers between devices: 11.1 us -> 9.27 us  [shift(): lax.ppermute(array, axis, [(i, (i + step) % size) for i in range(size)])]
    pallas_call x6 -> x10, Pallas kernels: 44.3 us -> 43.2 us  [the longest x1 10.9 us: coarse_forward(): pl.pallas_call(coarse_forward_kernel, in_specs=[WHOLE] * 11, out_specs=[W...]
  transfers between devices with their start and end apart: 23 -> 23, of which waited for: 7 -> 11; matrix products, arithmetic and copies ran while one was open for 4% -> 2% of each run, Pallas kernels for 22% -> 27%
where the time goes in v3:
time: 123 us
  Pallas kernels  52.9 us (43%)
  starting transfers between devices  32.3 us (26%)
  waiting for transfers between devices  25.7 us (21%)
  local copies, waits for them, and re-layouts  8.03 us (7%)
  matrix products  2.38 us (2%)
    ppermute x17, starting transfers between devices, swap(): lax.ppermute(array, axis, [(i, i ^ bits) for i in range(lax.axis_size(axi...  23 us
    ppermute x17, waiting for transfers between devices, swap(): lax.ppermute(array, axis, [(i, i ^ bits) for i in range(lax.axis_size(axi...  19 us
    pallas_call x1, Pallas kernels, coarse_forward(): pl.pallas_call(coarse_forward_kernel, in_specs=[WHOLE] * 11, out_specs=[W...  10.9 us
    pallas_call x1, Pallas kernels, coarse_backward(): pl.pallas_call(coarse_backward_kernel, in_specs=[WHOLE] * 10 + [ANY] * le...  10.9 us
    ppermute x6, starting transfers between devices, shift(): lax.ppermute(array, axis, [(i, (i + step) % size) for i in range(size)])  9.27 us
    pallas_call x1, Pallas kernels, local_backward(): pl.pallas_call(local_backward_kernel, in_specs=[WHOLE] * 7 + [ANY] * len(...  8 us
    unnamed x38, local copies, waits for them, and re-layouts  7.95 us
    ppermute x6, waiting for transfers between devices, shift(): lax.ppermute(array, axis, [(i, (i + step) % size) for i in range(size)])  6.66 us
  transfers between devices with their start and end apart: 23, of which 11 were waited for; matrix products, arithmetic and copies ran while one was open for 2% of the time, Pallas kernels for 27%

profile of v3, /device:TPU:0, one launch (start us, length us, event | category | flops | bytes accessed | tf_op | source)
XLA Modules:
  0.0 122.8 jit_solution(14732962737638261594)
XLA Ops:
  0.6 3.0 %shard_map.101 = (bf16[128,2176]{1,0:T(8,128)(2,1)}, bf16[64,2176]{1,0:T(8,128)(2,1)}, bf16[32,2176]{1,0:T(8,128)(2,1)}, bf16[512,128]{1,0:T(8,128)(2,1)}, bf16[512,128]{1,0:T(8,128)(2,1)}) custom-call(s32[1,512]{1,0:T(1,128)} %seg_hbm.1, bf16[512,1024]{1,0:T(8,128)(2,1)} %bitcast.16, bf16[512,1024]{1,0:T(8,128)(2,1)} %bitcast.19), custom_call_target="tpu_custom_call" | custom-call | flops 469762048 | bytes 2097152 | tf_op jit(solution)/shard_map/pallas_call | solution.py:122
  3.6 0.0 copy-start.9
  3.7 0.9 copy-done.9
  4.6 0.0 copy-start.4
  4.6 0.9 copy-done.10
  5.5 3.1 %collective-permute-start.2 = (bf16[32,2176]{1,0:T(8,128)(2,1)S(1)}, bf16[32,2176]{1,0:T(8,128)(2,1)S(1)}, u32[]{:S(2)}, u32[]{:S(2)}) collective-permute-start(bf16[32,2176]{1,0:T(8,128)(2,1)S(1)} %copy-done.10), channel_id=1, source_target_pairs={{0,64},{8,72},{16,80},{24,88},{32,96},{40,104},{48,112},{56,120},{... | collective-permute-start | bytes 417800 | tf_op jit(solution)/shard_map/ppermute | solution.py:33
  8.6 1.1 collective-permute-start.1
  9.7 2.0 %collective-permute-start.3 = (bf16[128,2176]{1,0:T(8,128)(2,1)S(1)}, bf16[128,2176]{1,0:T(8,128)(2,1)}, u32[]{:S(2)}, u32[]{:S(2)}) collective-permute-start(bf16[128,2176]{1,0:T(8,128)(2,1)S(1)} %copy-done.17), channel_id=1, source_target_pairs={{0,16},{8,24},{16,0},{24,8},{32,48},{40,56},{48,32},{56,40},{64,80... | collective-permute-start | bytes 1671176 | tf_op jit(solution)/shard_map/ppermute | solution.py:33
  11.7 2.4 %convolution_convert_fusion.refs_3_.refs_1_ = bf16[512,1024]{1,0:T(8,128)(2,1)S(1)} fusion(bf16[1024,2048]{1,0:T(8,128)(2,1)S(1)} %copy-done.2, bf16[1,512,2048]{2,1,0:T(8,128)(2,1)S(1)} %copy-done.4), kind=kOutput, calls=%fused_computation | convolution fusion | flops 2148007936 | bytes 7340032 | tf_op jit(solution)/shard_map/dot_general | solution.py:577
  14.1 0.0 copy-start
  14.1 0.0 copy-start.1
  14.1 0.0 copy-start.11
  14.2 1.0 collective-permute-done.1.refs_1_
  15.2 3.3 %collective-permute-done.refs_0_ = bf16[64,2176]{1,0:T(8,128)(2,1)S(1)} collective-permute-done((bf16[64,2176]{1,0:T(8,128)(2,1)S(1)}, bf16[64,2176]{1,0:T(8,128)(2,1)S(1)}, u32[]{:S(2)}, u32[]{:S(2)}) %collective-permute-start) | collective-permute-done | bytes 278560 | tf_op jit(solution)/shard_map/ppermute | solution.py:33
  18.5 5.4 %collective-permute-done.3.refs_4_.refs_5_ = bf16[128,2176]{1,0:T(8,128)(2,1)} collective-permute-done((bf16[128,2176]{1,0:T(8,128)(2,1)S(1)}, bf16[128,2176]{1,0:T(8,128)(2,1)}, u32[]{:S(2)}, u32[]{:S(2)}) %collective-permute-start.3) | collective-permute-done | bytes 557088 | tf_op jit(solution)/shard_map/ppermute | solution.py:33
  23.9 0.8 shard_map.103.refs_5_.refs_6_
  24.7 1.7 %collective-permute-start.4 = (bf16[128,2176]{1,0:T(8,128)(2,1)}, bf16[128,2176]{1,0:T(8,128)(2,1)}, u32[]{:S(2)}, u32[]{:S(2)}) collective-permute-start(bf16[128,2176]{1,0:T(8,128)(2,1)} %shard_map.103.refs_5_.refs_6_), channel_id=1, source_target_pairs={{0,16},{8,24},{16,0},{24,8},{32,48},{40,56},{48,32},{56,40},{64,80... | collective-permute-start | bytes 1671176 | tf_op jit(solution)/shard_map/ppermute | solution.py:33
  26.5 0.5 collective-permute-start.5
  27.0 6.5 %shard_map.104 = (bf16[8,512,512]{2,1,0:T(8,128)(2,1)S(1)}, f32[1024,512]{1,0:T(8,128)S(1)}, f32[8,8,512]{2,1,0:T(8,128)S(1)}) custom-call(bf16[512,1024]{1,0:T(8,128)(2,1)S(1)} %bitcast.23, bf16[512,1024]{1,0:T(8,128)(2,1)S(1)} %bitcast.17, bf16[512,1024]{1,0:T(8,128)(2,1)S(1)} %bitcast.20, bf16[512,128]{1,0:T(8,128)(2,1)S(1)} %copy-done.11, ...), custom_call_target="tpu_custom_call" | custom-call | flops 4294967296 | bytes 9437184 | tf_op jit(solution)/shard_map/pallas_call | solution.py:198
  33.5 2.0 %copy-done.13 = bf16[8,512,512]{2,1,0:T(8,128)(2,1)} copy-done((bf16[8,512,512]{2,1,0:T(8,128)(2,1)}, bf16[8,512,512]{2,1,0:T(8,128)(2,1)S(1)}, u32[]{:S(2)}) %copy-start.13) | copy-done | bytes 4194328
  35.5 1.3 %copy-done.15 = f32[1024,512]{1,0:T(8,128)} copy-done((f32[1024,512]{1,0:T(8,128)}, f32[1024,512]{1,0:T(8,128)S(1)}, u32[]{:S(2)}) %copy-start.15) | copy-done | bytes 2097176
  36.8 1.3 %collective-permute-done.4.refs_7_.refs_6_ = bf16[128,2176]{1,0:T(8,128)(2,1)} collective-permute-done((bf16[128,2176]{1,0:T(8,128)(2,1)}, bf16[128,2176]{1,0:T(8,128)(2,1)}, u32[]{:S(2)}, u32[]{:S(2)}) %collective-permute-start.4) | collective-permute-done | bytes 557088 | tf_op jit(solution)/shard_map/ppermute | solution.py:33
  38.1 0.0 collective-permute-start.7
  38.1 0.1 stack.23.place_ref
  38.2 2.2 %collective-permute-done.7.refs_10_.refs_9_ = bf16[128,2176]{1,0:T(8,128)(2,1)} collective-permute-done((bf16[128,2176]{1,0:T(8,128)(2,1)}, bf16[128,2176]{1,0:T(8,128)(2,1)}, u32[]{:S(2)}, u32[]{:S(2)}) %collective-permute-start.7) | collective-permute-done | bytes 557088 | tf_op jit(solution)/shard_map/ppermute | solution.py:33
  40.4 1.2 copy-done.7
  41.6 1.6 %copy-done.16 = f32[1024,512]{1,0:T(8,128)S(1)} copy-done((f32[1024,512]{1,0:T(8,128)S(1)}, f32[1024,512]{1,0:T(8,128)}, u32[]{:S(2)}) %copy-start.16) | copy-done | bytes 2097176
  43.2 10.9 %shard_map.105 = (bf16[8,768,512]{2,1,0:T(8,128)(2,1)S(1)}, bf16[512,1024]{1,0:T(8,128)(2,1)S(1)}, bf16[1024,512]{1,0:T(8,128)(2,1)S(1)}, f32[8,8,512]{2,1,0:T(8,128)S(1)}) custom-call(bf16[512,1024]{1,0:T(8,128)(2,1)S(1)} %bitcast.24, bf16[512,1024]{1,0:T(8,128)(2,1)S(1)} %convolution_convert_fusion.refs_3_.refs_1_, bf16[512,128]{1,0:T(8,128)(2,1)S(1)} %copy-done.11, ...), custom_call_target="tpu_custom_call" | custom-call | flops 6442450944 | bytes 16777216 | tf_op jit(solution)/shard_map/pallas_call | solution.py:254
  54.1 0.0 copy-start.8
  54.2 4.0 %shard_map.106 = (bf16[512,2048]{1,0:T(8,128)(2,1)S(1)}, bf16[512,2048]{1,0:T(8,128)(2,1)S(1)}) custom-call(s32[5]{0:T(128)S(1)} %stack.23.place_ref, bf16[1024,512]{1,0:T(8,128)(2,1)S(1)} %get-tuple-element.70.ot_ref, bf16[512,2048]{1,0:T(8,128)(2,1)S(1)} %bitcast.22), custom_call_target="tpu_custom_call" | custom-call | flops 2147483648 | bytes 6291456 | tf_op jit(solution)/shard_map/pallas_call | solution.py:423
  58.1 0.2 collective-permute-start.9
  58.3 10.9 %shard_map.107 = (bf16[2,384,1024]{2,1,0:T(8,128)(2,1)S(1)}, bf16[2,384,1024]{2,1,0:T(8,128)(2,1)S(1)}, f32[1024,512]{1,0:T(8,128)S(1)}) custom-call(bf16[512,1024]{1,0:T(8,128)(2,1)S(1)} %bitcast.25, bf16[512,1024]{1,0:T(8,128)(2,1)S(1)} %convolution_convert_fusion.refs_3_.refs_1_, f32[8,8,512]{2,1,0:T(8,128)S(1)} %get-tuple-element.67.refs_2_.refs_4_, ...), custom_call_target="tpu_custom_call" | custom-call | flops 6442450944 | bytes 16777216 | tf_op jit(solution)/shard_map/pallas_call | solution.py:305
  69.3 0.5 collective-permute-start.8
  69.7 0.5 shard_map.108
  70.2 1.6 %collective-permute-start.15 = (bf16[128,2048]{1,0:T(8,128)(2,1)S(1)}, bf16[128,2048]{1,0:T(8,128)(2,1)S(1)}, u32[]{:S(2)}, u32[]{:S(2)}) collective-permute-start(bf16[128,2048]{1,0:T(8,128)(2,1)S(1)} %get-tuple-element.89), channel_id=1, source_target_pairs={{0,2},{1,3},{2,4},{3,5},{4,6},{5,7},{6,0},{7,1},{8,10},{9,11},{10,... | collective-permute-start | bytes 1572872 | tf_op jit(solution)/shard_map/ppermute | solution.py:38
  71.8 2.9 %collective-permute-start.16 = (bf16[128,2048]{1,0:T(8,128)(2,1)S(1)}, bf16[128,2048]{1,0:T(8,128)(2,1)S(1)}, u32[]{:S(2)}, u32[]{:S(2)}) collective-permute-start(bf16[128,2048]{1,0:T(8,128)(2,1)S(1)} %get-tuple-element.90), channel_id=1, source_target_pairs={{0,4},{1,5},{2,6},{3,7},{4,0},{5,1},{6,2},{7,3},{8,12},{9,13},{10,... | collective-permute-start | bytes 1572872 | tf_op jit(solution)/shard_map/ppermute | solution.py:38
  74.7 1.3 %collective-permute-start.17 = (bf16[128,2048]{1,0:T(8,128)(2,1)S(1)}, bf16[128,2048]{1,0:T(8,128)(2,1)S(1)}, u32[]{:S(2)}, u32[]{:S(2)}) collective-permute-start(bf16[128,2048]{1,0:T(8,128)(2,1)S(1)} %get-tuple-element.91), channel_id=1, source_target_pairs={{0,6},{1,7},{2,0},{3,1},{4,2},{5,3},{6,4},{7,5},{8,14},{9,15},{10,... | collective-permute-start | bytes 1572872 | tf_op jit(solution)/shard_map/ppermute | solution.py:38
  76.1 0.4 shard_map.109
  76.4 1.6 %collective-permute-start.11 = (bf16[2,128,1024]{2,1,0:T(8,128)(2,1)S(1)}, bf16[2,128,1024]{2,1,0:T(8,128)(2,1)S(1)}, u32[]{:S(2)}, u32[]{:S(2)}) collective-permute-start(bf16[2,128,1024]{2,1,0:T(8,128)(2,1)S(1)} %get-tuple-element.84), channel_id=1, source_target_pairs={{0,16},{8,24},{16,0},{24,8},{32,48},{40,56},{48,32},{56,40},{64,80... | collective-permute-start | bytes 1572872 | tf_op jit(solution)/shard_map/ppermute | solution.py:33
  78.1 0.5 collective-permute-start.10
  78.6 8.0 %shard_map.110 = (bf16[512,1024]{1,0:T(8,128)(2,1)}, f32[512,1024]{1,0:T(8,128)S(1)}, f32[512,1024]{1,0:T(8,128)S(1)}, f32[8,128]{1,0:T(8,128)S(1)}) custom-call(bf16[512,1024]{1,0:T(8,128)(2,1)S(1)} %bitcast.26, bf16[512,1024]{1,0:T(8,128)(2,1)S(1)} %bitcast.18, bf16[512,1024]{1,0:T(8,128)(2,1)S(1)} %bitcast.21, ...), custom_call_target="tpu_custom_call" | custom-call | flops 4294967296 | bytes 16777216 | tf_op jit(solution)/shard_map/pallas_call | solution.py:344
  86.6 4.0 %shard_map.111 = (bf16[512,2048]{1,0:T(8,128)(2,1)}, f32[8,128]{1,0:T(8,128)S(1)}) custom-call(bf16[512,1024]{1,0:T(8,128)(2,1)S(1)} %get-tuple-element.66.a_ref, bf16[1024,2048]{1,0:T(8,128)(2,1)S(1)} %copy-done.3, f32[8,128]{1,0:T(8,128)S(1)} %get-tuple-element.78._), custom_call_target="tpu_custom_call" | custom-call | flops 2147483648 | bytes 7340032 | tf_op jit(solution)/shard_map/pallas_call | solution.py:368
  90.6 0.8 collective-permute-done.11.refs_1_
  91.4 0.1 shard_map.112
  91.5 1.5 %collective-permute-start.12 = (bf16[2,64,1024]{2,1,0:T(8,128)(2,1)S(1)}, bf16[2,64,1024]{2,1,0:T(8,128)(2,1)S(1)}, u32[]{:S(2)}, u32[]{:S(2)}) collective-permute-start(bf16[2,64,1024]{2,1,0:T(8,128)(2,1)S(1)} %get-tuple-element.86.refs_0_), channel_id=1, source_target_pairs={{0,32},{8,40},{16,48},{24,56},{32,0},{40,8},{48,16},{56,24},{64,96... | collective-permute-start | bytes 786440 | tf_op jit(solution)/shard_map/ppermute | solution.py:33
  93.0 0.0 collective-permute-done.15.b_ref
  93.0 2.1 %collective-permute-start.13 = (bf16[2,32,1024]{2,1,0:T(8,128)(2,1)S(1)}, bf16[2,32,1024]{2,1,0:T(8,128)(2,1)S(1)}, u32[]{:S(2)}, u32[]{:S(2)}) collective-permute-start(bf16[2,32,1024]{2,1,0:T(8,128)(2,1)S(1)} %get-tuple-element.87), channel_id=1, source_target_pairs={{0,96},{8,104},{16,112},{24,120},{32,64},{40,72},{48,80},{56,88},{... | collective-permute-start | bytes 393224 | tf_op jit(solution)/shard_map/ppermute | solution.py:33
  95.1 2.8 %collective-permute-done.16.c_ref = bf16[128,2048]{1,0:T(8,128)(2,1)S(1)} collective-permute-done((bf16[128,2048]{1,0:T(8,128)(2,1)S(1)}, bf16[128,2048]{1,0:T(8,128)(2,1)S(1)}, u32[]{:S(2)}, u32[]{:S(2)}) %collective-permute-start.16) | collective-permute-done | bytes 524320 | tf_op jit(solution)/shard_map/ppermute | solution.py:38
  97.9 2.9 %collective-permute-start.14 = (bf16[2,32,1024]{2,1,0:T(8,128)(2,1)S(1)}, bf16[2,32,1024]{2,1,0:T(8,128)(2,1)S(1)}, u32[]{:S(2)}, u32[]{:S(2)}) collective-permute-start(bf16[2,32,1024]{2,1,0:T(8,128)(2,1)S(1)} %get-tuple-element.88), channel_id=1, source_target_pairs={{0,64},{8,72},{16,80},{24,88},{32,96},{40,104},{48,112},{56,120},{... | collective-permute-start | bytes 393224 | tf_op jit(solution)/shard_map/ppermute | solution.py:33
  100.8 0.0 collective-permute-done.17.d_ref
  100.8 0.8 shard_map.113
  101.6 0.1 collective-permute-start.18
  101.8 2.6 %collective-permute-start.19 = (bf16[32,2048]{1,0:T(8,128)(2,1)S(1)}, bf16[32,2048]{1,0:T(8,128)(2,1)S(1)}, u32[]{:S(2)}, u32[]{:S(2)}) collective-permute-start(bf16[32,2048]{1,0:T(8,128)(2,1)S(1)} %get-tuple-element.96), channel_id=1, source_target_pairs={{0,64},{8,72},{16,80},{24,88},{32,96},{40,104},{48,112},{56,120},{... | collective-permute-start | bytes 393224 | tf_op jit(solution)/shard_map/ppermute | solution.py:38
  104.3 0.7 collective-permute-start.20
  105.0 1.9 %shard_map.114 = (bf16[512,1024]{1,0:T(8,128)(2,1)}, bf16[512,1024]{1,0:T(8,128)(2,1)}, f32[8,128]{1,0:T(8,128)S(1)}) custom-call(f32[512,1024]{1,0:T(8,128)S(1)} %get-tuple-element.81.refs_0_, f32[512,1024]{1,0:T(8,128)S(1)} %get-tuple-element.82.refs_1_, bf16[2,128,1024]{2,1,0:T(8,128)(2,1)S(1)} %collective-permute-done.10.refs_2_, ...), custom_call_target="tpu_custom_call" | custom-call | flops 268435456 | bytes 10485760 | tf_op jit(solution)/shard_map/pallas_call | solution.py:511
  107.0 3.4 %collective-permute-done.18.b_ref = bf16[32,2048]{1,0:T(8,128)(2,1)S(1)} collective-permute-done((bf16[32,2048]{1,0:T(8,128)(2,1)S(1)}, bf16[32,2048]{1,0:T(8,128)(2,1)S(1)}, u32[]{:S(2)}, u32[]{:S(2)}) %collective-permute-start.18) | collective-permute-done | bytes 131104 | tf_op jit(solution)/shard_map/ppermute | solution.py:38
  110.3 0.4 collective-permute-done.20.d_ref
  110.8 0.6 shard_map.115
  111.4 1.6 %collective-permute-start.21 = (bf16[16,2048]{1,0:T(8,128)(2,1)S(1)}, bf16[16,2048]{1,0:T(8,128)(2,1)S(1)}, u32[]{:S(2)}, u32[]{:S(2)}) collective-permute-start(bf16[16,2048]{1,0:T(8,128)(2,1)S(1)} %get-tuple-element.100), channel_id=1, source_target_pairs={{0,16},{8,24},{16,0},{24,8},{32,48},{40,56},{48,32},{56,40},{64,80... | collective-permute-start | bytes 196616 | tf_op jit(solution)/shard_map/ppermute | solution.py:33
  113.0 2.7 %collective-permute-done.21.b_ref = bf16[16,2048]{1,0:T(8,128)(2,1)S(1)} collective-permute-done((bf16[16,2048]{1,0:T(8,128)(2,1)S(1)}, bf16[16,2048]{1,0:T(8,128)(2,1)S(1)}, u32[]{:S(2)}, u32[]{:S(2)}) %collective-permute-start.21) | collective-permute-done | bytes 65568 | tf_op jit(solution)/shard_map/ppermute | solution.py:33
  115.7 0.6 shard_map.116
  116.3 3.6 %collective-permute-start.22 = (f32[8,2048]{1,0:T(8,128)S(1)}, f32[8,2048]{1,0:T(8,128)S(1)}, u32[]{:S(2)}, u32[]{:S(2)}) collective-permute-start(f32[8,2048]{1,0:T(8,128)S(1)} %get-tuple-element.102), channel_id=1, source_target_pairs={{0,1},{1,0},{2,3},{3,2},{4,5},{5,4},{6,7},{7,6},{8,9},{9,8},{10,11... | collective-permute-start | bytes 196616 | tf_op jit(solution)/shard_map/ppermute | solution.py:33
  119.9 2.2 %collective-permute-done.22 = f32[8,2048]{1,0:T(8,128)S(1)} collective-permute-done((f32[8,2048]{1,0:T(8,128)S(1)}, f32[8,2048]{1,0:T(8,128)S(1)}, u32[]{:S(2)}, u32[]{:S(2)}) %collective-permute-start.22) | collective-permute-done | bytes 65568 | tf_op jit(solution)/shard_map/ppermute | solution.py:33
  122.2 0.6 add.3
  (39 shorter events, 0.1 us)
Async XLA Ops:
  3.6 0.9 copy-start.9
  4.5 0.9 copy-start.10
  4.6 5.2 %copy-start.18 = (bf16[64,2176]{1,0:T(8,128)(2,1)S(1)}, bf16[64,2176]{1,0:T(8,128)(2,1)}, u32[]{:S(2)}) copy-start(bf16[64,2176]{1,0:T(8,128)(2,1)} %get-tuple-element.58) | copy-start | bytes 835588
  4.6 5.2 %copy-start.17 = (bf16[128,2176]{1,0:T(8,128)(2,1)S(1)}, bf16[128,2176]{1,0:T(8,128)(2,1)}, u32[]{:S(2)}) copy-start(bf16[128,2176]{1,0:T(8,128)(2,1)} %get-tuple-element.60) | copy-start | bytes 1671172
  4.6 7.2 %copy-start.2 = (bf16[1024,2048]{1,0:T(8,128)(2,1)S(1)}, bf16[1024,2048]{1,0:T(8,128)(2,1)}, u32[]{:S(2)}) copy-start(bf16[1024,2048]{1,0:T(8,128)(2,1)} %w_ref.1) | copy-start | bytes 12582916
  4.6 7.2 %copy-start.4 = (bf16[1,512,2048]{2,1,0:T(8,128)(2,1)S(1)}, bf16[1,512,2048]{2,1,0:T(8,128)(2,1)}, u32[]{:S(2)}) copy-start(bf16[1,512,2048]{2,1,0:T(8,128)(2,1)} %param.11) | copy-start | bytes 6291460
  5.5 8.7 %collective-permute-start.2 = (bf16[32,2176]{1,0:T(8,128)(2,1)S(1)}, bf16[32,2176]{1,0:T(8,128)(2,1)S(1)}, u32[]{:S(2)}, u32[]{:S(2)}) collective-permute-start(bf16[32,2176]{1,0:T(8,128)(2,1)S(1)} %copy-done.10), channel_id=1, source_target_pairs={{0,64},{8,72},{16,80},{24,88},{32,96},{40,104},{48,112},{56,120},{... | collective-permute-start | bytes 417800 | tf_op jit(solution)/shard_map/ppermute | solution.py:33
  8.6 6.7 %collective-permute-start.1 = (bf16[32,2176]{1,0:T(8,128)(2,1)S(1)}, bf16[32,2176]{1,0:T(8,128)(2,1)S(1)}, u32[]{:S(2)}, u32[]{:S(2)}) collective-permute-start(bf16[32,2176]{1,0:T(8,128)(2,1)S(1)} %copy-done.10), channel_id=1, source_target_pairs={{0,96},{8,104},{16,112},{24,120},{32,64},{40,72},{48,80},{56,88},{... | collective-permute-start | bytes 417800 | tf_op jit(solution)/shard_map/ppermute | solution.py:33
  9.7 8.8 %collective-permute-start = (bf16[64,2176]{1,0:T(8,128)(2,1)S(1)}, bf16[64,2176]{1,0:T(8,128)(2,1)S(1)}, u32[]{:S(2)}, u32[]{:S(2)}) collective-permute-start(bf16[64,2176]{1,0:T(8,128)(2,1)S(1)} %copy-done.18), channel_id=1, source_target_pairs={{0,32},{8,40},{16,48},{24,56},{32,0},{40,8},{48,16},{56,24},{64,96... | collective-permute-start | bytes 835592 | tf_op jit(solution)/shard_map/ppermute | solution.py:33
  9.7 14.2 %collective-permute-start.3 = (bf16[128,2176]{1,0:T(8,128)(2,1)S(1)}, bf16[128,2176]{1,0:T(8,128)(2,1)}, u32[]{:S(2)}, u32[]{:S(2)}) collective-permute-start(bf16[128,2176]{1,0:T(8,128)(2,1)S(1)} %copy-done.17), channel_id=1, source_target_pairs={{0,16},{8,24},{16,0},{24,8},{32,48},{40,56},{48,32},{56,40},{64,80... | collective-permute-start | bytes 1671176 | tf_op jit(solution)/shard_map/ppermute | solution.py:33
  11.7 15.3 %copy-start.6 = (bf16[1,512,1024]{2,1,0:T(8,128)(2,1)S(1)}, bf16[1,512,1024]{2,1,0:T(8,128)(2,1)}, u32[]{:S(2)}) copy-start(bf16[1,512,1024]{2,1,0:T(8,128)(2,1)} %param.6) | copy-start | bytes 3145732
  14.1 12.9 %copy-start = (bf16[1,512,1024]{2,1,0:T(8,128)(2,1)S(1)}, bf16[1,512,1024]{2,1,0:T(8,128)(2,1)}, u32[]{:S(2)}) copy-start(bf16[1,512,1024]{2,1,0:T(8,128)(2,1)} %param.7) | copy-start | bytes 3145732
  14.1 12.9 %copy-start.1 = (bf16[1,512,1024]{2,1,0:T(8,128)(2,1)S(1)}, bf16[1,512,1024]{2,1,0:T(8,128)(2,1)}, u32[]{:S(2)}) copy-start(bf16[1,512,1024]{2,1,0:T(8,128)(2,1)} %param.8) | copy-start | bytes 3145732
  14.1 12.9 %copy-start.11 = (bf16[512,128]{1,0:T(8,128)(2,1)S(1)}, bf16[512,128]{1,0:T(8,128)(2,1)}, u32[]{:S(2)}) copy-start(bf16[512,128]{1,0:T(8,128)(2,1)} %get-tuple-element.54.refs_3_.refs_2_) | copy-start | bytes 393220
  14.1 12.8 %copy-start.12 = (bf16[512,128]{1,0:T(8,128)(2,1)S(1)}, bf16[512,128]{1,0:T(8,128)(2,1)}, u32[]{:S(2)}) copy-start(bf16[512,128]{1,0:T(8,128)(2,1)} %get-tuple-element.55.refs_4_) | copy-start | bytes 393220
  24.7 13.4 %collective-permute-start.4 = (bf16[128,2176]{1,0:T(8,128)(2,1)}, bf16[128,2176]{1,0:T(8,128)(2,1)}, u32[]{:S(2)}, u32[]{:S(2)}) collective-permute-start(bf16[128,2176]{1,0:T(8,128)(2,1)} %shard_map.103.refs_5_.refs_6_), channel_id=1, source_target_pairs={{0,16},{8,24},{16,0},{24,8},{32,48},{40,56},{48,32},{56,40},{64,80... | collective-permute-start | bytes 1671176 | tf_op jit(solution)/shard_map/ppermute | solution.py:33
  26.5 11.7 %collective-permute-start.6 = (bf16[128,2176]{1,0:T(8,128)(2,1)}, bf16[128,2176]{1,0:T(8,128)(2,1)}, u32[]{:S(2)}, u32[]{:S(2)}) collective-permute-start(bf16[128,2176]{1,0:T(8,128)(2,1)} %shard_map.103.refs_5_.refs_6_), channel_id=1, source_target_pairs={{0,8},{8,0},{16,24},{24,16},{32,40},{40,32},{48,56},{56,48},{64,72... | collective-permute-start | bytes 1671176 | tf_op jit(solution)/shard_map/ppermute | solution.py:33
  26.5 11.7 %collective-permute-start.5 = (bf16[128,2176]{1,0:T(8,128)(2,1)}, bf16[128,2176]{1,0:T(8,128)(2,1)}, u32[]{:S(2)}, u32[]{:S(2)}) collective-permute-start(bf16[128,2176]{1,0:T(8,128)(2,1)} %collective-permute-done.3.refs_4_.refs_5_), channel_id=1, source_target_pairs={{0,8},{8,0},{16,24},{24,16},{32,40},{40,32},{48,56},{56,48},{64,72... | collective-permute-start | bytes 1671176 | tf_op jit(solution)/shard_map/ppermute | solution.py:33
  33.5 2.0 %copy-start.13 = (bf16[8,512,512]{2,1,0:T(8,128)(2,1)}, bf16[8,512,512]{2,1,0:T(8,128)(2,1)S(1)}, u32[]{:S(2)}) copy-start(bf16[8,512,512]{2,1,0:T(8,128)(2,1)S(1)} %get-tuple-element.68.refs_5_) | copy-start | bytes 12582916
  35.5 1.3 %copy-start.15 = (f32[1024,512]{1,0:T(8,128)}, f32[1024,512]{1,0:T(8,128)S(1)}, u32[]{:S(2)}) copy-start(f32[1024,512]{1,0:T(8,128)S(1)} %get-tuple-element.62.refs_3_) | copy-start | bytes 6291460
  38.1 2.3 %collective-permute-start.7 = (bf16[128,2176]{1,0:T(8,128)(2,1)}, bf16[128,2176]{1,0:T(8,128)(2,1)}, u32[]{:S(2)}, u32[]{:S(2)}) collective-permute-start(bf16[128,2176]{1,0:T(8,128)(2,1)} %collective-permute-done.4.refs_7_.refs_6_), channel_id=1, source_target_pairs={{0,8},{8,0},{16,24},{24,16},{32,40},{40,32},{48,56},{56,48},{64,72... | collective-permute-start | bytes 1671176 | tf_op jit(solution)/shard_map/ppermute | solution.py:33
  40.4 1.2 copy-start.7
  41.6 1.6 %copy-start.16 = (f32[1024,512]{1,0:T(8,128)S(1)}, f32[1024,512]{1,0:T(8,128)}, u32[]{:S(2)}) copy-start(f32[1024,512]{1,0:T(8,128)} %copy-done.15) | copy-start | bytes 6291460
  43.2 10.9 %copy-start.5 = (bf16[1,512,2048]{2,1,0:T(8,128)(2,1)S(1)}, bf16[1,512,2048]{2,1,0:T(8,128)(2,1)}, u32[]{:S(2)}) copy-start(bf16[1,512,2048]{2,1,0:T(8,128)(2,1)} %param.11) | copy-start | bytes 6291460
  54.1 4.2 %copy-start.8 = (bf16[1,512,1024]{2,1,0:T(8,128)(2,1)S(1)}, bf16[1,512,1024]{2,1,0:T(8,128)(2,1)}, u32[]{:S(2)}) copy-start(bf16[1,512,1024]{2,1,0:T(8,128)(2,1)} %param.6) | copy-start | bytes 3145732
  58.1 11.6 %collective-permute-start.9 = (bf16[512,2048]{1,0:T(8,128)(2,1)S(1)}, bf16[512,2048]{1,0:T(8,128)(2,1)S(1)}, u32[]{:S(2)}, u32[]{:S(2)}) collective-permute-start(bf16[512,2048]{1,0:T(8,128)(2,1)S(1)} %get-tuple-element.71.refs_10_), channel_id=1, source_target_pairs={{0,8},{8,0},{16,24},{24,16},{32,40},{40,32},{48,56},{56,48},{64,72... | collective-permute-start | bytes 6291464 | tf_op jit(solution)/shard_map/ppermute | solution.py:33
  69.3 6.8 %collective-permute-start.8 = (bf16[2,384,1024]{2,1,0:T(8,128)(2,1)S(1)}, bf16[2,384,1024]{2,1,0:T(8,128)(2,1)S(1)}, u32[]{:S(2)}, u32[]{:S(2)}) collective-permute-start(bf16[2,384,1024]{2,1,0:T(8,128)(2,1)S(1)} %get-tuple-element.74), channel_id=1, source_target_pairs={{0,8},{8,0},{16,24},{24,16},{32,40},{40,32},{48,56},{56,48},{64,72... | collective-permute-start | bytes 4718600 | tf_op jit(solution)/shard_map/ppermute | solution.py:33
  69.7 8.8 %copy-start.14 = (bf16[8,512,512]{2,1,0:T(8,128)(2,1)S(1)}, bf16[8,512,512]{2,1,0:T(8,128)(2,1)}, u32[]{:S(2)}) copy-start(bf16[8,512,512]{2,1,0:T(8,128)(2,1)} %copy-done.13) | copy-start | bytes 12582916
  70.2 22.8 %collective-permute-start.15 = (bf16[128,2048]{1,0:T(8,128)(2,1)S(1)}, bf16[128,2048]{1,0:T(8,128)(2,1)S(1)}, u32[]{:S(2)}, u32[]{:S(2)}) collective-permute-start(bf16[128,2048]{1,0:T(8,128)(2,1)S(1)} %get-tuple-element.89), channel_id=1, source_target_pairs={{0,2},{1,3},{2,4},{3,5},{4,6},{5,7},{6,0},{7,1},{8,10},{9,11},{10,... | collective-permute-start | bytes 1572872 | tf_op jit(solution)/shard_map/ppermute | solution.py:38
  71.8 26.1 %collective-permute-start.16 = (bf16[128,2048]{1,0:T(8,128)(2,1)S(1)}, bf16[128,2048]{1,0:T(8,128)(2,1)S(1)}, u32[]{:S(2)}, u32[]{:S(2)}) collective-permute-start(bf16[128,2048]{1,0:T(8,128)(2,1)S(1)} %get-tuple-element.90), channel_id=1, source_target_pairs={{0,4},{1,5},{2,6},{3,7},{4,0},{5,1},{6,2},{7,3},{8,12},{9,13},{10,... | collective-permute-start | bytes 1572872 | tf_op jit(solution)/shard_map/ppermute | solution.py:38
  74.7 26.1 %collective-permute-start.17 = (bf16[128,2048]{1,0:T(8,128)(2,1)S(1)}, bf16[128,2048]{1,0:T(8,128)(2,1)S(1)}, u32[]{:S(2)}, u32[]{:S(2)}) collective-permute-start(bf16[128,2048]{1,0:T(8,128)(2,1)S(1)} %get-tuple-element.91), channel_id=1, source_target_pairs={{0,6},{1,7},{2,0},{3,1},{4,2},{5,3},{6,4},{7,5},{8,14},{9,15},{10,... | collective-permute-start | bytes 1572872 | tf_op jit(solution)/shard_map/ppermute | solution.py:38
  76.4 14.9 %collective-permute-start.11 = (bf16[2,128,1024]{2,1,0:T(8,128)(2,1)S(1)}, bf16[2,128,1024]{2,1,0:T(8,128)(2,1)S(1)}, u32[]{:S(2)}, u32[]{:S(2)}) collective-permute-start(bf16[2,128,1024]{2,1,0:T(8,128)(2,1)S(1)} %get-tuple-element.84), channel_id=1, source_target_pairs={{0,16},{8,24},{16,0},{24,8},{32,48},{40,56},{48,32},{56,40},{64,80... | collective-permute-start | bytes 1572872 | tf_op jit(solution)/shard_map/ppermute | solution.py:33
  78.1 23.7 %collective-permute-start.10 = (bf16[2,128,1024]{2,1,0:T(8,128)(2,1)S(1)}, bf16[2,128,1024]{2,1,0:T(8,128)(2,1)S(1)}, u32[]{:S(2)}, u32[]{:S(2)}) collective-permute-start(bf16[2,128,1024]{2,1,0:T(8,128)(2,1)S(1)} %get-tuple-element.77.refs_7_), channel_id=1, source_target_pairs={{0,16},{8,24},{16,0},{24,8},{32,48},{40,56},{48,32},{56,40},{64,80... | collective-permute-start | bytes 1572872 | tf_op jit(solution)/shard_map/ppermute | solution.py:33
  78.6 8.0 %copy-start.3 = (bf16[1024,2048]{1,0:T(8,128)(2,1)S(1)}, bf16[1024,2048]{1,0:T(8,128)(2,1)}, u32[]{:S(2)}) copy-start(bf16[1024,2048]{1,0:T(8,128)(2,1)} %w_ref.1) | copy-start | bytes 12582916
  91.5 13.5 %collective-permute-start.12 = (bf16[2,64,1024]{2,1,0:T(8,128)(2,1)S(1)}, bf16[2,64,1024]{2,1,0:T(8,128)(2,1)S(1)}, u32[]{:S(2)}, u32[]{:S(2)}) collective-permute-start(bf16[2,64,1024]{2,1,0:T(8,128)(2,1)S(1)} %get-tuple-element.86.refs_0_), channel_id=1, source_target_pairs={{0,32},{8,40},{16,48},{24,56},{32,0},{40,8},{48,16},{56,24},{64,96... | collective-permute-start | bytes 786440 | tf_op jit(solution)/shard_map/ppermute | solution.py:33
  93.0 11.3 %collective-permute-start.13 = (bf16[2,32,1024]{2,1,0:T(8,128)(2,1)S(1)}, bf16[2,32,1024]{2,1,0:T(8,128)(2,1)S(1)}, u32[]{:S(2)}, u32[]{:S(2)}) collective-permute-start(bf16[2,32,1024]{2,1,0:T(8,128)(2,1)S(1)} %get-tuple-element.87), channel_id=1, source_target_pairs={{0,96},{8,104},{16,112},{24,120},{32,64},{40,72},{48,80},{56,88},{... | collective-permute-start | bytes 393224 | tf_op jit(solution)/shard_map/ppermute | solution.py:33
  97.9 7.1 %collective-permute-start.14 = (bf16[2,32,1024]{2,1,0:T(8,128)(2,1)S(1)}, bf16[2,32,1024]{2,1,0:T(8,128)(2,1)S(1)}, u32[]{:S(2)}, u32[]{:S(2)}) collective-permute-start(bf16[2,32,1024]{2,1,0:T(8,128)(2,1)S(1)} %get-tuple-element.88), channel_id=1, source_target_pairs={{0,64},{8,72},{16,80},{24,88},{32,96},{40,104},{48,112},{56,120},{... | collective-permute-start | bytes 393224 | tf_op jit(solution)/shard_map/ppermute | solution.py:33
  101.6 8.7 %collective-permute-start.18 = (bf16[32,2048]{1,0:T(8,128)(2,1)S(1)}, bf16[32,2048]{1,0:T(8,128)(2,1)S(1)}, u32[]{:S(2)}, u32[]{:S(2)}) collective-permute-start(bf16[32,2048]{1,0:T(8,128)(2,1)S(1)} %get-tuple-element.95), channel_id=1, source_target_pairs={{0,32},{8,40},{16,48},{24,56},{32,64},{40,72},{48,80},{56,88},{64,... | collective-permute-start | bytes 393224 | tf_op jit(solution)/shard_map/ppermute | solution.py:38
  101.8 8.6 %collective-permute-start.19 = (bf16[32,2048]{1,0:T(8,128)(2,1)S(1)}, bf16[32,2048]{1,0:T(8,128)(2,1)S(1)}, u32[]{:S(2)}, u32[]{:S(2)}) collective-permute-start(bf16[32,2048]{1,0:T(8,128)(2,1)S(1)} %get-tuple-element.96), channel_id=1, source_target_pairs={{0,64},{8,72},{16,80},{24,88},{32,96},{40,104},{48,112},{56,120},{... | collective-permute-start | bytes 393224 | tf_op jit(solution)/shard_map/ppermute | solution.py:38
  104.3 6.5 %collective-permute-start.20 = (bf16[32,2048]{1,0:T(8,128)(2,1)S(1)}, bf16[32,2048]{1,0:T(8,128)(2,1)S(1)}, u32[]{:S(2)}, u32[]{:S(2)}) collective-permute-start(bf16[32,2048]{1,0:T(8,128)(2,1)S(1)} %get-tuple-element.97), channel_id=1, source_target_pairs={{0,96},{8,104},{16,112},{24,120},{32,0},{40,8},{48,16},{56,24},{64... | collective-permute-start | bytes 393224 | tf_op jit(solution)/shard_map/ppermute | solution.py:38
  111.4 4.3 %collective-permute-start.21 = (bf16[16,2048]{1,0:T(8,128)(2,1)S(1)}, bf16[16,2048]{1,0:T(8,128)(2,1)S(1)}, u32[]{:S(2)}, u32[]{:S(2)}) collective-permute-start(bf16[16,2048]{1,0:T(8,128)(2,1)S(1)} %get-tuple-element.100), channel_id=1, source_target_pairs={{0,16},{8,24},{16,0},{24,8},{32,48},{40,56},{48,32},{56,40},{64,80... | collective-permute-start | bytes 196616 | tf_op jit(solution)/shard_map/ppermute | solution.py:33
  116.3 5.9 %collective-permute-start.22 = (f32[8,2048]{1,0:T(8,128)S(1)}, f32[8,2048]{1,0:T(8,128)S(1)}, u32[]{:S(2)}, u32[]{:S(2)}) collective-permute-start(f32[8,2048]{1,0:T(8,128)S(1)} %get-tuple-element.102), channel_id=1, source_target_pairs={{0,1},{1,0},{2,3},{3,2},{4,5},{5,4},{6,7},{7,6},{8,9},{9,8},{10,11... | collective-permute-start | bytes 196616 | tf_op jit(solution)/shard_map/ppermute | solution.py:33
